TPU v7x, 32 devices: a whole 2x2x4 slice. The times are simulated.
32 devices in a mesh: node: 4 (over z), dev: 8 (over y, x, core).
Axes of the slice: x: 2, y: 2, z: 4, core: 2. Of those that a mesh axis runs over, the one named last changes fastest.
Arguments:
- image: bfloat16 [128, 14, 14, 512], P(('node', 'dev')), may hold values from -30 to 30
- crop_sides: int32 [128], P(('node', 'dev')), may hold values from 6 to 14, as said below
- proj_in: bfloat16 [512, 512], replicated, may hold values from -0.25 to 0.25
- kernel_large: bfloat16 [31, 31, 512], replicated, may hold values from -0.1875 to 0.1875
- kernel_small: bfloat16 [5, 5, 512], replicated, may hold values from -1.25 to 1.25
- proj_out: bfloat16 [512, 512], replicated, may hold values from -0.25 to 0.25
- proj_up: bfloat16 [512, 2048], replicated, may hold values from -0.25 to 0.25
- proj_down: bfloat16 [2048, 512], replicated, may hold values from -0.125 to 0.125
- norm_gain: float32 [7, 512], replicated, may hold values from 0.5 to 1.5
- norm_shift: float32 [7, 512], replicated, may hold values from -2 to 2
- wide_gain: float32 [2048], replicated, may hold values from 0.5 to 1.5
- wide_shift: float32 [2048], replicated, may hold values from -2 to 2
- cotangent: bfloat16 [128, 14, 14, 512], P(('node', 'dev')), may hold values from -6 to 6
Outputs:
- block_out: bfloat16 [128, 14, 14, 512], P(('node', 'dev'))
- grad_image: float32 [128, 14, 14, 512], P(('node', 'dev'))
- grad_proj_in: float32 [512, 512], replicated
- grad_kernel_large: float32 [31, 31, 512], replicated
- grad_kernel_small: float32 [5, 5, 512], replicated
- grad_proj_out: float32 [512, 512], replicated
- grad_proj_up: float32 [512, 2048], replicated
- grad_proj_down: float32 [2048, 512], replicated
- grad_norm_gain: float32 [7, 512], replicated
- grad_norm_shift: float32 [7, 512], replicated
- grad_wide_gain: float32 [2048], replicated
- grad_wide_shift: float32 [2048], replicated
Inputs may be any that keep to these rules, and one draw needn't show every extreme that they name: `crop_sides`: each crop's side is 6 or 14 cells; its map fills the top left corner of its 14 x 14 canvas, the other cells are padding.
All inputs are finite; a program needn't handle non-finite values.
Results may differ from a plain program's by a relative error of at most 0.012.
Values sent between devices are 32-bit elements; how exact they have to be, the bound alone decides.
No kernel may reach another device: no remote copies, remote signals or barrier semaphores. Data moves between devices by JAX's collectives and lax.ppermute only.
A program may use at most 192 MiB of HBM per device.

v0:
```python
import jax
import jax.numpy as jnp
from jax import lax
from jax.sharding import PartitionSpec as P

EPSILON = 1e-05


def canvas_mask(crop_sides, canvas):
    places = jnp.arange(canvas, dtype=jnp.int32)
    inside_rows = places[None, :, None] < crop_sides[:, None, None]
    inside_cols = places[None, None, :] < crop_sides[:, None, None]
    return jnp.logical_and(inside_rows, inside_cols).astype(jnp.float32)[..., None]


def pointwise(values, weight):
    flattened = values.reshape(-1, values.shape[-1])
    result = jnp.dot(flattened, weight, preferred_element_type=jnp.float32)
    return result.reshape(values.shape[:-1] + (weight.shape[1],))


def transposed(gradient, weight):
    flattened = gradient.reshape(-1, gradient.shape[-1])
    result = lax.dot_general(
        flattened, weight, (((1,), (1,)), ((), ())), preferred_element_type=jnp.float32
    )
    return result.reshape(gradient.shape[:-1] + (weight.shape[0],))


def weight_grad(inputs, gradient):
    flat_inputs = inputs.reshape(-1, inputs.shape[-1])
    flat_grads = gradient.reshape(-1, gradient.shape[-1])
    return lax.dot_general(
        flat_inputs, flat_grads, (((0,), (0,)), ((), ())), preferred_element_type=jnp.float32
    )


def depthwise(values, kernel):
    return lax.conv_general_dilated(
        values,
        kernel[:, :, None, :],
        (1, 1),
        "SAME",
        dimension_numbers=("NHWC", "HWIO", "NHWC"),
        feature_group_count=values.shape[-1],
        preferred_element_type=jnp.float32,
    )


def depthwise_input_grad(gradient_low, kernel):
    return depthwise(gradient_low, kernel[::-1, ::-1, :])


def depthwise_kernel_grad(values, gradient_low, side):
    margin = (side - 1) // 2
    result = lax.conv_general_dilated(
        values,
        gradient_low,
        (1, 1),
        ((margin, margin), (margin, margin)),
        dimension_numbers=("CHWN", "IHWO", "NHWC"),
        batch_group_count=values.shape[-1],
        preferred_element_type=jnp.float32,
    )
    return result[0]


def moments(values, valid_mask):
    masked = valid_mask * values
    return (
        jnp.sum(valid_mask),
        jnp.sum(masked, axis=(0, 1, 2)),
        jnp.sum(masked * values, axis=(0, 1, 2)),
    )


def finish(values, valid_mask, pixel_count, column_sum, square, scaling, offsets):
    column_mean = column_sum / pixel_count
    spread = square / pixel_count - column_mean * column_mean
    reciprocal = lax.rsqrt(spread + EPSILON)
    normed = (values - column_mean) * reciprocal
    return ((normed * scaling + offsets) * valid_mask, (normed, reciprocal, pixel_count))


def norm_forward(values, valid_mask, scaling, offsets):
    pixel_count, column_sum, square = moments(values, valid_mask)
    pixel_count, column_sum, square = lax.psum((pixel_count, column_sum, square), ("node", "dev"))
    return finish(values, valid_mask, pixel_count, column_sum, square, scaling, offsets)


def grad_moments(gradient, valid_mask, saved):
    masked = gradient * valid_mask
    return (masked, jnp.sum(masked, axis=(0, 1, 2)), jnp.sum(masked * saved[0], axis=(0, 1, 2)))


def grad_finish(masked, valid_mask, saved, scaling, shift_sum, gain_sum):
    normed, reciprocal, pixel_count = saved
    return (
        valid_mask
        * scaling
        * reciprocal
        * (masked - shift_sum / pixel_count - normed * gain_sum / pixel_count)
    )


def norm_backward(gradient, valid_mask, saved, scaling):
    masked, shift_sum, gain_sum = grad_moments(gradient, valid_mask, saved)
    shift_sum, gain_sum = lax.psum((shift_sum, gain_sum), ("node", "dev"))
    return (
        grad_finish(masked, valid_mask, saved, scaling, shift_sum, gain_sum),
        gain_sum,
        shift_sum,
    )


def settle_joined(gradients):
    joined = jnp.concatenate([gradient.reshape(-1) for gradient in gradients])
    devices = lax.axis_size(("node", "dev"))
    padding_count = -joined.shape[0] % devices
    joined = jnp.pad(joined, (0, padding_count))
    owned_part = lax.psum_scatter(joined, ("node", "dev"), scatter_dimension=0, tiled=True)
    gathered = lax.all_gather(owned_part, ("node", "dev"), axis=0, tiled=True)
    results = []
    offset = 0
    for gradient in gradients:
        results.append(gathered[offset : offset + gradient.size].reshape(gradient.shape))
        offset = offset + gradient.size
    return results


def gelu_back(values, gradient):
    unused, gelu_pull = jax.vjp(jax.nn.gelu, values)
    return gelu_pull(gradient)[0]


def local(
    image,
    crop_sides,
    proj_in,
    kernel_large,
    kernel_small,
    proj_out,
    proj_up,
    proj_down,
    norm_gain,
    norm_shift,
    wide_gain,
    wide_shift,
    cotangent,
):
    valid_mask = canvas_mask(crop_sides, image.shape[1])
    resid_in = image.astype(jnp.float32) * valid_mask
    pre_out, pre_saved = norm_forward(resid_in, valid_mask, norm_gain[0], norm_shift[0])
    pre_low = pre_out.astype(jnp.bfloat16)
    proj_pre = pointwise(pre_low, proj_in)
    mid_norm, mid_saved = norm_forward(proj_pre, valid_mask, norm_gain[1], norm_shift[1])
    mixer_low = jax.nn.gelu(mid_norm).astype(jnp.bfloat16)
    large_conv = depthwise(mixer_low, kernel_large)
    small_conv = depthwise(mixer_low, kernel_small)
    large_norm, large_saved = norm_forward(large_conv, valid_mask, norm_gain[2], norm_shift[2])
    small_norm, small_saved = norm_forward(small_conv, valid_mask, norm_gain[3], norm_shift[3])
    merged = large_norm + small_norm
    merged_low = jax.nn.gelu(merged).astype(jnp.bfloat16)
    proj_back = pointwise(merged_low, proj_out)
    back_norm, back_saved = norm_forward(proj_back, valid_mask, norm_gain[4], norm_shift[4])
    resid_mid = resid_in + back_norm
    ffn_norm, ffn_saved = norm_forward(resid_mid, valid_mask, norm_gain[5], norm_shift[5])
    ffn_low = ffn_norm.astype(jnp.bfloat16)
    hidden_pre = pointwise(ffn_low, proj_up)
    hidden_norm, hidden_saved = norm_forward(hidden_pre, valid_mask, wide_gain, wide_shift)
    hidden_low = jax.nn.gelu(hidden_norm).astype(jnp.bfloat16)
    ffn_proj = pointwise(hidden_low, proj_down)
    ffn_out, out_saved = norm_forward(ffn_proj, valid_mask, norm_gain[6], norm_shift[6])
    block_out = (resid_mid + ffn_out).astype(jnp.bfloat16)
    upstream = cotangent.astype(jnp.float32)
    down_grad, gain_last, shift_last = norm_backward(upstream, valid_mask, out_saved, norm_gain[6])
    down_low = down_grad.astype(jnp.bfloat16)
    grad_down = weight_grad(hidden_low, down_low)
    hidden_grad = gelu_back(hidden_norm, transposed(down_low, proj_down))
    up_grad, gain_wide, shift_wide = norm_backward(hidden_grad, valid_mask, hidden_saved, wide_gain)
    up_low = up_grad.astype(jnp.bfloat16)
    grad_up = weight_grad(ffn_low, up_low)
    ffn_grad, gain_ffn, shift_ffn = norm_backward(
        transposed(up_low, proj_up), valid_mask, ffn_saved, norm_gain[5]
    )
    resid_grad = upstream + ffn_grad
    back_grad, gain_back, shift_back = norm_backward(
        resid_grad, valid_mask, back_saved, norm_gain[4]
    )
    back_low = back_grad.astype(jnp.bfloat16)
    grad_out = weight_grad(merged_low, back_low)
    merged_grad = gelu_back(merged, transposed(back_low, proj_out))
    large_grad, gain_large, shift_large = norm_backward(
        merged_grad, valid_mask, large_saved, norm_gain[2]
    )
    small_grad, gain_small, shift_small = norm_backward(
        merged_grad, valid_mask, small_saved, norm_gain[3]
    )
    large_low = large_grad.astype(jnp.bfloat16)
    small_low = small_grad.astype(jnp.bfloat16)
    grad_large = depthwise_kernel_grad(mixer_low, large_low, kernel_large.shape[0])
    grad_small = depthwise_kernel_grad(mixer_low, small_low, kernel_small.shape[0])
    mixer_back = depthwise_input_grad(large_low, kernel_large) + depthwise_input_grad(
        small_low, kernel_small
    )
    mid_grad = gelu_back(mid_norm, mixer_back)
    pre_grad, gain_mid, shift_mid = norm_backward(mid_grad, valid_mask, mid_saved, norm_gain[1])
    pre_round = pre_grad.astype(jnp.bfloat16)
    grad_in = weight_grad(pre_low, pre_round)
    first_grad, gain_first, shift_first = norm_backward(
        transposed(pre_round, proj_in), valid_mask, pre_saved, norm_gain[0]
    )
    grad_image = (resid_grad + first_grad) * valid_mask
    grad_in, grad_large, grad_small, grad_out, grad_up, grad_down = settle_joined(
        [grad_in, grad_large, grad_small, grad_out, grad_up, grad_down]
    )
    gain_grads = jnp.stack(
        [gain_first, gain_mid, gain_large, gain_small, gain_back, gain_ffn, gain_last]
    )
    shift_grads = jnp.stack(
        [shift_first, shift_mid, shift_large, shift_small, shift_back, shift_ffn, shift_last]
    )
    return (
        block_out,
        grad_image,
        grad_in,
        grad_large,
        grad_small,
        grad_out,
        grad_up,
        grad_down,
        gain_grads,
        shift_grads,
        gain_wide,
        shift_wide,
    )


def solution(mesh):
    return jax.shard_map(
        local,
        mesh=mesh,
        in_specs=(
            P(("node", "dev"), None, None, None),
            P(("node", "dev")),
            P(),
            P(),
            P(),
            P(),
            P(),
            P(),
            P(),
            P(),
            P(),
            P(),
            P(("node", "dev"), None, None, None),
        ),
        out_specs=(
            P(("node", "dev"), None, None, None),
            P(("node", "dev"), None, None, None),
            P(),
            P(),
            P(),
            P(),
            P(),
            P(),
            P(),
            P(),
            P(),
            P(),
        ),
        check_vma=False,
    )
```

profile of v0, /device:TPU:0, one launch (start us, length us, event | category | flops | bytes accessed | tf_op | source)
XLA Modules:
  0.0 1948.8 jit_solution(15853556746676919474)
XLA Ops:
  13.7 3.6 rev.6
  17.9 42.3 %all-reduce.15 = (f32[512]{0:T(512)S(1)}, f32[]{:T(128)}, f32[512]{0:T(512)S(1)}) all-reduce(f32[512]{0:T(512)S(1)} %get-tuple-element.78, f32[]{:T(128)} %convert_reduce_fusion, f32[512]{0:T(512)S(1)} %get-tuple-element.77), channel_id=1, replica_groups=mesh['node'=4,'dev'=8] {'node','dev'}, use_global_device_ids=true, to_apply=%region_5.0 | all-reduce | flops 1025 | bytes 8200 | tf_op jit(solution)/shard_map/psum | solution.py:87
  60.8 3.2 multiply_reduce_fusion.7
  64.0 40.3 %all-reduce.14 = (f32[512]{0:T(512)S(1)}, f32[512]{0:T(512)S(1)}) all-reduce(f32[512]{0:T(512)S(1)} %get-tuple-element.65, f32[512]{0:T(512)S(1)} %get-tuple-element.64), channel_id=1, replica_groups=mesh['node'=4,'dev'=8] {'node','dev'}, use_global_device_ids=true, to_apply=%region_9.0 | all-reduce | flops 1024 | bytes 8192 | tf_op jit(solution)/shard_map/psum | solution.py:87
  107.3 4.5 fusion.63
  111.9 208.8 %fusion.20 = f32[4,14,14,512]{3,0,2,1:T(4,128)S(1)} fusion(bf16[31,31,1,512]{3,1,0,2:T(8,128)(2,1)S(1)} %bitcast.113, bf16[4,14,14,512]{3,2,1,0:T(8,128)(2,1)S(1)} %multiply_convert_fusion.8), kind=kOutput, calls=%fused_computation.51 | convolution fusion | flops 157351936 | bytes 3392512 | tf_op jit(solution)/shard_map/conv_general_dilated | solution.py:39
  321.9 39.9 %all-reduce.13 = (f32[512]{0:T(512)S(1)}, f32[512]{0:T(512)S(1)}, f32[512]{0:T(512)S(1)}, f32[512]{0:T(512)S(1)}) all-reduce(f32[512]{0:T(512)S(1)} %get-tuple-element.79, f32[512]{0:T(512)S(1)} %get-tuple-element.80, f32[512]{0:T(512)S(1)} %get-tuple-element.72, ...), channel_id=1, replica_groups=mesh['node'=4,'dev'=8] {'node','dev'}, use_global_device_ids=true, to_apply=%region_17.0 | all-reduce | flops 2048 | bytes 16384 | tf_op jit(solution)/shard_map/psum | solution.py:87
  362.4 3.5 multiply_convert_fusion.7
  367.8 40.1 %all-reduce.12 = (f32[512]{0:T(512)S(1)}, f32[512]{0:T(512)S(1)}) all-reduce(f32[512]{0:T(512)S(1)} %get-tuple-element.63, f32[512]{0:T(512)S(1)} %get-tuple-element.62), channel_id=1, replica_groups=mesh['node'=4,'dev'=8] {'node','dev'}, use_global_device_ids=true, to_apply=%region_21.0 | all-reduce | flops 1024 | bytes 8192 | tf_op jit(solution)/shard_map/psum | solution.py:87
  408.5 3.6 multiply_reduce_fusion.3
  412.1 39.8 %all-reduce.11 = (f32[512]{0:T(512)S(1)}, f32[512]{0:T(512)S(1)}) all-reduce(f32[512]{0:T(512)S(1)} %get-tuple-element.61, f32[512]{0:T(512)S(1)} %get-tuple-element.60), channel_id=1, replica_groups=mesh['node'=4,'dev'=8] {'node','dev'}, use_global_device_ids=true, to_apply=%region_25.0 | all-reduce | flops 1024 | bytes 8192 | tf_op jit(solution)/shard_map/psum | solution.py:87
  452.4 7.5 multiply_reduce_fusion
  459.9 40.5 %all-reduce.10 = (f32[2048]{0:T(1024)S(1)}, f32[2048]{0:T(1024)S(1)}) all-reduce(f32[2048]{0:T(1024)S(1)} %get-tuple-element.49, f32[2048]{0:T(1024)S(1)} %get-tuple-element.48), channel_id=1, replica_groups=mesh['node'=4,'dev'=8] {'node','dev'}, use_global_device_ids=true, to_apply=%region_29.0 | all-reduce | flops 4096 | bytes 32768 | tf_op jit(solution)/shard_map/psum | solution.py:87
  501.0 5.7 multiply_convert_fusion.1
  506.7 3.5 multiply_reduce_fusion.2
  510.2 39.7 %all-reduce.9 = (f32[512]{0:T(512)S(1)}, f32[512]{0:T(512)S(1)}) all-reduce(f32[512]{0:T(512)S(1)} %get-tuple-element.59, f32[512]{0:T(512)S(1)} %get-tuple-element.58), channel_id=1, replica_groups=mesh['node'=4,'dev'=8] {'node','dev'}, use_global_device_ids=true, to_apply=%region_33.0 | all-reduce | flops 1024 | bytes 8192 | tf_op jit(solution)/shard_map/psum | solution.py:87
  550.5 4.1 fusion.10
  554.6 40.3 %all-reduce.8 = (f32[512]{0:T(512)S(1)}, f32[512]{0:T(512)S(1)}) all-reduce(f32[512]{0:T(512)S(1)} %get-tuple-element.76, f32[512]{0:T(512)S(1)} %get-tuple-element.75), channel_id=1, replica_groups=mesh['node'=4,'dev'=8] {'node','dev'}, use_global_device_ids=true, to_apply=%region_37.0 | all-reduce | flops 1024 | bytes 8192 | tf_op jit(solution)/shard_map/psum | solution.py:108
  595.5 8.3 convolution_bitcast_fusion
  603.8 12.6 fusion.70
  616.4 40.2 %all-reduce.7 = (f32[2048]{0:T(1024)S(1)}, f32[2048]{0:T(1024)S(1)}) all-reduce(f32[2048]{0:T(1024)S(1)} %get-tuple-element.51, f32[2048]{0:T(1024)S(1)} %get-tuple-element.50), channel_id=1, replica_groups=mesh['node'=4,'dev'=8] {'node','dev'}, use_global_device_ids=true, to_apply=%region_41.0 | all-reduce | flops 4096 | bytes 32768 | tf_op jit(solution)/shard_map/psum | solution.py:108
  657.1 7.5 multiply_convert_fusion
  664.7 3.4 multiply_reduce_fusion.17
  668.1 4.6 convolution_bitcast_fusion.1
  672.7 40.4 %all-reduce.6 = (f32[512]{0:T(512)S(1)}, f32[512]{0:T(512)S(1)}) all-reduce(f32[512]{0:T(512)S(1)} %get-tuple-element.57, f32[512]{0:T(512)S(1)} %get-tuple-element.56), channel_id=1, replica_groups=mesh['node'=4,'dev'=8] {'node','dev'}, use_global_device_ids=true, to_apply=%region_45.0 | all-reduce | flops 1024 | bytes 8192 | tf_op jit(solution)/shard_map/psum | solution.py:108
  713.7 5.3 multiply_reduce_fusion.16
  719.0 39.5 %all-reduce.5 = (f32[512]{0:T(512)S(1)}, f32[512]{0:T(512)S(1)}) all-reduce(f32[512]{0:T(512)S(1)} %get-tuple-element.55, f32[512]{0:T(512)S(1)} %get-tuple-element.54), channel_id=1, replica_groups=mesh['node'=4,'dev'=8] {'node','dev'}, use_global_device_ids=true, to_apply=%region_49.0 | all-reduce | flops 1024 | bytes 8192 | tf_op jit(solution)/shard_map/psum | solution.py:108
  759.0 3.3 multiply_convert_fusion.5
  764.4 4.4 multiply_reduce_fusion.12
  768.8 3.1 copy.109
  776.1 40.7 %all-reduce.4 = (f32[512]{0:T(512)S(1)}, f32[512]{0:T(512)S(1)}, f32[512]{0:T(512)S(1)}) all-reduce(f32[512]{0:T(512)S(1)} %get-tuple-element.69, f32[512]{0:T(512)S(1)} %get-tuple-element.70, f32[512]{0:T(512)S(1)} %get-tuple-element.68), channel_id=1, replica_groups=mesh['node'=4,'dev'=8] {'node','dev'}, use_global_device_ids=true, to_apply=%region_55.0 | all-reduce | flops 1536 | bytes 12288 | tf_op jit(solution)/shard_map/psum | solution.py:108
  817.4 5.1 multiply_convert_fusion.4
  823.4 8.6 convolution_reduce_fusion.1
  832.1 361.2 %convolution_reduce_fusion = f32[31,31,512]{2,1,0:T(8,128)S(1)} fusion(bf16[4,14,14,512]{3,2,1,0:T(8,128)(2,1)} %get-tuple-element.121, bf16[4,14,14,512]{3,2,1,0:T(8,128)(2,1)} %copy-done.21), kind=kOutput, calls=%fused_computation.111 | convolution fusion | flops 157351936 | bytes 3573760 | tf_op jit(solution)/shard_map/conv_general_dilated | solution.py:56
  1193.3 170.0 %fusion.18 = f32[4,14,14,512]{3,0,2,1:T(4,128)} fusion(bf16[31,31,1,512]{3,1,0,2:T(8,128)(2,1)S(1)} %bitcast.114, bf16[4,14,14,512]{3,2,1,0:T(8,128)(2,1)} %get-tuple-element.121), kind=kOutput, calls=%fused_computation.49 | convolution fusion | flops 157351936 | bytes 3392512 | tf_op jit(solution)/shard_map/conv_general_dilated | solution.py:39
  1364.7 6.6 fusion.50
  1371.3 3.6 fusion.71
  1375.0 39.4 %all-reduce.3 = (f32[512]{0:T(512)S(1)}, f32[512]{0:T(512)S(1)}) all-reduce(f32[512]{0:T(512)S(1)} %get-tuple-element.67, f32[512]{0:T(512)S(1)} %get-tuple-element.66), channel_id=1, replica_groups=mesh['node'=4,'dev'=8] {'node','dev'}, use_global_device_ids=true, to_apply=%region_59.0 | all-reduce | flops 1024 | bytes 8192 | tf_op jit(solution)/shard_map/psum | solution.py:108
  1420.7 17.1 dynamic-update-slice.2
  1441.5 4.6 constant_dynamic-update-slice_fusion.1
  1448.4 230.2 %all-reduce.21.cloned.1.call-done = f32[3126272]{0:T(1024)} async-done(((f32[3126272]{0:T(1024)}), f32[3126272]{0:T(1024)}) %all-reduce.21.cloned.1.call-update) | async-done | bytes 12505104
  1678.5 4.7 broadcast.131
  1688.2 3.6 multiply_reduce_fusion.15
  1691.8 41.6 %all-reduce.2 = (f32[512]{0:T(512)S(1)}, f32[512]{0:T(512)S(1)}) all-reduce(f32[512]{0:T(512)S(1)} %get-tuple-element.53, f32[512]{0:T(512)S(1)} %get-tuple-element.52), channel_id=1, replica_groups=mesh['node'=4,'dev'=8] {'node','dev'}, use_global_device_ids=true, to_apply=%region_63.0 | all-reduce | flops 1024 | bytes 8192 | tf_op jit(solution)/shard_map/psum | solution.py:108
  1740.4 175.5 %all-reduce.19.cloned.1.call-done = f32[3126272]{0:T(1024)} async-done(((f32[3126272]{0:T(1024)}), f32[3126272]{0:T(1024)}) %all-reduce.19.cloned.1.call-update) | async-done | bytes 12505104
  1920.6 7.3 fusion.73
  1927.9 4.9 slice.119
  1936.8 5.0 reshape.216
  (163 shorter events, 60.5 us)
Async XLA Ops:
  7.2 499.5 %copy-start = (bf16[2048,512]{1,0:T(8,128)(2,1)S(1)}, bf16[2048,512]{1,0:T(8,128)(2,1)}, u32[]{:S(2)}) copy-start(bf16[2048,512]{1,0:T(8,128)(2,1)} %param.20) | copy-start | bytes 6291460
  7.2 10.2 copy-start.12
  7.2 1671.3 %all-reduce.21.cloned.1.call-start = ((), (), s32[]{:S(2)}) async-start(), calls=%async_computation.1 | async-start | bytes 25010176
  10.0 54.0 %copy-start.39 = (f32[1,512]{1,0:T(1,128)}, f32[1,512]{1,0:T(1,128)S(1)}, u32[]{:S(2)}) copy-start(f32[1,512]{1,0:T(1,128)S(1)} %get-tuple-element.128) | copy-start | bytes 6148
  10.0 94.8 %copy-start.30 = (f32[1,512]{1,0:T(1,128)}, f32[1,512]{1,0:T(1,128)S(1)}, u32[]{:S(2)}) copy-start(f32[1,512]{1,0:T(1,128)S(1)} %get-tuple-element.127) | copy-start | bytes 6148
  11.0 49.7 %copy-start.49 = (f32[1,512]{1,0:T(1,128)}, f32[1,512]{1,0:T(1,128)S(1)}, u32[]{:S(2)}) copy-start(f32[1,512]{1,0:T(1,128)S(1)} %get-tuple-element.135) | copy-start | bytes 6148
  11.1 93.8 %copy-start.36 = (f32[1,512]{1,0:T(1,128)}, f32[1,512]{1,0:T(1,128)S(1)}, u32[]{:S(2)}) copy-start(f32[1,512]{1,0:T(1,128)S(1)} %get-tuple-element.134) | copy-start | bytes 6148
  60.8 3.2 copy-start.41
  60.8 3.2 copy-start.43
  64.0 43.3 %copy-start.27 = (bf16[5,5,512]{2,1,0:T(8,128)(2,1)S(1)}, bf16[5,5,512]{2,1,0:T(8,128)(2,1)}, u32[]{:S(2)}) copy-start(bf16[5,5,512]{2,1,0:T(8,128)(2,1)} %param.17) | copy-start | bytes 76804
  104.9 7.0 copy-start.32
  104.9 7.0 copy-start.34
  107.3 4.6 copy-start.21
  107.3 4.6 copy-start.19
  111.9 208.8 %copy-start.7 = (f32[4,14,14,512]{3,0,2,1:T(4,128)}, f32[4,14,14,512]{3,0,2,1:T(4,128)S(1)}, u32[]{:S(2)}) copy-start(f32[4,14,14,512]{3,0,2,1:T(4,128)S(1)} %fusion.63) | copy-start | bytes 4816900
  362.4 3.6 copy-start.52
  452.4 48.6 %copy-start.29 = (f32[2048]{0:T(1024)S(1)}, f32[2048]{0:T(1024)}, u32[]{:S(2)}) copy-start(f32[2048]{0:T(1024)} %param.23) | copy-start | bytes 24580
  452.4 48.6 %copy-start.48 = (f32[2048]{0:T(1024)S(1)}, f32[2048]{0:T(1024)}, u32[]{:S(2)}) copy-start(f32[2048]{0:T(1024)} %param.24) | copy-start | bytes 24580
  506.7 3.5 copy-start.15
  594.9 8.9 copy-start.46
  595.4 8.4 copy-start.16
  595.4 8.4 copy-start.17
  656.6 8.1 copy-start.38
  656.6 8.1 copy-start.45
  657.1 7.5 copy-start.2
  657.1 7.5 copy-start.51
  759.0 3.4 copy-start.24
  762.4 2.0 copy-start.53
  764.4 4.4 copy-start.13
  768.8 3.1 copy-start.3
  817.4 6.1 copy-start.22
  832.1 361.2 %copy-start.20 = (bf16[31,31,512]{2,1,0:T(8,128)(2,1)S(1)}, bf16[31,31,512]{2,1,0:T(8,128)(2,1)}, u32[]{:S(2)}) copy-start(bf16[31,31,512]{2,1,0:T(8,128)(2,1)} %rev.6) | copy-start | bytes 2952196
  1364.7 6.6 copy-start.5
  1364.7 6.6 copy-start.18
  1364.7 6.6 copy-start.31
  1364.7 6.6 copy-start.33
  1364.7 6.6 copy-start.35
  1364.7 6.6 copy-start.37
  1414.9 2.7 copy-start.40
  1415.0 2.7 copy-start.42
  1415.0 2.7 copy-start.44
  1415.0 2.7 copy-start.50
  1418.8 1.9 copy-start.11
  1441.5 4.6 copy-start.4
  1448.3 467.6 %all-reduce.19.cloned.1.call-start = ((), (), s32[]{:S(2)}) async-start(), calls=%async_computation | async-start | bytes 25010176
  1688.2 45.7 %copy-start.6 = (f32[4,14,14,512]{3,2,1,0:T(8,128)S(1)}, f32[4,14,14,512]{3,2,1,0:T(8,128)}, u32[]{:S(2)}) copy-start(f32[4,14,14,512]{3,2,1,0:T(8,128)} %get-tuple-element.114) | copy-start | bytes 4816900
  1737.0 2.2 copy-start.47
  1936.8 5.0 copy-start.1
  (9 other events, 12.6 us)
Sparse Core Ops, SparseCore 0:
  1448.4 230.0 all-reduce.20
  1685.7 230.2 all-reduce.18
where the time goes:
time: 1960 us; the launch traced here: 1950 us
  matrix products  814 us (42%)
  blocking collectives  565 us (29%)
  waiting for transfers between devices  406 us (21%)
  local copies, waits for them, and re-layouts  88 us (4%)
  other arithmetic  60.8 us (3%)
    unnamed x4, waiting for transfers between devices  406 us
    conv_general_dilated x4, matrix products, depthwise(): lax.conv_general_dilated(values, kernel[:, :, None, :], (1, 1), 'SAME', d...  390 us
    conv_general_dilated x2, matrix products, depthwise_kernel_grad(): lax.conv_general_dilated(values, gradient_low, (1, 1), ((margin, margin),...  370 us
    psum x7, blocking collectives, norm_forward(): lax.psum((pixel_count, column_sum, square), ('node', 'dev'))  283 us
    psum x7, blocking collectives, norm_backward(): shift_sum, gain_sum = lax.psum((shift_sum, gain_sum), ('node', 'dev'))  282 us
    unnamed x121, local copies, waits for them, and re-layouts  48.9 us
  transfers between devices with their start and end apart: 2, of which 2 were waited for; matrix products, arithmetic and copies ran while one was open for 1% of the time, Pallas kernels for 0%

commit v1 on v0

--- a/solution.py
+++ b/solution.py
@@ -1,5 +1,6 @@
 import jax
 import jax.numpy as jnp
+import numpy as np
 from jax import lax
 from jax.sharding import PartitionSpec as P
 
@@ -35,34 +36,101 @@
     )
 
 
-def depthwise(values, kernel):
-    return lax.conv_general_dilated(
-        values,
-        kernel[:, :, None, :],
-        (1, 1),
-        "SAME",
-        dimension_numbers=("NHWC", "HWIO", "NHWC"),
-        feature_group_count=values.shape[-1],
-        preferred_element_type=jnp.float32,
-    )
-
-
-def depthwise_input_grad(gradient_low, kernel):
-    return depthwise(gradient_low, kernel[::-1, ::-1, :])
-
-
-def depthwise_kernel_grad(values, gradient_low, side):
-    margin = (side - 1) // 2
-    result = lax.conv_general_dilated(
-        values,
-        gradient_low,
-        (1, 1),
-        ((margin, margin), (margin, margin)),
-        dimension_numbers=("CHWN", "IHWO", "NHWC"),
-        batch_group_count=values.shape[-1],
-        preferred_element_type=jnp.float32,
-    )
-    return result[0]
+def wave_tables(canvas):
+    period = 2 * canvas - 1
+    pairs = [(0, v) for v in range(canvas)]
+    pairs += [(u, v) for u in range(1, canvas) for v in range(period)]
+    waves = np.array(pairs)
+
+    def tables(places):
+        grid = np.stack(np.meshgrid(places, places, indexing="ij"), -1).reshape(-1, 2)
+        angle = 2 * np.pi * ((waves @ grid.T) % period) / period
+        return np.cos(angle).astype(np.float32), np.sin(angle).astype(np.float32)
+
+    share = np.full((len(pairs), 1), 2.0 / period**2, np.float32)
+    share[0] = 1.0 / period**2
+    return tables, share
+
+
+def spread(table, values):
+    return lax.dot_general(
+        table, values, (((1,), (0,)), ((), ())), precision=lax.Precision.HIGH, preferred_element_type=jnp.float32
+    )
+
+
+def gather_back(table, values):
+    return lax.dot_general(
+        table, values, (((0,), (0,)), ((), ())), precision=lax.Precision.HIGH, preferred_element_type=jnp.float32
+    )
+
+
+def to_waves(values):
+    count, canvas, _, channels = values.shape
+    tables, _ = wave_tables(canvas)
+    cosines, sines = tables(np.arange(canvas))
+    flat = values.astype(jnp.float32).reshape(count, canvas * canvas, channels)
+    flat = flat.transpose(1, 0, 2).reshape(canvas * canvas, count * channels)
+    real = spread(cosines, flat).reshape(-1, count, channels)
+    imag = -spread(sines, flat).reshape(-1, count, channels)
+    return real, imag
+
+
+def from_waves(real, imag, canvas):
+    waves, count, channels = real.shape
+    tables, share = wave_tables(canvas)
+    cosines, sines = tables(np.arange(canvas))
+    flat = gather_back(cosines * share, real.reshape(waves, -1))
+    flat = flat - gather_back(sines * share, imag.reshape(waves, -1))
+    return flat.reshape(canvas, canvas, count, channels).transpose(2, 0, 1, 3)
+
+
+def kernel_waves(kernel, canvas):
+    side = kernel.shape[0]
+    reach = min((side - 1) // 2, canvas - 1)
+    middle = (side - 1) // 2
+    tables, _ = wave_tables(canvas)
+    cosines, sines = tables(np.arange(-reach, reach + 1))
+    used = kernel[middle - reach : middle + reach + 1, middle - reach : middle + reach + 1]
+    flat = used.astype(jnp.float32).reshape(-1, kernel.shape[2])
+    return spread(cosines, flat)[:, None], spread(sines, flat)[:, None]
+
+
+def kernel_grad(value_waves, grad_waves, side, canvas):
+    reach = min((side - 1) // 2, canvas - 1)
+    tables, share = wave_tables(canvas)
+    cosines, sines = tables(np.arange(-reach, reach + 1))
+    real = jnp.sum(value_waves[0] * grad_waves[0] + value_waves[1] * grad_waves[1], axis=1)
+    imag = jnp.sum(value_waves[1] * grad_waves[0] - value_waves[0] * grad_waves[1], axis=1)
+    flat = gather_back(cosines * share, real) - gather_back(sines * share, imag)
+    taps = 2 * reach + 1
+    rim = (side - taps) // 2
+    return jnp.pad(flat.reshape(taps, taps, -1), ((rim, rim), (rim, rim), (0, 0)))
+
+
+def times(left, right):
+    return (left[0] * right[0] - left[1] * right[1], left[0] * right[1] + left[1] * right[0])
+
+
+def times_conj(left, right):
+    return (left[0] * right[0] + left[1] * right[1], left[0] * right[1] - left[1] * right[0])
+
+
+AXES = ("node", "dev")
+
+
+def total(parts):
+    sizes = [part.size for part in parts]
+    flat = jnp.concatenate([part.reshape(-1) for part in parts])
+    flat = jnp.pad(flat, (0, -flat.shape[0] % 1024)).reshape(-1, 128)
+    devices = lax.axis_size(AXES)
+    copies = jnp.broadcast_to(flat[None], (devices,) + flat.shape)
+    flat = jnp.sum(lax.all_to_all(copies, AXES, 0, 0, tiled=True), axis=0).reshape(-1)
+    results = []
+    offset = 0
+    for part, size in zip(parts, sizes):
+        results.append(flat[offset : offset + size].reshape(part.shape))
+        offset += size
+    return results
 
 
 def moments(values, valid_mask):
@@ -84,7 +152,7 @@
 
 def norm_forward(values, valid_mask, scaling, offsets):
     pixel_count, column_sum, square = moments(values, valid_mask)
-    pixel_count, column_sum, square = lax.psum((pixel_count, column_sum, square), ("node", "dev"))
+    pixel_count, column_sum, square = total((pixel_count, column_sum, square))
     return finish(values, valid_mask, pixel_count, column_sum, square, scaling, offsets)
 
 
@@ -105,7 +173,7 @@
 
 def norm_backward(gradient, valid_mask, saved, scaling):
     masked, shift_sum, gain_sum = grad_moments(gradient, valid_mask, saved)
-    shift_sum, gain_sum = lax.psum((shift_sum, gain_sum), ("node", "dev"))
+    shift_sum, gain_sum = total((shift_sum, gain_sum))
     return (
         grad_finish(masked, valid_mask, saved, scaling, shift_sum, gain_sum),
         gain_sum,
@@ -114,18 +182,7 @@
 
 
 def settle_joined(gradients):
-    joined = jnp.concatenate([gradient.reshape(-1) for gradient in gradients])
-    devices = lax.axis_size(("node", "dev"))
-    padding_count = -joined.shape[0] % devices
-    joined = jnp.pad(joined, (0, padding_count))
-    owned_part = lax.psum_scatter(joined, ("node", "dev"), scatter_dimension=0, tiled=True)
-    gathered = lax.all_gather(owned_part, ("node", "dev"), axis=0, tiled=True)
-    results = []
-    offset = 0
-    for gradient in gradients:
-        results.append(gathered[offset : offset + gradient.size].reshape(gradient.shape))
-        offset = offset + gradient.size
-    return results
+    return lax.psum(gradients, AXES)
 
 
 def gelu_back(values, gradient):
@@ -155,8 +212,12 @@
     proj_pre = pointwise(pre_low, proj_in)
     mid_norm, mid_saved = norm_forward(proj_pre, valid_mask, norm_gain[1], norm_shift[1])
     mixer_low = jax.nn.gelu(mid_norm).astype(jnp.bfloat16)
-    large_conv = depthwise(mixer_low, kernel_large)
-    small_conv = depthwise(mixer_low, kernel_small)
+    canvas = image.shape[1]
+    mixer_waves = to_waves(mixer_low)
+    large_waves = kernel_waves(kernel_large, canvas)
+    small_waves = kernel_waves(kernel_small, canvas)
+    large_conv = from_waves(*times(large_waves, mixer_waves), canvas)
+    small_conv = from_waves(*times(small_waves, mixer_waves), canvas)
     large_norm, large_saved = norm_forward(large_conv, valid_mask, norm_gain[2], norm_shift[2])
     small_norm, small_saved = norm_forward(small_conv, valid_mask, norm_gain[3], norm_shift[3])
     merged = large_norm + small_norm
@@ -198,11 +259,13 @@
     )
     large_low = large_grad.astype(jnp.bfloat16)
     small_low = small_grad.astype(jnp.bfloat16)
-    grad_large = depthwise_kernel_grad(mixer_low, large_low, kernel_large.shape[0])
-    grad_small = depthwise_kernel_grad(mixer_low, small_low, kernel_small.shape[0])
-    mixer_back = depthwise_input_grad(large_low, kernel_large) + depthwise_input_grad(
-        small_low, kernel_small
-    )
+    large_grad_waves = to_waves(large_low)
+    small_grad_waves = to_waves(small_low)
+    grad_large = kernel_grad(mixer_waves, large_grad_waves, kernel_large.shape[0], canvas)
+    grad_small = kernel_grad(mixer_waves, small_grad_waves, kernel_small.shape[0], canvas)
+    back_large = times_conj(large_waves, large_grad_waves)
+    back_small = times_conj(small_waves, small_grad_waves)
+    mixer_back = from_waves(back_large[0] + back_small[0], back_large[1] + back_small[1], canvas)
     mid_grad = gelu_back(mid_norm, mixer_back)
     pre_grad, gain_mid, shift_mid = norm_backward(mid_grad, valid_mask, mid_saved, norm_gain[1])
     pre_round = pre_grad.astype(jnp.bfloat16)

time: 1960 us -> 702 us (0.36)
  matrix products: 814 us -> 120 us
  blocking collectives: 565 us -> 142 us
  waiting for transfers between devices: 406 us -> 185 us
  starting transfers between devices: 0.08 us -> 40.8 us
  other arithmetic: 60.8 us -> 88.8 us
    conv_general_dilated x6 -> x0, matrix products: 760 us -> none  [the longest x4 390 us: depthwise(): lax.conv_general_dilated(values, kernel[:, :, None, :], (1, 1), 'SAME', d...]
    psum x14 -> x1, blocking collectives: 565 us -> 43.4 us  [settle_joined(): return lax.psum(gradients, AXES)]
    unnamed x4 -> x1, waiting for transfers between devices: 406 us -> 0.02 us
    psum x0 -> x1, waiting for transfers between devices: none -> 155 us  [settle_joined(): return lax.psum(gradients, AXES)]
    all_to_all x0 -> x7, blocking collectives: none -> 99 us  [total(): lax.all_to_all(copies, AXES, 0, 0, tiled=True)]
    dot_general x0 -> x20, matrix products: none -> 59.6 us  [the longest x10 34 us: gather_back(): lax.dot_general(table, values, (((0,), (0,)), ((), ())), precision=lax.Pr...]
    all_to_all x0 -> x9, starting transfers between devices: none -> 40.8 us  [total(): lax.all_to_all(copies, AXES, 0, 0, tiled=True)]
    all_to_all x0 -> x9, waiting for transfers between devices: none -> 29.5 us  [total(): lax.all_to_all(copies, AXES, 0, 0, tiled=True)]
  transfers between devices with their start and end apart: 2 -> 10, of which waited for: 2 -> 6; matrix products, arithmetic and copies ran while one was open for 1% -> 16% of each run, Pallas kernels for 0% -> 0%
where the time goes in v1:
time: 702 us; the launch traced here: 697 us
  waiting for transfers between devices  185 us (26%)
  blocking collectives  142 us (20%)
  matrix products  120 us (17%)
  local copies, waits for them, and re-layouts  104 us (15%)
  other arithmetic  88.8 us (13%)
  starting transfers between devices  40.8 us (6%)
  between operations  15.5 us (2%)
    psum x1, waiting for transfers between devices, settle_joined(): return lax.psum(gradients, AXES)  155 us
    all_to_all x7, blocking collectives, total(): lax.all_to_all(copies, AXES, 0, 0, tiled=True)  99 us
    psum x1, blocking collectives, settle_joined(): return lax.psum(gradients, AXES)  43.4 us
    all_to_all x9, starting transfers between devices, total(): lax.all_to_all(copies, AXES, 0, 0, tiled=True)  40.8 us
    unnamed x173, local copies, waits for them, and re-layouts  40.6 us
    dot_general x10, matrix products, gather_back(): lax.dot_general(table, values, (((0,), (0,)), ((), ())), precision=lax.Pr...  34 us
    all_to_all x9, waiting for transfers between devices, total(): lax.all_to_all(copies, AXES, 0, 0, tiled=True)  29.5 us
    dot_general x10, matrix products, spread(): lax.dot_general(table, values, (((1,), (0,)), ((), ())), precision=lax.Pr...  25.5 us
  transfers between devices with their start and end apart: 10, of which 6 were waited for; matrix products, arithmetic and copies ran while one was open for 16% of the time, Pallas kernels for 0%

profile of v1, /device:TPU:0, one launch (start us, length us, event | category | flops | bytes accessed | tf_op | source)
XLA Modules:
  0.0 696.7 jit_solution(18234706864396516259)
XLA Ops:
  12.1 7.3 %all-to-all-start = ((f32[32,16,128]{2,1,0:T(8,128)}), f32[32,16,128]{2,1,0:T(8,128)S(1)}, u32[]{:S(2)}, u32[]{:S(2)}) async-start(f32[32,16,128]{2,1,0:T(8,128)} %broadcast_in_dim.49), calls=%async_computation | async-start | bytes 524288 | tf_op jit(solution)/shard_map/all_to_all | solution.py:127
  26.3 3.7 all-to-all-done
  79.0 6.4 fusion.23
  90.1 3.6 reshape.439
  98.1 5.8 all-to-all-start.3
  104.7 9.9 %all-to-all-done.3 = f32[32,16,128]{2,1,0:T(8,128)S(1)} async-done(((f32[32,16,128]{2,1,0:T(8,128)}), f32[32,16,128]{2,1,0:T(8,128)S(1)}, u32[]{:S(2)}, u32[]{:S(2)}) %all-to-all-start.3) | async-done | bytes 262176 | tf_op jit(solution)/shard_map/all_to_all | solution.py:127
  119.2 10.0 %all-to-all-done.2 = f32[32,16,128]{2,1,0:T(8,128)} async-done(((f32[32,16,128]{2,1,0:T(8,128)}), f32[32,16,128]{2,1,0:T(8,128)}, u32[]{:S(2)}, u32[]{:S(2)}) %all-to-all-start.2) | async-done | bytes 262176 | tf_op jit(solution)/shard_map/all_to_all | solution.py:127
  132.0 3.5 multiply_convert_fusion.7
  138.2 12.7 %all_to_all.80 = f32[32,16,128]{2,1,0:T(8,128)S(1)} all-to-all(f32[32,16,128]{2,1,0:T(8,128)S(1)} %broadcast_in_dim.57), channel_id=1, replica_groups=mesh['node'=4,'dev'=8] {'node','dev'}, dimensions={0} | all-to-all | bytes 524288 | tf_op jit(solution)/shard_map/all_to_all | solution.py:127
  152.2 3.6 fusion.101
  156.5 12.8 %all_to_all.81 = f32[32,16,128]{2,1,0:T(8,128)S(1)} all-to-all(f32[32,16,128]{2,1,0:T(8,128)S(1)} %broadcast_in_dim.59), channel_id=1, replica_groups=mesh['node'=4,'dev'=8] {'node','dev'}, dimensions={0} | all-to-all | bytes 524288 | tf_op jit(solution)/shard_map/all_to_all | solution.py:127
  170.6 7.4 %fusion = (f32[2048]{0:T(1024)S(1)}, f32[2048]{0:T(1024)S(1)}, f32[4,14,14,2048]{3,2,1,0:T(8,128)}) fusion(f32[4,14,14]{2,1,0:T(8,128)S(1)} %and_convert_fusion, bf16[512,2048]{1,0:T(8,128)(2,1)} %param.39, f32[4,14,14,512]{3,2,1,0:T(8,128)} %get-tuple-element.90, f32[512]{0:T(512)S(1)} %bitcast.411, f32[512]{0:T(512)S(1)} %bitcast.406, ...), kind=kOutput, calls=%fused_computation.4 | convolution fusion | flops 1652994048 | bytes 10153024 | tf_op jit(solution)/shard_map/dot_general | solution.py:19
  178.9 20.5 %all_to_all.82 = f32[32,40,128]{2,1,0:T(8,128)} all-to-all(f32[32,40,128]{2,1,0:T(8,128)S(1)} %broadcast_in_dim.61), channel_id=1, replica_groups=mesh['node'=4,'dev'=8] {'node','dev'}, dimensions={0} | all-to-all | bytes 1310720 | tf_op jit(solution)/shard_map/all_to_all | solution.py:127
  201.7 5.7 multiply_convert_fusion.1
  207.5 3.5 fusion.102
  211.7 13.8 %all_to_all.83 = f32[32,16,128]{2,1,0:T(8,128)S(1)} all-to-all(f32[32,16,128]{2,1,0:T(8,128)S(1)} %broadcast_in_dim.63), channel_id=1, replica_groups=mesh['node'=4,'dev'=8] {'node','dev'}, dimensions={0} | all-to-all | bytes 524288 | tf_op jit(solution)/shard_map/all_to_all | solution.py:127
  226.8 4.1 fusion.66
  230.9 10.4 %all_to_all.84 = f32[32,8,128]{2,1,0:T(8,128)S(1)} all-to-all(f32[32,8,128]{2,1,0:T(8,128)S(1)} %broadcast_in_dim.64), channel_id=1, replica_groups=mesh['node'=4,'dev'=8] {'node','dev'}, dimensions={0} | all-to-all | bytes 262144 | tf_op jit(solution)/shard_map/all_to_all | solution.py:127
  242.6 13.6 %fusion.121 = (f32[2048]{0:T(1024)S(1)}, f32[2048]{0:T(1024)S(1)}, f32[4,14,14,2048]{3,2,1,0:T(8,128)}) fusion(f32[2048]{0:T(1024)S(1)} %get-tuple-element.101, f32[4,14,14,2048]{3,2,1,0:T(8,128)} %get-tuple-element.162, f32[2048]{0:T(1024)S(1)} %get-tuple-element.100, f32[4,14,14]{2,1,0:T(8,128)S(1)} %and_convert_fusion, f32[2048]{0:T(1024)S(1)} %copy-done.70, ...), kind=kOutput, calls=%fused_computation.239 | convolution fusion | flops 1693937664 | bytes 17413188 | tf_op jit(solution)/shard_map/dot_general | solution.py:25
  256.2 17.6 %all_to_all.85 = f32[32,32,128]{2,1,0:T(8,128)S(1)} all-to-all(f32[32,32,128]{2,1,0:T(8,128)S(1)} %broadcast_in_dim.65), channel_id=1, replica_groups=mesh['node'=4,'dev'=8] {'node','dev'}, dimensions={0} | all-to-all | bytes 1048576 | tf_op jit(solution)/shard_map/all_to_all | solution.py:127
  275.1 7.6 %multiply_convert_fusion = bf16[4,14,14,2048]{3,2,1,0:T(8,128)(2,1)S(1)} fusion(f32[4,14,14,2048]{3,2,1,0:T(8,128)} %get-tuple-element.164, f32[4,14,14,2048]{3,2,1,0:T(8,128)} %get-tuple-element.162, f32[]{:T(128)} %bitcast.46, f32[2048]{0:T(1024)S(1)} %slice_bitcast_fusion, f32[2048]{0:T(1024)S(1)} %get-tuple-element.88, f32[2048]{0:T(1024)S(1)} %copy-done.52, ...), kind=kLoop, calls=%fused_computation.12 | loop fusion | flops 16056320 | bytes 16100420 | tf_op jit(solution)/shard_map/convert_element_type | solution.py:242
  282.8 3.4 multiply_reduce_fusion.17
  286.3 11.1 %all_to_all.86 = f32[32,8,128]{2,1,0:T(8,128)S(1)} all-to-all(f32[32,8,128]{2,1,0:T(8,128)S(1)} %broadcast_in_dim.66), channel_id=1, replica_groups=mesh['node'=4,'dev'=8] {'node','dev'}, dimensions={0} | all-to-all | bytes 262144 | tf_op jit(solution)/shard_map/all_to_all | solution.py:127
  298.1 5.3 multiply_reduce_fusion.16
  306.6 8.2 %convolution_bitcast_fusion = f32[2048,512]{1,0:T(8,128)} fusion(bf16[4,14,14,2048]{3,2,1,0:T(8,128)(2,1)} %copy-done.29, f32[4,14,14,512]{3,2,1,0:T(8,128)} %get-tuple-element.163, f32[]{:T(128)} %bitcast.51, f32[512]{0:T(512)S(1)} %get-tuple-element.132, f32[512]{0:T(512)S(1)} %get-tuple-element.131, f32[512]{0:T(512)S(1)} %bitcast.450, ...), kind=kOutput, calls=%fused_computation.17 | convolution fusion | flops 1648984064 | bytes 9827396 | tf_op jit(solution)/shard_map/dot_general | solution.py:34
  315.6 3.8 multiply_convert_fusion.5
  319.5 4.2 multiply_reduce_fusion.12
  324.4 6.2 all-to-all-start.12
  330.6 6.6 convolution_bitcast_fusion.1
  339.5 4.3 all-to-all-start.13
  347.7 4.3 all-to-all-done.13
  352.7 4.4 multiply_convert_fusion.4
  366.2 10.5 %fusion.16 = (f32[365,2048]{1,0:T(8,128)}, f32[365,2048]{1,0:T(8,128)}, f32[365,2048]{1,0:T(8,128)}, f32[365,2048]{1,0:T(8,128)}, f32[365,2048]{1,0:T(8,128)}) fusion(f32[365,2048]{1,0:T(8,128)S(1)} %copy-done.7, f32[2048,365]{0,1:T(8,128)} %fusion.141, f32[2048,365]{0,1:T(8,128)S(1)} %copy-done.4, f32[2048,365]{0,1:T(8,128)S(1)} %fusion.140, ...), kind=kOutput, calls=%fused_computation.30 | convolution fusion | flops 890296320 | bytes 30989776 | tf_op jit(solution)/shard_map/dot_general | solution.py:56
  377.2 6.6 fusion.10
  383.8 5.8 fusion.61
  389.6 3.3 reshape.458
  392.9 4.2 fusion.122
  400.4 5.3 add.263
  405.7 4.5 reduce_sum.548
  410.2 5.1 sub.305
  415.3 4.5 reduce_sum.549
  440.6 5.1 sub.309
  445.7 4.5 reduce_sum.551
  450.2 5.1 add.265
  455.3 3.7 reduce_sum.550
  463.4 5.9 all-to-all-start.15
  470.8 43.4 %psum.44 = f32[5,5,512]{2,1,0:T(8,128)} all-reduce(f32[5,5,512]{2,1,0:T(8,128)S(1)} %reshape.460), channel_id=1, replica_groups=mesh['node'=4,'dev'=8] {'node','dev'}, use_global_device_ids=true, to_apply=%region_54.55 | all-reduce | flops 12800 | bytes 102400 | tf_op jit(solution)/shard_map/psum | solution.py:185
  521.7 155.4 %all-reduce.12.cloned.1.call-done = (f32[512,512]{1,0:T(8,128)}, f32[31,31,512]{2,1,0:T(8,128)}, f32[512,512]{1,0:T(8,128)}, f32[512,2048]{1,0:T(8,128)}, f32[2048,512]{1,0:T(8,128)}) async-done(((f32[512,512]{1,0:T(8,128)}, f32[31,31,512]{2,1,0:T(8,128)}, f32[512,512]{1,0:T(8,128)}, f32[512,2048]{1,0:T(8,128)}, f32[2048,512]{1,0:T(8,128)}), (f32[512,512]{1,0:T(8,128)}, f32[31,31,512]{2,1,0:T(8,128)}, ...) | async-done | bytes 12453904 | tf_op jit(solution)/shard_map/psum | solution.py:185
  (311 shorter events, 163.0 us)
Async XLA Ops:
  7.2 200.3 %copy-start = (bf16[2048,512]{1,0:T(8,128)(2,1)S(1)}, bf16[2048,512]{1,0:T(8,128)(2,1)}, u32[]{:S(2)}) copy-start(bf16[2048,512]{1,0:T(8,128)(2,1)} %param.40) | copy-start | bytes 6291460
  12.1 17.9 %all-to-all-start = ((f32[32,16,128]{2,1,0:T(8,128)}), f32[32,16,128]{2,1,0:T(8,128)S(1)}, u32[]{:S(2)}, u32[]{:S(2)}) async-start(f32[32,16,128]{2,1,0:T(8,128)} %broadcast_in_dim.49), calls=%async_computation | async-start | bytes 524288 | tf_op jit(solution)/shard_map/all_to_all | solution.py:127
  20.4 11.0 %copy-start.62 = (f32[1,512]{1,0:T(1,128)}, f32[1,512]{1,0:T(1,128)S(1)}, u32[]{:S(2)}) copy-start(f32[1,512]{1,0:T(1,128)S(1)} %get-tuple-element.107) | copy-start | bytes 6148
  20.4 40.9 %copy-start.53 = (f32[1,512]{1,0:T(1,128)}, f32[1,512]{1,0:T(1,128)S(1)}, u32[]{:S(2)}) copy-start(f32[1,512]{1,0:T(1,128)S(1)} %get-tuple-element.106) | copy-start | bytes 6148
  23.1 8.3 %copy-start.25 = (bf16[4,14,14,512]{3,0,2,1:T(4,128)(2,1)S(1)}, bf16[4,14,14,512]{3,0,2,1:T(4,128)(2,1)}, u32[]{:S(2)}) copy-start(bf16[4,14,14,512]{3,0,2,1:T(4,128)(2,1)} %param.33) | copy-start | bytes 2408452
  23.1 8.3 %copy-start.71 = (f32[1,512]{1,0:T(1,128)}, f32[1,512]{1,0:T(1,128)S(1)}, u32[]{:S(2)}) copy-start(f32[1,512]{1,0:T(1,128)S(1)} %get-tuple-element.114) | copy-start | bytes 6148
  23.1 38.2 %copy-start.59 = (f32[1,512]{1,0:T(1,128)}, f32[1,512]{1,0:T(1,128)S(1)}, u32[]{:S(2)}) copy-start(f32[1,512]{1,0:T(1,128)S(1)} %get-tuple-element.113) | copy-start | bytes 6148
  34.6 7.3 %copy-start.50 = (bf16[5,5,512]{2,1,0:T(8,128)(2,1)S(1)}, bf16[5,5,512]{2,1,0:T(8,128)(2,1)}, u32[]{:S(2)}) copy-start(bf16[5,5,512]{2,1,0:T(8,128)(2,1)} %param.37) | copy-start | bytes 76804
  36.0 24.0 %all-to-all-start.1 = ((f32[32,16,128]{2,1,0:T(8,128)}), f32[32,16,128]{2,1,0:T(8,128)S(1)}, u32[]{:S(2)}, u32[]{:S(2)}) async-start(f32[32,16,128]{2,1,0:T(8,128)} %broadcast_in_dim.51), calls=%async_computation.1 | async-start | bytes 524288 | tf_op jit(solution)/shard_map/all_to_all | solution.py:127
  66.6 6.1 copy-start.2
  66.6 4.3 copy-start.12
  66.6 4.3 copy-start.34
  67.6 5.1 copy-start.5
  79.0 6.4 copy-start.3
  79.0 6.4 copy-start.6
  79.0 7.2 %copy-start.8 = (f32[46,8,4,512]{3,1,2,0:T(8,128)S(1)}, f32[46,8,4,512]{3,1,2,0:T(8,128)}, u32[]{:S(2)}) copy-start(f32[46,8,4,512]{3,1,2,0:T(8,128)} %copy.78) | copy-start | bytes 9043972
  79.0 8.1 %copy-start.10 = (f32[46,8,4,512]{3,1,2,0:T(8,128)S(1)}, f32[46,8,4,512]{3,1,2,0:T(8,128)}, u32[]{:S(2)}) copy-start(f32[46,8,4,512]{3,1,2,0:T(8,128)} %copy.80) | copy-start | bytes 9043972
  98.1 16.4 %all-to-all-start.3 = ((f32[32,16,128]{2,1,0:T(8,128)}), f32[32,16,128]{2,1,0:T(8,128)S(1)}, u32[]{:S(2)}, u32[]{:S(2)}) async-start(f32[32,16,128]{2,1,0:T(8,128)} %broadcast_in_dim.55), calls=%async_computation.3 | async-start | bytes 524288 | tf_op jit(solution)/shard_map/all_to_all | solution.py:127
  115.3 13.9 %all-to-all-start.2 = ((f32[32,16,128]{2,1,0:T(8,128)}), f32[32,16,128]{2,1,0:T(8,128)}, u32[]{:S(2)}, u32[]{:S(2)}) async-start(f32[32,16,128]{2,1,0:T(8,128)} %broadcast_in_dim.53), calls=%async_computation.2 | async-start | bytes 524288 | tf_op jit(solution)/shard_map/all_to_all | solution.py:127
  178.0 23.7 %copy-start.52 = (f32[2048]{0:T(1024)S(1)}, f32[2048]{0:T(1024)}, u32[]{:S(2)}) copy-start(f32[2048]{0:T(1024)} %param.43) | copy-start | bytes 24580
  178.0 23.7 %copy-start.70 = (f32[2048]{0:T(1024)S(1)}, f32[2048]{0:T(1024)}, u32[]{:S(2)}) copy-start(f32[2048]{0:T(1024)} %param.44) | copy-start | bytes 24580
  273.9 8.8 %copy-start.51 = (f32[2048]{0:T(1024)}, f32[2048]{0:T(1024)S(1)}, u32[]{:S(2)}) copy-start(f32[2048]{0:T(1024)S(1)} %slice_bitcast_fusion) | copy-start | bytes 24580
  275.1 7.6 %copy-start.18 = (f32[4,14,14,512]{3,2,1,0:T(8,128)S(1)}, f32[4,14,14,512]{3,2,1,0:T(8,128)}, u32[]{:S(2)}) copy-start(f32[4,14,14,512]{3,2,1,0:T(8,128)} %get-tuple-element.90) | copy-start | bytes 4816900
  275.1 7.6 %copy-start.73 = (bf16[512,2048]{1,0:T(8,128)(2,1)S(1)}, bf16[512,2048]{1,0:T(8,128)(2,1)}, u32[]{:S(2)}) copy-start(bf16[512,2048]{1,0:T(8,128)(2,1)} %param.39) | copy-start | bytes 6291460
  304.1 10.8 %all-to-all-start.11 = ((f32[32,8,128]{2,1,0:T(8,128)}), f32[32,8,128]{2,1,0:T(8,128)S(1)}, u32[]{:S(2)}, u32[]{:S(2)}) async-start(f32[32,8,128]{2,1,0:T(8,128)} %broadcast_in_dim.67), calls=%async_computation.11 | async-start | bytes 262144 | tf_op jit(solution)/shard_map/all_to_all | solution.py:127
  315.6 3.9 copy-start.19
  315.6 3.9 copy-start.21
  315.6 3.9 copy-start.75
  319.5 4.2 copy-start.43
  324.4 14.4 %all-to-all-start.12 = ((f32[32,8,128]{2,1,0:T(8,128)}), f32[32,8,128]{2,1,0:T(8,128)S(1)}, u32[]{:S(2)}, u32[]{:S(2)}) async-start(f32[32,8,128]{2,1,0:T(8,128)} %broadcast_in_dim.68), calls=%async_computation.12 | async-start | bytes 262144 | tf_op jit(solution)/shard_map/all_to_all | solution.py:127
  339.5 12.5 %all-to-all-start.13 = ((f32[32,8,128]{2,1,0:T(8,128)}), f32[32,8,128]{2,1,0:T(8,128)S(1)}, u32[]{:S(2)}, u32[]{:S(2)}) async-start(f32[32,8,128]{2,1,0:T(8,128)} %broadcast_in_dim.69), calls=%async_computation.13 | async-start | bytes 262144 | tf_op jit(solution)/shard_map/all_to_all | solution.py:127
  343.8 8.9 %copy-start.20 = (f32[14,14,4,512]{3,2,1,0:T(4,128)S(1)}, f32[14,14,4,512]{3,2,1,0:T(4,128)}, u32[]{:S(2)}) copy-start(f32[14,14,4,512]{3,2,1,0:T(4,128)} %reshape.443) | copy-start | bytes 4816900
  362.3 3.8 copy-start.7
  366.1 10.6 %copy-start.9 = (f32[46,8,4,512]{3,1,2,0:T(8,128)S(1)}, f32[46,8,4,512]{3,1,2,0:T(8,128)}, u32[]{:S(2)}) copy-start(f32[46,8,4,512]{3,1,2,0:T(8,128)} %copy.78) | copy-start | bytes 9043972
  366.1 10.6 %copy-start.11 = (f32[46,8,4,512]{3,1,2,0:T(8,128)S(1)}, f32[46,8,4,512]{3,1,2,0:T(8,128)}, u32[]{:S(2)}) copy-start(f32[46,8,4,512]{3,1,2,0:T(8,128)} %copy.80) | copy-start | bytes 9043972
  366.1 10.6 %copy-start.13 = (f32[46,8,4,512]{3,1,2,0:T(8,128)S(1)}, f32[46,8,4,512]{3,1,2,0:T(8,128)}, u32[]{:S(2)}) copy-start(f32[46,8,4,512]{3,1,2,0:T(8,128)} %copy.81) | copy-start | bytes 9043972
  366.1 11.0 %copy-start.15 = (f32[46,8,4,512]{3,1,2,0:T(8,128)S(1)}, f32[46,8,4,512]{3,1,2,0:T(8,128)}, u32[]{:S(2)}) copy-start(f32[46,8,4,512]{3,1,2,0:T(8,128)} %copy.82) | copy-start | bytes 9043972
  377.2 6.6 copy-start.16
  377.2 6.6 copy-start.17
  377.2 6.6 copy-start.31
  397.8 33.7 %all-to-all-start.14 = ((f32[32,8,128]{2,1,0:T(8,128)}), f32[32,8,128]{2,1,0:T(8,128)S(1)}, u32[]{:S(2)}, u32[]{:S(2)}) async-start(f32[32,8,128]{2,1,0:T(8,128)} %broadcast_in_dim.70), calls=%async_computation.14 | async-start | bytes 262144 | tf_op jit(solution)/shard_map/all_to_all | solution.py:127
  400.4 276.6 %all-reduce.12.cloned.1.call-start = ((), (), s32[]{:S(2)}) async-start(), calls=%async_computation.16 | async-start | bytes 25034752 | tf_op jit(solution)/shard_map/psum | solution.py:185
  455.3 3.8 copy-start.46
  455.3 4.1 copy-start.45
  459.4 9.9 %copy-start.49 = (f32[365,25]{1,0:T(8,128)S(1)}, f32[365,25]{1,0:T(8,128)}, u32[]{:S(2)}) copy-start(f32[365,25]{1,0:T(8,128)} %constant.61.clone) | copy-start | bytes 109504
  462.7 52.3 %copy-start.23 = (f32[4,14,14,512]{3,2,1,0:T(8,128)S(1)}, f32[4,14,14,512]{3,2,1,0:T(8,128)}, u32[]{:S(2)}) copy-start(f32[4,14,14,512]{3,2,1,0:T(8,128)} %get-tuple-element.87) | copy-start | bytes 4816900
  463.4 50.9 %all-to-all-start.15 = ((f32[32,8,128]{2,1,0:T(8,128)}), f32[32,8,128]{2,1,0:T(8,128)S(1)}, u32[]{:S(2)}, u32[]{:S(2)}) async-start(f32[32,8,128]{2,1,0:T(8,128)} %broadcast_in_dim.71), calls=%async_computation.15 | async-start | bytes 262144 | tf_op jit(solution)/shard_map/all_to_all | solution.py:127
  677.0 3.7 copy-start.41
  (38 other events, 105.8 us)
Sparse Core Ops, SparseCore 0:
  438.0 238.9 all-reduce.11

commit v2 on v0

v2 whole, which is shorter than its diff:
```python
import functools
import math

import jax
import jax.numpy as jnp
import ml_dtypes
import numpy as np
from jax import lax
from jax.experimental import pallas as pl
from jax.experimental.pallas import tpu as pltpu
from jax.sharding import PartitionSpec as P

EPSILON = 1e-05
ROOT = 0.7978845608028654
CUBIC = 0.044715
AXES = ("node", "chip", "core")
ROW = 16
F32 = jnp.float32
BF16 = jnp.bfloat16


def split(table):
    high = table.astype(ml_dtypes.bfloat16)
    low = (table - high.astype(np.float64)).astype(ml_dtypes.bfloat16)
    return high, low


@functools.lru_cache(maxsize=None)
def wave_tables(canvas, side_large, side_small):
    period = 2 * canvas - 1
    pairs = [(0, v) for v in range(canvas)]
    pairs += [(u, v) for u in range(1, canvas) for v in range(period)]
    waves = np.array(pairs)
    half = -(-len(pairs) // 16) * 16

    def table(places_h, places_w, keep, sign):
        grid = np.stack(np.meshgrid(places_h, places_w, indexing="ij"), -1).reshape(-1, 2)
        angle = 2 * np.pi * ((waves @ grid.T) % period) / period
        out = np.zeros((2 * half, grid.shape[0]))
        out[: len(pairs)] = np.cos(angle) * keep
        out[half : half + len(pairs)] = sign * np.sin(angle) * keep
        return out

    share = np.zeros((2 * half, 1))
    share[: len(pairs)] = 2.0 / period**2
    share[half : half + len(pairs)] = 2.0 / period**2
    share[0] = 1.0 / period**2

    inside = (np.arange(ROW) < canvas).astype(np.float64)
    cells = table(np.arange(canvas), np.arange(ROW), np.tile(inside, canvas), -1.0)

    def taps(side, row):
        middle = (side - 1) // 2
        offsets_h = np.arange(side) - middle
        offsets_w = np.arange(row) - middle
        keep = (np.abs(offsets_h) < canvas)[:, None] & (np.abs(offsets_w) < canvas)[None, :]
        keep = keep & (np.arange(row) < side)[None, :]
        return table(offsets_h, offsets_w, keep.reshape(-1).astype(np.float64), 1.0)

    def taps_back(side, row):
        first, count = used_rows(side, canvas)
        return taps(side, row)[:, first * row : (first + count) * row]

    def tap_row(side):
        return -(-side // 16) * 16

    large = taps(side_large, tap_row(side_large))
    small = taps(side_small, tap_row(side_small))
    turn = np.ones((2 * half, 1))
    turn[half:] = -1.0
    return dict(
        half=half,
        ahead=split(cells),
        back=split((cells * share).T),
        large=split(large),
        small=split(small),
        large_back=split((taps_back(side_large, 32) * turn * share).T),
        small_back=split((taps_back(side_small, 8) * turn * share).T),
    )


def used_rows(side, canvas):
    first = max(0, (side - 1) // 2 - (canvas - 1))
    return first, side - 2 * first


def dot(left, right):
    return jnp.dot(left, right, preferred_element_type=F32)


def dot_nt(left, right):
    return lax.dot_general(left, right, (((1,), (1,)), ((), ())), preferred_element_type=F32)


def dot_tn(left, right):
    return lax.dot_general(left, right, (((0,), (0,)), ((), ())), preferred_element_type=F32)


def halves(values):
    high = values.astype(BF16)
    return high, (values - high.astype(F32)).astype(BF16)


def gelu(values):
    inner = values * (ROOT + (ROOT * CUBIC) * (values * values))
    return values * (0.5 + 0.5 * jnp.tanh(inner))


def gelu_slope(values):
    square = values * values
    bend = jnp.tanh(values * (ROOT + (ROOT * CUBIC) * square))
    slope = ROOT + (3.0 * ROOT * CUBIC) * square
    return 0.5 + 0.5 * bend + values * slope * (0.5 - 0.5 * bend * bend)


def rows(at):
    return pl.ds(pl.multiple_of(at * ROW, ROW), ROW)


def fold(values):
    return values[:8] + values[8:]


def twice(values):
    return jnp.concatenate([values, values], axis=0)


def columns_inside(side, channels):
    places = lax.broadcasted_iota(jnp.int32, (ROW, 128), 0)
    inside = (places < side).astype(F32)
    return jnp.concatenate([inside] * (channels // 128), axis=1)


def first_step():
    return pl.program_id(0) == 0


def last_step():
    return pl.program_id(0) == pl.num_programs(0) - 1


def received(sent, width):
    summed = jnp.sum(sent[...], axis=0, keepdims=True)
    return [summed[:, at : at + width] for at in range(0, summed.shape[1], width)]


def keep(coefs, values):
    for at, value in enumerate(values):
        coefs[at] = jnp.broadcast_to(value, coefs.shape[1:])


def note(out, values):
    values = list(values)
    values += [jnp.zeros_like(values[0])] * (out.shape[0] - len(values))
    out[...] = jnp.concatenate(values, axis=0)


def add_sums(sums, parts):
    @pl.when(first_step())
    def _():
        sums[...] = jnp.zeros_like(sums)

    for at, part in enumerate(parts):
        sums[at] += part


def publish(sums, out, extra=()):
    @pl.when(last_step())
    def _():
        parts = [jnp.sum(sums[at], axis=0, keepdims=True) for at in range(sums.shape[0])]
        parts += list(extra)
        out[...] = jnp.broadcast_to(jnp.concatenate(parts, axis=1), out.shape)


def norm_coefs(column_sum, square, count, scaling, offsets):
    mean = column_sum / count
    reciprocal = lax.rsqrt(square / count - mean * mean + EPSILON)
    factor = scaling * reciprocal
    return mean, reciprocal, factor, offsets - mean * factor


def back_coefs(shift_sum, gain_sum, count, mean, reciprocal, scaling):
    factor = scaling * reciprocal
    slope = factor * reciprocal * gain_sum / count
    return factor, factor * shift_sum / count - slope * mean, slope


def zeros(count, channels):
    return tuple(jnp.zeros((8, channels), F32) for _ in range(count))


def enter_stage(sides, image, cotangent, x_out, u_out, sent, padded, sums):
    at_crop = pl.program_id(0)
    side = sides[at_crop]
    canvas, channels = image.shape[1], image.shape[3]
    inside = columns_inside(side, channels)

    @pl.when(first_step())
    def _():
        padded[...] = jnp.zeros_like(padded)

    def step(at, carry):
        mask = jnp.where(at < side, inside, 0.0)
        start = pl.multiple_of(at * ROW, ROW)
        padded[0, pl.ds(start, canvas), :] = image[0, at].astype(F32)
        padded[1, pl.ds(start, canvas), :] = cotangent[0, at].astype(F32)
        x = padded[0, rows(at), :] * mask
        u = padded[1, rows(at), :] * mask
        x_out[rows(at), :] = x.astype(BF16)
        u_out[rows(at), :] = u.astype(BF16)
        return carry[0] + fold(x), carry[1] + fold(x * x)

    add_sums(sums, lax.fori_loop(0, canvas, step, zeros(2, channels), unroll=7))
    count = jnp.int32(0)
    for at in range(sides.shape[0]):
        count += sides[at] * sides[at]
    publish(sums, sent, [jnp.full((1, 128), count.astype(F32))])


def first_stage(sides, came, scale, offset, x_in, weight, low_out, pre_out, sent, seen, coefs, sums):
    channels = x_in.shape[1]
    canvas = x_in.shape[0] // ROW
    side = sides[pl.program_id(0)]

    @pl.when(first_step())
    def _():
        parts = received(came, 128)
        tiles = channels // 128
        column_sum = jnp.concatenate(parts[:tiles], axis=1)
        square = jnp.concatenate(parts[tiles : 2 * tiles], axis=1)
        count = jnp.concatenate([parts[2 * tiles]] * tiles, axis=1)
        mean, reciprocal, factor, constant = norm_coefs(column_sum, square, count, scale[0:1], offset[0:1])
        keep(coefs, [factor, constant])
        note(seen, [count, mean, reciprocal, column_sum, square])

    inside = columns_inside(side, channels)
    factor, constant = twice(coefs[0]), twice(coefs[1])

    def step(at, carry):
        mask = jnp.where(at < side, inside, 0.0)
        low_out[rows(at), :] = (mask * (factor * x_in[rows(at), :].astype(F32) + constant)).astype(BF16)
        return carry

    lax.fori_loop(0, canvas, step, 0, unroll=7)
    pre_out[...] = dot(low_out[...], weight[...])

    def measure(at, carry):
        pre = pre_out[rows(at), :]
        return carry[0] + fold(pre), carry[1] + fold(pre * pre)

    add_sums(sums, lax.fori_loop(0, canvas, measure, zeros(2, channels), unroll=7))
    publish(sums, sent)


def times(spectrum, kernel, half, at, conj):
    real, imag = pl.ds(pl.multiple_of(at * 16, 16), 16), pl.ds(pl.multiple_of(half + at * 16, 16), 16)
    a, b = spectrum[real, :], spectrum[imag, :]
    c, d = kernel[real, :], kernel[imag, :]
    if conj:
        return real, imag, a * c + b * d, b * c - a * d
    return real, imag, a * c - b * d, a * d + b * c


def ahead(tables, values):
    return dot(tables[0][...], values) + dot(tables[1][...], values)


def back(tables, high, low):
    return dot(tables[0][...], high) + dot(tables[0][...], low) + dot(tables[1][...], high)


def mixer_stage(
    sides, came, seen, scale, offset, pre_in, ahead_t, back_t, large_w, small_w,
    low_out, large_out, small_out, sent, noted, coefs, sums, spectrum, high, low,
):
    channels = pre_in.shape[1]
    canvas = pre_in.shape[0] // ROW
    half = spectrum.shape[0] // 2
    side = sides[pl.program_id(0)]

    @pl.when(first_step())
    def _():
        mean, reciprocal, factor, constant = norm_coefs(
            *received(came, channels), seen[0:1], scale[1:2], offset[1:2]
        )
        keep(coefs, [factor, constant])
        note(noted, [mean, reciprocal])

    inside = columns_inside(side, channels)
    factor, constant = twice(coefs[0]), twice(coefs[1])

    def step(at, carry):
        mask = jnp.where(at < side, inside, 0.0)
        low_out[rows(at), :] = gelu(mask * (factor * pre_in[rows(at), :] + constant)).astype(BF16)
        return carry

    lax.fori_loop(0, canvas, step, 0, unroll=7)
    spectrum[...] = ahead(ahead_t, low_out[...])
    parts = ()
    for kernel, out in ((large_w, large_out), (small_w, small_out)):

        def product(at, carry):
            real, imag, new_real, new_imag = times(spectrum, kernel, half, at, False)
            high[real, :], low[real, :] = halves(new_real)
            high[imag, :], low[imag, :] = halves(new_imag)
            return carry

        lax.fori_loop(0, half // 16, product, 0, unroll=4)
        out[...] = back(back_t, high[...], low[...])

        def measure(at, carry):
            conv = jnp.where(at < side, inside, 0.0) * out[rows(at), :]
            out[rows(at), :] = conv
            return carry[0] + fold(conv), carry[1] + fold(conv * conv)

        parts += lax.fori_loop(0, canvas, measure, zeros(2, channels), unroll=7)
    add_sums(sums, parts)
    publish(sums, sent)


def merge_stage(
    sides, came, seen, scale, offset, large_in, small_in, x_in, u_in, weight,
    low_out, proj_out, sent, noted, coefs, sums,
):
    channels = x_in.shape[1]
    canvas = x_in.shape[0] // ROW
    side = sides[pl.program_id(0)]

    @pl.when(first_step())
    def _():
        large_sum, large_square, small_sum, small_square = received(came, channels)
        large = norm_coefs(large_sum, large_square, seen[0:1], scale[2:3], offset[2:3])
        small = norm_coefs(small_sum, small_square, seen[0:1], scale[3:4], offset[3:4])
        keep(coefs, [large[2], small[2], large[3] + small[3]])
        note(noted, [large[0], large[1], small[0], small[1], large[2], small[2], large[3] + small[3]])

    inside = columns_inside(side, channels)
    large, small, constant = twice(coefs[0]), twice(coefs[1]), twice(coefs[2])

    def step(at, carry):
        mask = jnp.where(at < side, inside, 0.0)
        merged = mask * (large * large_in[rows(at), :] + small * small_in[rows(at), :] + constant)
        low_out[rows(at), :] = gelu(merged).astype(BF16)
        return carry

    lax.fori_loop(0, canvas, step, 0, unroll=7)
    proj_out[...] = dot(low_out[...], weight[...])

    def measure(at, carry):
        proj = proj_out[rows(at), :]
        x, u = x_in[rows(at), :].astype(F32), u_in[rows(at), :].astype(F32)
        parts = (proj, proj * proj, proj * x, proj * u)
        return tuple(old + fold(part) for old, part in zip(carry, parts))

    add_sums(sums, lax.fori_loop(0, canvas, measure, zeros(4, channels), unroll=2))
    publish(sums, sent)


def widen_stage(
    sides, came, seen, scale, offset, x_in, proj_in, weight, low_out, hidden_out, sent, noted, coefs, sums
):
    channels = x_in.shape[1]
    canvas = x_in.shape[0] // ROW
    side = sides[pl.program_id(0)]

    @pl.when(first_step())
    def _():
        proj_sum, proj_square, cross, _ = parts = received(came, channels)
        count, x_mean, x_sum, x_square = seen[0:1], seen[1:2], seen[3:4], seen[4:5]
        mean, reciprocal, factor, constant = norm_coefs(
            proj_sum, proj_square, count, scale[4:5], offset[4:5]
        )
        mid_mean = x_mean + factor * mean + constant
        x_var = x_square / count - x_mean * x_mean
        proj_var = proj_square / count - mean * mean
        both = cross / count - x_mean * mean
        mid_var = x_var + factor * factor * proj_var + 2.0 * factor * both
        mid_reciprocal = lax.rsqrt(mid_var + EPSILON)
        mid_factor = scale[5:6] * mid_reciprocal
        keep(coefs, [mid_factor, mid_factor * factor, mid_factor * (constant - mid_mean) + offset[5:6]])
        note(noted, [mean, reciprocal, mid_mean, mid_reciprocal] + parts)

    inside = columns_inside(side, channels)
    from_x, from_proj, constant = twice(coefs[0]), twice(coefs[1]), twice(coefs[2])

    def step(at, carry):
        mask = jnp.where(at < side, inside, 0.0)
        x = x_in[rows(at), :].astype(F32)
        low_out[rows(at), :] = (mask * (from_x * x + from_proj * proj_in[rows(at), :] + constant)).astype(BF16)
        return carry

    lax.fori_loop(0, canvas, step, 0, unroll=7)
    parts = [[], []]
    for at_block in range(hidden_out.shape[1] // channels):
        block = slice(at_block * channels, (at_block + 1) * channels)
        hidden_out[:, block] = dot(low_out[...], weight[:, block])

        def measure(at, carry):
            hidden = hidden_out[rows(at), block]
            return carry[0] + fold(hidden), carry[1] + fold(hidden * hidden)

        found = lax.fori_loop(0, canvas, measure, zeros(2, channels), unroll=7)
        parts[0].append(found[0])
        parts[1].append(found[1])
    add_sums(sums, [jnp.concatenate(part, axis=1) for part in parts])
    hand_over(sums, sent)


def hand_over(sums, out):
    @pl.when(last_step())
    def _():
        out[...] = jnp.concatenate([jnp.sum(sums[at], axis=0, keepdims=True) for at in range(2)], axis=0)


def narrow_stage(
    sides, came, seen, wide_scale, wide_offset, hidden_in, u_in, weight, low_out, proj_out, sent, noted, coefs, sums
):
    channels = u_in.shape[1]
    canvas = u_in.shape[0] // ROW
    wide = hidden_in.shape[1]
    side = sides[pl.program_id(0)]

    @pl.when(first_step())
    def _():
        count = jnp.concatenate([seen[0:1]] * (wide // channels), axis=1)
        mean, reciprocal, factor, constant = norm_coefs(
            came[0:1], came[1:2], count, wide_scale[...], wide_offset[...]
        )
        keep(coefs, [factor, constant])
        note(noted, [mean, reciprocal, factor, constant, count])

    for at_block in range(wide // channels):
        block = slice(at_block * channels, (at_block + 1) * channels)
        factor, constant = twice(coefs[0, :, block]), twice(coefs[1, :, block])

        def step(at, carry):
            low_out[rows(at), block] = gelu(factor * hidden_in[rows(at), block] + constant).astype(BF16)
            return carry

        lax.fori_loop(0, canvas, step, 0, unroll=7)
    proj_out[...] = dot(low_out[...], weight[...])
    inside = columns_inside(side, channels)

    def measure(at, carry):
        proj = jnp.where(at < side, inside, 0.0) * proj_out[rows(at), :]
        proj_out[rows(at), :] = proj
        u = u_in[rows(at), :].astype(F32)
        parts = (proj, proj * proj, proj * u, u)
        return tuple(old + fold(part) for old, part in zip(carry, parts))

    add_sums(sums, lax.fori_loop(0, canvas, measure, zeros(4, channels), unroll=2))
    publish(sums, sent)


def wide_back_stage(
    sides, came, seen, wide_seen, scale, offset, proj_in, u_in, hidden_in, weight,
    down_out, grad_out, sent, noted, coefs, sums,
):
    channels = u_in.shape[1]
    canvas = u_in.shape[0] // ROW
    wide = hidden_in.shape[1]
    side = sides[pl.program_id(0)]

    @pl.when(first_step())
    def _():
        proj_sum, proj_square, cross, u_sum = received(came, channels)
        count = seen[0:1]
        mean, reciprocal, factor, constant = norm_coefs(
            proj_sum, proj_square, count, scale[6:7], offset[6:7]
        )
        gain_sum = reciprocal * (cross - mean * u_sum)
        keep(coefs, back_coefs(u_sum, gain_sum, count, mean, reciprocal, scale[6:7]))
        note(noted, [mean, reciprocal, u_sum, gain_sum, factor, constant])

    inside = columns_inside(side, channels)
    factor, constant, slope = twice(coefs[0]), twice(coefs[1]), twice(coefs[2])

    def step(at, carry):
        mask = jnp.where(at < side, inside, 0.0)
        u = u_in[rows(at), :].astype(F32)
        down_out[rows(at), :] = (mask * (factor * u - constant - slope * proj_in[rows(at), :])).astype(BF16)
        return carry

    lax.fori_loop(0, canvas, step, 0, unroll=7)
    parts = [[], []]
    for at_block in range(wide // channels):
        block = slice(at_block * channels, (at_block + 1) * channels)
        grad_out[:, block] = dot(down_out[...], weight[:, block])
        wide_factor = jnp.broadcast_to(wide_seen[2:3, block], (ROW, channels))
        wide_constant = jnp.broadcast_to(wide_seen[3:4, block], (ROW, channels))

        def measure(at, carry):
            hidden = hidden_in[rows(at), block]
            grad = grad_out[rows(at), block] * gelu_slope(wide_factor * hidden + wide_constant)
            grad_out[rows(at), block] = grad
            return carry[0] + fold(grad), carry[1] + fold(grad * hidden)

        found = lax.fori_loop(0, canvas, measure, zeros(2, channels))
        parts[0].append(found[0])
        parts[1].append(found[1])
    add_sums(sums, [jnp.concatenate(part, axis=1) for part in parts])
    hand_over(sums, sent)


def narrow_back_stage(
    sides, came, wide_seen, wide_scale, grad_in, hidden_in, x_in, proj_in, weight,
    up_out, ffn_out, sent, noted, coefs, sums,
):
    channels = x_in.shape[1]
    canvas = x_in.shape[0] // ROW
    wide = hidden_in.shape[1]
    side = sides[pl.program_id(0)]

    @pl.when(first_step())
    def _():
        mean, reciprocal, count = wide_seen[0:1], wide_seen[1:2], wide_seen[4:5]
        shift_sum = came[0:1]
        gain_sum = reciprocal * (came[1:2] - mean * shift_sum)
        keep(coefs, back_coefs(shift_sum, gain_sum, count, mean, reciprocal, wide_scale[...]))
        note(noted, [gain_sum, shift_sum])

    for at_block in range(wide // channels):
        block = slice(at_block * channels, (at_block + 1) * channels)
        factor, constant, slope = (twice(coefs[at, :, block]) for at in range(3))

        def step(at, carry):
            grad = factor * grad_in[rows(at), block] - constant - slope * hidden_in[rows(at), block]
            up_out[rows(at), block] = grad.astype(BF16)
            return carry

        lax.fori_loop(0, canvas, step, 0, unroll=7)
    ffn_out[...] = dot(up_out[...], weight[...])
    inside = columns_inside(side, channels)

    def measure(at, carry):
        grad = jnp.where(at < side, inside, 0.0) * ffn_out[rows(at), :]
        ffn_out[rows(at), :] = grad
        parts = (grad, grad * x_in[rows(at), :].astype(F32), grad * proj_in[rows(at), :])
        return tuple(old + fold(part) for old, part in zip(carry, parts))

    add_sums(sums, lax.fori_loop(0, canvas, measure, zeros(3, channels), unroll=2))
    publish(sums, sent)


def mid_back_stage(
    sides, came, seen, merge_seen, mid_seen, last_seen, scale, offset,
    x_in, u_in, proj_in, ffn_in, large_in, small_in, weight,
    resid_out, back_out, grad_out, sent, noted, coefs, sums,
):
    channels = x_in.shape[1]
    canvas = x_in.shape[0] // ROW
    side = sides[pl.program_id(0)]

    @pl.when(first_step())
    def _():
        ffn_sum, ffn_x, ffn_proj = received(came, channels)
        count, u_sum = seen[0:1], last_seen[2:3]
        mean, reciprocal, mid_mean, mid_reciprocal = (mid_seen[at : at + 1] for at in range(4))
        proj_sum, proj_square, cross, proj_u = (mid_seen[at : at + 1] for at in range(4, 8))
        proj_factor = scale[4:5] * reciprocal
        proj_constant = offset[4:5] - mean * proj_factor
        ffn_mid = ffn_x + proj_factor * ffn_proj + proj_constant * ffn_sum
        mid_gain = mid_reciprocal * (ffn_mid - mid_mean * ffn_sum)
        factor, constant, slope = back_coefs(ffn_sum, mid_gain, count, mid_mean, mid_reciprocal, scale[5:6])
        mid_proj = cross + proj_factor * proj_square + proj_constant * proj_sum
        resid_sum = u_sum
        resid_proj = proj_u + factor * ffn_proj - constant * proj_sum - slope * mid_proj
        gain = reciprocal * (resid_proj - mean * resid_sum)
        second = back_coefs(resid_sum, gain, count, mean, reciprocal, scale[4:5])
        keep(coefs, [factor, constant + slope * proj_constant, slope, slope * proj_factor, *second])
        note(noted, [mid_gain, ffn_sum, gain, resid_sum])

    inside = columns_inside(side, channels)

    def step(at, carry):
        mask = jnp.where(at < side, inside, 0.0)
        x, u = x_in[rows(at), :].astype(F32), u_in[rows(at), :].astype(F32)
        proj = proj_in[rows(at), :]
        resid = twice(coefs[0]) * ffn_in[rows(at), :] - twice(coefs[1]) - twice(coefs[2]) * x
        resid = u + mask * (resid - twice(coefs[3]) * proj)
        resid_out[rows(at), :] = resid
        down = twice(coefs[4]) * resid - twice(coefs[5]) - twice(coefs[6]) * proj
        back_out[rows(at), :] = (mask * down).astype(BF16)
        return carry

    lax.fori_loop(0, canvas, step, 0)
    grad_out[...] = dot(back_out[...], weight[...])
    large = jnp.broadcast_to(merge_seen[4:5], (ROW, channels))
    small = jnp.broadcast_to(merge_seen[5:6], (ROW, channels))
    constant = jnp.broadcast_to(merge_seen[6:7], (ROW, channels))

    def measure(at, carry):
        large_conv, small_conv = large_in[rows(at), :], small_in[rows(at), :]
        grad = grad_out[rows(at), :] * gelu_slope(large * large_conv + small * small_conv + constant)
        grad_out[rows(at), :] = grad
        parts = (grad, grad * large_conv, grad * small_conv)
        return tuple(old + fold(part) for old, part in zip(carry, parts))

    add_sums(sums, lax.fori_loop(0, canvas, measure, zeros(3, channels), unroll=2))
    publish(sums, sent)


def mixer_back_stage(
    sides, came, seen, merge_seen, first_seen, scale, offset, large_in, small_in, grad_in, pre_in,
    ahead_t, back_t, large_w, small_w,
    large_out, small_out, grad_out, sent, noted, coefs, sums, large_s, small_s, high, low,
):
    channels = pre_in.shape[1]
    canvas = pre_in.shape[0] // ROW
    half = large_s.shape[0] // 2
    side = sides[pl.program_id(0)]

    @pl.when(first_step())
    def _():
        shift_sum, with_large, with_small = received(came, channels)
        count = seen[0:1]
        large_mean, large_r, small_mean, small_r = (merge_seen[at : at + 1] for at in range(4))
        large_gain = large_r * (with_large - large_mean * shift_sum)
        small_gain = small_r * (with_small - small_mean * shift_sum)
        keep(
            coefs,
            [
                *back_coefs(shift_sum, large_gain, count, large_mean, large_r, scale[2:3]),
                *back_coefs(shift_sum, small_gain, count, small_mean, small_r, scale[3:4]),
            ],
        )
        note(noted, [large_gain, small_gain, shift_sum])

    inside = columns_inside(side, channels)

    def step(at, carry):
        mask = jnp.where(at < side, inside, 0.0)
        grad = grad_in[rows(at), :]
        large = twice(coefs[0]) * grad - twice(coefs[1]) - twice(coefs[2]) * large_in[rows(at), :]
        small = twice(coefs[3]) * grad - twice(coefs[4]) - twice(coefs[5]) * small_in[rows(at), :]
        large_out[rows(at), :] = (mask * large).astype(BF16)
        small_out[rows(at), :] = (mask * small).astype(BF16)
        return carry

    lax.fori_loop(0, canvas, step, 0)
    large_s[...] = ahead(ahead_t, large_out[...])
    small_s[...] = ahead(ahead_t, small_out[...])

    def product(at, carry):
        real, imag, one_real, one_imag = times(large_s, large_w, half, at, True)
        _, _, two_real, two_imag = times(small_s, small_w, half, at, True)
        high[real, :], low[real, :] = halves(one_real + two_real)
        high[imag, :], low[imag, :] = halves(one_imag + two_imag)
        return carry

    lax.fori_loop(0, half // 16, product, 0, unroll=4)
    grad_out[...] = back(back_t, high[...], low[...])
    reciprocal = first_seen[1:2]
    factor = scale[1:2] * reciprocal
    constant = jnp.broadcast_to(offset[1:2] - first_seen[0:1] * factor, (ROW, channels))
    factor = jnp.broadcast_to(factor, (ROW, channels))

    def measure(at, carry):
        mask = jnp.where(at < side, inside, 0.0)
        pre = pre_in[rows(at), :]
        grad = mask * grad_out[rows(at), :] * gelu_slope(factor * pre + constant)
        grad_out[rows(at), :] = grad
        return carry[0] + fold(grad), carry[1] + fold(grad * pre)

    add_sums(sums, lax.fori_loop(0, canvas, measure, zeros(2, channels)))
    publish(sums, sent)


def first_back_stage(
    sides, came, seen, first_seen, scale, grad_in, pre_in, x_in, weight,
    low_out, grad_out, sent, noted, coefs, sums,
):
    channels = pre_in.shape[1]
    canvas = pre_in.shape[0] // ROW
    side = sides[pl.program_id(0)]

    @pl.when(first_step())
    def _():
        shift_sum, with_pre = received(came, channels)
        mean, reciprocal = first_seen[0:1], first_seen[1:2]
        gain_sum = reciprocal * (with_pre - mean * shift_sum)
        keep(coefs, back_coefs(shift_sum, gain_sum, seen[0:1], mean, reciprocal, scale[1:2]))
        note(noted, [gain_sum, shift_sum])

    inside = columns_inside(side, channels)
    factor, constant, slope = twice(coefs[0]), twice(coefs[1]), twice(coefs[2])

    def step(at, carry):
        mask = jnp.where(at < side, inside, 0.0)
        grad = factor * grad_in[rows(at), :] - constant - slope * pre_in[rows(at), :]
        low_out[rows(at), :] = (mask * grad).astype(BF16)
        return carry

    lax.fori_loop(0, canvas, step, 0, unroll=7)
    grad_out[...] = dot(low_out[...], weight[...])

    def measure(at, carry):
        grad = grad_out[rows(at), :]
        return carry[0] + fold(grad), carry[1] + fold(grad * x_in[rows(at), :].astype(F32))

    add_sums(sums, lax.fori_loop(0, canvas, measure, zeros(2, channels), unroll=7))
    publish(sums, sent)


def leave_stage(sides, came, seen, scale, resid_in, grad_in, x_in, image_out, noted, coefs):
    channels = x_in.shape[1]
    canvas = x_in.shape[0] // ROW
    side = sides[pl.program_id(0)]

    @pl.when(first_step())
    def _():
        shift_sum, with_x = received(came, channels)
        count, mean, reciprocal = (seen[at : at + 1] for at in range(3))
        gain_sum = reciprocal * (with_x - mean * shift_sum)
        keep(coefs, back_coefs(shift_sum, gain_sum, count, mean, reciprocal, scale[0:1]))
        note(noted, [gain_sum, shift_sum])

    inside = columns_inside(side, channels)
    factor, constant, slope = twice(coefs[0]), twice(coefs[1]), twice(coefs[2])

    def step(at, carry):
        mask = jnp.where(at < side, inside, 0.0)
        grad = factor * grad_in[rows(at), :] - constant - slope * x_in[rows(at), :].astype(F32)
        image_out[0, at] = (mask * (resid_in[rows(at), :] + grad))[:canvas]
        return carry

    lax.fori_loop(0, canvas, step, 0, unroll=7)


def block_out_stage(sides, mid_seen, last_seen, scale, offset, x_in, mid_in, last_in, out):
    channels = x_in.shape[1]
    canvas = x_in.shape[0] // ROW
    side = sides[pl.program_id(0)]
    inside = columns_inside(side, channels)
    factor = scale[4:5] * mid_seen[1:2]
    constant = offset[4:5] - mid_seen[0:1] * factor + last_seen[5:6]
    constant = jnp.broadcast_to(constant, (ROW, channels))
    factor = jnp.broadcast_to(factor, (ROW, channels))
    last = jnp.broadcast_to(last_seen[4:5], (ROW, channels))

    def step(at, carry):
        mask = jnp.where(at < side, inside, 0.0)
        added = factor * mid_in[rows(at), :] + last * last_in[rows(at), :] + constant
        out[0, at] = (x_in[rows(at), :].astype(F32) + mask * added)[:canvas].astype(BF16)
        return carry

    lax.fori_loop(0, canvas, step, 0, unroll=7)


def kernel_waves_stage(large, small, large_t, small_t, large_out, small_out, large_rows, small_rows):
    for kernel, table, out, flat in (
        (large, large_t, large_out, large_rows),
        (small, small_t, small_out, small_rows),
    ):
        side = kernel.shape[0]
        row = flat.shape[0] // side
        flat[...] = jnp.zeros_like(flat)
        for at in range(side):
            flat[at * row : at * row + side, :] = kernel[at]
        out[...] = ahead(table, flat[...])


def kernel_grad_stage(
    place, mixer, large, small, merged, merged_grad, ahead_t, large_t, small_t, other_out, mine_out,
    mixer_s, grad_s, large_sum, small_sum, flat, proj_sum,
):
    half = mixer_s.shape[0] // 2
    at_crop = pl.program_id(0)
    proj = dot_tn(merged[...], merged_grad[...])

    @pl.when(at_crop == 0)
    def _():
        proj_sum[...] = proj

    @pl.when(at_crop != 0)
    def _():
        proj_sum[...] += proj

    mixer_s[...] = ahead(ahead_t, mixer[...])
    for grad, total in ((large, large_sum), (small, small_sum)):
        grad_s[...] = ahead(ahead_t, grad[...])

        def product(at, carry):
            real, imag, new_real, new_imag = times(mixer_s, grad_s, half, at, True)

            @pl.when(at_crop == 0)
            def _():
                total[real, :] = new_real
                total[imag, :] = new_imag

            @pl.when(at_crop != 0)
            def _():
                total[real, :] += new_real
                total[imag, :] += new_imag

            return carry

        lax.fori_loop(0, half // 16, product, 0, unroll=4)

    @pl.when(last_step())
    def _():
        start = 0
        for total, table in ((large_sum, large_t), (small_sum, small_t)):
            size = table[0].shape[0]
            flat[start : start + size, :] = back(table, *halves(total[...]))
            start += size
        flat[start:, :] = jnp.zeros((flat.shape[0] - start, flat.shape[1]), F32)
        size, rest = flat.shape[0] // 2, proj_sum.shape[0] // 2
        for out, core in ((mine_out, place[0]), (other_out, 1 - place[0])):
            out[:size, :] = flat[pl.ds(pl.multiple_of(core * size, 8), size), :]
            out[size:, :] = proj_sum[pl.ds(pl.multiple_of(core * rest, 8), rest), :]


def kernel_grad_out_stage(settled, large_out, small_out, proj_out, flat, *, canvas):
    rest = proj_out.shape[0] // 2
    size = settled.shape[0] // 2 - rest
    for core in range(2):
        start = core * (size + rest)
        flat[core * size : (core + 1) * size, :] = settled[start : start + size, :]
        proj_out[core * rest : (core + 1) * rest, :] = settled[start + size : start + size + rest, :]
    start = 0
    for out, row in ((large_out, 32), (small_out, 8)):
        side = out.shape[0]
        first, count = used_rows(side, canvas)
        for at in range(side):
            if first <= at < first + count:
                out[at] = flat[start : start + side, :]
                start += row
            else:
                out[at] = jnp.zeros(out.shape[1:], F32)


def weight_grad_stage(place, inputs, gradient, out):
    out[...] = dot_tn(inputs[...], gradient[...])


SMEM = pl.BlockSpec(memory_space=pltpu.SMEM)


def whole(shape):
    return pl.BlockSpec(shape, lambda at: (0,) * len(shape))


VMEM = 62 * 1024 * 1024


def call(kernel, crops, ins, outs, scratch):
    def spec(shape, kind):
        if kind == "smem":
            return SMEM
        if kind == "rows":
            return pl.BlockSpec((shape[0] // crops, shape[1]), lambda at: (at, 0))
        if kind == "map":
            return pl.BlockSpec((1,) + tuple(shape[1:]), lambda at: (at, 0, 0, 0))
        return whole(tuple(shape))

    flat, specs, places = [], [], []
    for value, kind in ins:
        group = value if isinstance(value, tuple) else (value,)
        places.append((len(flat), len(group) if isinstance(value, tuple) else 0))
        for part in group:
            flat.append(part)
            specs.append(spec(part.shape, kind))

    def body(*refs):
        given = [refs[at : at + size] if size else refs[at] for at, size in places]
        kernel(*given, *refs[len(flat) :])

    return pl.pallas_call(
        body,
        grid=(crops,),
        in_specs=specs,
        out_specs=[spec(shape, kind) for shape, _, kind in outs],
        out_shape=[jax.ShapeDtypeStruct(shape, dtype) for shape, dtype, _ in outs],
        scratch_shapes=[pltpu.VMEM(shape, dtype) for shape, dtype in scratch],
        compiler_params=pltpu.CompilerParams(
            dimension_semantics=("arbitrary",), vmem_limit_bytes=VMEM
        ),
        cost_estimate=pl.CostEstimate(
            flops=0,
            bytes_accessed=sum(part.size * part.dtype.itemsize for part in flat)
            + sum(math.prod(shape) * jnp.dtype(dtype).itemsize for shape, dtype, _ in outs),
            transcendentals=0,
        ),
        name=getattr(kernel, "func", kernel).__name__,
    )(*flat)


def weight_grad(inputs, gradient, place=None):
    deep, high = inputs.shape
    wide = gradient.shape[1]
    if place is None:
        place = jnp.zeros((1,), jnp.int32)
    else:
        high = high // 2
    block, across = min(high, 512), min(wide, 512)
    return pl.pallas_call(
        weight_grad_stage,
        grid_spec=pltpu.PrefetchScalarGridSpec(
            num_scalar_prefetch=1,
            grid=(high // block, wide // across),
            in_specs=[
                pl.BlockSpec((deep, block), lambda i, j, place: (0, place[0] * (high // block) + i)),
                pl.BlockSpec((deep, across), lambda i, j, place: (0, j)),
            ],
            out_specs=pl.BlockSpec((block, across), lambda i, j, place: (i, j)),
        ),
        out_shape=jax.ShapeDtypeStruct((high, wide), F32),
        compiler_params=pltpu.CompilerParams(
            dimension_semantics=("arbitrary", "arbitrary"), vmem_limit_bytes=VMEM
        ),
        cost_estimate=pl.CostEstimate(
            flops=2 * deep * high * wide,
            bytes_accessed=2 * deep * (high + wide) + 4 * high * wide,
            transcendentals=0,
        ),
        name="weight_grad_stage",
    )(place, inputs, gradient)


def exchange(sent):
    return lax.all_to_all(sent, AXES, 0, 0, tiled=True)


SWAP = [(0, 1), (1, 0)]


def wide_exchange(sums):
    core = lax.axis_index("core")
    mine = lax.dynamic_index_in_dim(sums, core, 0, False)
    other = lax.dynamic_index_in_dim(sums, 1 - core, 0, False)
    mine = mine + lax.ppermute(other, "core", SWAP)
    chips = lax.axis_size(("node", "chip"))
    copies = jnp.broadcast_to(mine[None], (chips,) + mine.shape)
    mine = jnp.sum(lax.all_to_all(copies, ("node", "chip"), 0, 0, tiled=True), axis=0)
    other = lax.ppermute(mine, "core", SWAP)
    return jnp.where(core == 0, jnp.stack([mine, other]), jnp.stack([other, mine]))


def sum_and_cut(arrays, place, ways):
    count, wide = arrays[0].shape
    part = count // ways

    def body(place, *refs):
        total = refs[0][...]
        for ref in refs[1 : len(arrays)]:
            total = total + ref[...]
        for at, out in enumerate(refs[len(arrays) :]):

            @pl.when(pl.program_id(0) == at)
            def _():
                out[...] = total

    return pl.pallas_call(
        body,
        grid_spec=pltpu.PrefetchScalarGridSpec(
            num_scalar_prefetch=1,
            grid=(ways,),
            in_specs=[pl.BlockSpec((part, wide), lambda at, place: (place[0] ^ at, 0))] * len(arrays),
            out_specs=[pl.BlockSpec((part, wide), lambda at, place: (0, 0))] * ways,
        ),
        out_shape=[jax.ShapeDtypeStruct((part, wide), F32)] * ways,
        compiler_params=pltpu.CompilerParams(dimension_semantics=("arbitrary",), vmem_limit_bytes=VMEM),
        cost_estimate=pl.CostEstimate(
            flops=0, bytes_accessed=4 * count * wide * (len(arrays) + 1), transcendentals=0
        ),
        name="sum_and_cut",
    )(place, *arrays)


def join(parts, place):
    part, wide = parts[0].shape
    ways = len(parts)

    def body(place, *refs):
        for at, ref in enumerate(refs[:ways]):

            @pl.when(pl.program_id(0) == at)
            def _():
                refs[ways][...] = ref[...]

    return pl.pallas_call(
        body,
        grid_spec=pltpu.PrefetchScalarGridSpec(
            num_scalar_prefetch=1,
            grid=(ways,),
            in_specs=[pl.BlockSpec((part, wide), lambda at, place: (0, 0))] * ways,
            out_specs=pl.BlockSpec((part, wide), lambda at, place: (place[0] ^ at, 0)),
        ),
        out_shape=jax.ShapeDtypeStruct((ways * part, wide), F32),
        compiler_params=pltpu.CompilerParams(dimension_semantics=("arbitrary",), vmem_limit_bytes=VMEM),
        cost_estimate=pl.CostEstimate(flops=0, bytes_accessed=8 * ways * part * wide, transcendentals=0),
        name="join",
    )(place, *parts)


def place_on(axis):
    return lax.axis_index(axis)[None]


def across(parts, axis):
    size = lax.axis_size(axis)
    return [
        lax.ppermute(part, axis, [(at, at ^ k) for at in range(size)]) if k else part
        for k, part in enumerate(parts)
    ]


class Settle:
    def __init__(self, other, mine, steps):
        half = mine.shape[0]
        self.first = mine
        if half % (8 * lax.axis_size(("node", "chip"))):
            first = lax.axis_index("core") == 0
            both = jnp.where(first, jnp.concatenate([mine, other]), jnp.concatenate([other, mine]))
            self.value = lax.psum(both, AXES)
            self.steps = []
        else:
            self.parts = [mine, lax.ppermute(other, "core", SWAP)]
            self.steps = list(steps)

    def chip(self):
        self.cut("chip")

    def node(self):
        self.cut("node")

    def cut(self, axis):
        self.parts = sum_and_cut(self.parts, place_on(axis), lax.axis_size(axis))
        self.mark = self.parts[0]
        self.parts = across(self.parts, axis)

    def piece(self):
        (self.mark,) = sum_and_cut(self.parts, place_on("node") * 0, 1)
        self.parts = across([self.mark] * lax.axis_size("node"), "node")

    def gather(self):
        (self.mark,) = sum_and_cut(self.parts, place_on("node") * 0, 1)
        self.value = lax.all_gather(self.mark, ("core", "chip", "node"), axis=0, tiled=True)

    def to_chip(self):
        self.join("node", "chip")

    def to_core(self):
        self.join("chip", "core")

    def end(self):
        self.value = self.mark = join(self.parts, place_on("core"))

    def join(self, axis, onward):
        self.mark = join(self.parts, place_on(axis))
        self.parts = across([self.mark] * lax.axis_size(onward), onward)

    def step(self, token):
        if not self.steps:
            return token
        self.parts, token = lax.optimization_barrier((self.parts, token))
        getattr(self, self.steps.pop(0))()
        return self.mark


BY_PERMUTES = ("chip", "node", "piece", "to_chip", "to_core", "end")
BY_GATHER = ("chip", "node", "gather")


def settle_weight_grad(inputs, gradient, steps):
    core = place_on("core")
    other = weight_grad(inputs, gradient, 1 - core)
    gradient, other = lax.optimization_barrier((gradient, other))
    mine = weight_grad(inputs, gradient, core)
    return Settle(other, mine, steps)


def together(value, *tokens):
    return lax.optimization_barrier((value, tokens))[0]


def local(
    image, crop_sides, proj_in, kernel_large, kernel_small, proj_out, proj_up, proj_down,
    norm_gain, norm_shift, wide_gain, wide_shift, cotangent,
):
    crops, canvas, _, channels = image.shape
    wide = proj_up.shape[1]
    devices = lax.axis_size(AXES)
    cells = crops * canvas * ROW
    tables = wave_tables(canvas, kernel_large.shape[0], kernel_small.shape[0])
    half = tables["half"]

    def const(name):
        return tuple(jnp.asarray(part) for part in tables[name])

    ahead_t, back_t = const("ahead"), const("back")
    sides = (crop_sides, "smem")
    scale, offset = (norm_gain, "whole"), (norm_shift, "whole")
    wide_scale, wide_offset = (wide_gain[None], "whole"), (wide_shift[None], "whole")
    full, full_low = ((cells, channels), F32, "rows"), ((cells, channels), BF16, "rows")
    wide_full, wide_low = ((cells, wide), F32, "rows"), ((cells, wide), BF16, "rows")
    seen_out, wide_seen_out = ((8, channels), F32, "whole"), ((8, wide), F32, "whole")

    def send(count):
        return ((devices, count), F32, "whole")

    def coefs(count, width=channels):
        return ((count, 8, width), F32)

    def run(kernel, ins, outs, scratch):
        return call(kernel, crops, ins, outs, scratch)

    def r(value):
        return (value, "rows")

    def w(value):
        return (value, "whole")

    x, u, sent = run(
        enter_stage,
        [sides, (image, "map"), (cotangent, "map")],
        [full_low, full_low, send(2 * channels + 128)],
        [((2, canvas * ROW, channels), F32), coefs(2)],
    )
    came = exchange(sent)
    spectrum_out = ((2 * half, channels), F32, "whole")
    large_w, small_w = call(
        kernel_waves_stage,
        1,
        [w(kernel_large), w(kernel_small), w(const("large")), w(const("small"))],
        [spectrum_out, spectrum_out],
        [
            ((tables["large"][0].shape[1], channels), BF16),
            ((tables["small"][0].shape[1], channels), BF16),
        ],
    )
    pre_low, pre, sent, seen = run(
        first_stage,
        [sides, w(came), scale, offset, r(x), w(proj_in)],
        [full_low, full, send(2 * channels), seen_out],
        [coefs(2), coefs(2)],
    )
    spectrum = ((2 * half, channels), F32)
    spectrum_low = ((2 * half, channels), BF16)
    mixer_low, large, small, sent, first_seen = run(
        mixer_stage,
        [sides, w(exchange(sent)), w(seen), scale, offset, r(pre), w(ahead_t), w(back_t), w(large_w), w(small_w)],
        [full_low, full, full, send(4 * channels), seen_out],
        [coefs(2), coefs(4), spectrum, spectrum_low, spectrum_low],
    )
    merged_low, proj, sent, merge_seen = run(
        merge_stage,
        [sides, w(exchange(sent)), w(seen), scale, offset, r(large), r(small), r(x), r(u), w(proj_out)],
        [full_low, full, send(4 * channels), seen_out],
        [coefs(3), coefs(4)],
    )
    ffn_low, hidden, sent, mid_seen = run(
        widen_stage,
        [sides, w(exchange(sent)), w(seen), scale, offset, r(x), r(proj), w(proj_up)],
        [full_low, wide_full, ((2, wide), F32, "whole"), seen_out],
        [coefs(3), coefs(2, wide)],
    )
    hidden_low, last, sent, wide_seen = run(
        narrow_stage,
        [sides, w(wide_exchange(sent)), w(seen), wide_scale, wide_offset, r(hidden), r(u), w(proj_down)],
        [wide_low, full, send(4 * channels), wide_seen_out],
        [coefs(2, wide), coefs(4)],
    )
    down_low, hidden_grad, sent, last_seen = run(
        wide_back_stage,
        [sides, w(exchange(sent)), w(seen), w(wide_seen), scale, offset, r(last), r(u), r(hidden), w(proj_down.T)],
        [full_low, wide_full, ((2, wide), F32, "whole"), seen_out],
        [coefs(3), coefs(2, wide)],
    )
    came = wide_exchange(sent)
    grad_down = weight_grad(hidden_low, down_low)
    came = together(came, grad_down)
    up_low, ffn_grad, sent, wide_noted = run(
        narrow_back_stage,
        [sides, w(came), w(wide_seen), wide_scale, r(hidden_grad), r(hidden), r(x), r(proj), w(proj_up.T)],
        [wide_low, full, send(3 * channels), wide_seen_out],
        [coefs(3, wide), coefs(3)],
    )
    came = exchange(sent)
    grad_up = weight_grad(ffn_low, up_low)
    came = together(came, grad_up)
    grad_down, grad_up = lax.psum((grad_down, grad_up), AXES)
    resid_grad, back_low, merged_grad, sent, mid_noted = run(
        mid_back_stage,
        [
            sides, w(came), w(seen), w(merge_seen), w(mid_seen), w(last_seen), scale, offset,
            r(x), r(u), r(proj), r(ffn_grad), r(large), r(small), w(proj_out.T),
        ],
        [full, full_low, full, send(3 * channels), seen_out],
        [coefs(7), coefs(3)],
    )
    came = exchange(sent)
    large_low, small_low, mixer_grad, sent, mixer_noted = run(
        mixer_back_stage,
        [
            sides, w(came), w(seen), w(merge_seen), w(first_seen), scale, offset,
            r(large), r(small), r(merged_grad), r(pre), w(ahead_t), w(back_t), w(large_w), w(small_w),
        ],
        [full_low, full_low, full, send(2 * channels), seen_out],
        [coefs(6), coefs(2), spectrum, spectrum, spectrum_low, spectrum_low],
    )
    came = exchange(sent)
    taps_t = (const("large_back"), const("small_back"))
    tap_rows = sum(table[0].shape[0] for table in taps_t)
    tap_rows = -(-tap_rows // (16 * devices)) * 16 * devices
    half_taps = (((tap_rows + channels) // 2, channels), F32, "whole")
    other, mine = run(
        kernel_grad_stage,
        [
            (place_on("core"), "smem"), r(mixer_low), r(large_low), r(small_low), r(merged_low), r(back_low),
            w(ahead_t), w(taps_t[0]), w(taps_t[1]),
        ],
        [half_taps, half_taps],
        [spectrum, spectrum, spectrum, spectrum, ((tap_rows, channels), F32), ((channels, channels), F32)],
    )
    settle_taps = Settle(other, mine, BY_PERMUTES)
    came = together(came, settle_taps.step(sent))
    pre_round, first_grad, sent, first_noted = run(
        first_back_stage,
        [sides, w(came), w(seen), w(first_seen), scale, r(mixer_grad), r(pre), r(x), w(proj_in.T)],
        [full_low, full, send(2 * channels), seen_out],
        [coefs(3), coefs(2)],
    )
    settle_in = settle_weight_grad(pre_low, pre_round, BY_PERMUTES)
    came = exchange(together(sent, settle_in.first))
    token = settle_in.step(settle_taps.step(settle_in.first))
    (block_out,) = run(
        block_out_stage,
        [sides, w(mid_seen), w(last_seen), scale, offset, r(x), r(proj), r(together(last, token))],
        [(image.shape, BF16, "map")],
        [],
    )
    token = settle_in.step(settle_taps.step(block_out))
    came = together(came, token)
    grad_image, enter_noted = run(
        leave_stage,
        [sides, w(came), w(seen), scale, r(resid_grad), r(first_grad), r(x)],
        [(image.shape, F32, "map"), seen_out],
        [coefs(3)],
    )
    token = grad_image
    while settle_in.steps or settle_taps.steps:
        token = settle_in.step(settle_taps.step(token))
    grad_in = settle_in.value
    grad_large, grad_small, grad_out = call(
        functools.partial(kernel_grad_out_stage, canvas=canvas),
        1,
        [w(settle_taps.value)],
        [(kernel_large.shape, F32, "whole"), (kernel_small.shape, F32, "whole"), (proj_out.shape, F32, "whole")],
        [((tap_rows, channels), F32)],
    )
    gain_grads = jnp.stack(
        [enter_noted[0], first_noted[0], mixer_noted[0], mixer_noted[1], mid_noted[2], mid_noted[0], last_seen[3]]
    )
    shift_grads = jnp.stack(
        [enter_noted[1], first_noted[1], mixer_noted[2], mixer_noted[2], mid_noted[3], mid_noted[1], last_seen[2]]
    )
    return (
        block_out, grad_image, grad_in, grad_large, grad_small, grad_out, grad_up, grad_down,
        gain_grads, shift_grads, wide_noted[0], wide_noted[1],
    )


def solution(mesh):
    nodes, devices = mesh.devices.shape
    chips = jax.sharding.Mesh(mesh.devices.reshape(nodes, devices // 2, 2), AXES)
    maps = P(AXES, None, None, None)
    return jax.shard_map(
        local,
        mesh=chips,
        in_specs=(maps, P(AXES)) + (P(),) * 10 + (maps,),
        out_specs=(maps, maps) + (P(),) * 10,
        check_vma=False,
    )
```

time: 1960 us -> 492 us (0.25)
  matrix products: 814 us -> 0 us
  blocking collectives: 565 us -> 53 us
  waiting for transfers between devices: 406 us -> 101 us
  Pallas kernels: 0 us -> 199 us
  other arithmetic: 60.8 us -> 1.45 us
  starting transfers between devices: 0.08 us -> 56.4 us
  local copies, waits for them, and re-layouts: 88 us -> 62.6 us
    conv_general_dilated x6 -> x0, matrix products: 760 us -> none  [the longest x4 390 us: depthwise(): lax.conv_general_dilated(values, kernel[:, :, None, :], (1, 1), 'SAME', d...]
    psum x14 -> x0, blocking collectives: 565 us -> none  [the longest x7 283 us: norm_forward(): lax.psum((pixel_count, column_sum, square), ('node', 'dev'))]
    unnamed x4 -> x1, waiting for transfers between devices: 406 us -> 0.02 us
    pallas_call x0 -> x32, Pallas kernels: none -> 199 us  [the longest x16 150 us: call(): pl.pallas_call(body, grid=(crops,), in_specs=specs, out_specs=[spec(shape...]
    dot_general x12 -> x0, matrix products: 54.8 us -> none  [the longest x4 24 us: transposed(): lax.dot_general(flattened, weight, (((1,), (1,)), ((), ())), preferred_el...]
    all_to_all x0 -> x4, blocking collectives: none -> 53 us  [the longest x3 42.1 us: exchange(): return lax.all_to_all(sent, AXES, 0, 0, tiled=True)]
    ppermute x0 -> x32, starting transfers between devices: none -> 36.9 us  [the longest x26 34.7 us: across(): lax.ppermute(part, axis, [(at, at ^ k) for at in range(size)])]
    psum x0 -> x1, waiting for transfers between devices: none -> 34.1 us  [local(): grad_down, grad_up = lax.psum((grad_down, grad_up), AXES)]
  transfers between devices with their start and end apart: 2 -> 40, of which waited for: 2 -> 21; matrix products, arithmetic and copies ran while one was open for 1% -> 5% of each run, Pallas kernels for 0% -> 15%
where the time goes in v2:
time: 492 us; the launch traced here: 489 us
  Pallas kernels  199 us (40%)
  waiting for transfers between devices  101 us (21%)
  local copies, waits for them, and re-layouts  62.6 us (13%)
  starting transfers between devices  56.4 us (11%)
  blocking collectives  53 us (11%)
  between operations  14.4 us (3%)
    pallas_call x16, Pallas kernels, call(): pl.pallas_call(body, grid=(crops,), in_specs=specs, out_specs=[spec(shape...  150 us
    all_to_all x3, blocking collectives, exchange(): return lax.all_to_all(sent, AXES, 0, 0, tiled=True)  42.1 us
    unnamed x97, local copies, waits for them, and re-layouts  41.9 us
    ppermute x26, starting transfers between devices, across(): lax.ppermute(part, axis, [(at, at ^ k) for at in range(size)])  34.7 us
    psum x1, waiting for transfers between devices, local(): grad_down, grad_up = lax.psum((grad_down, grad_up), AXES)  34.1 us
    all_to_all x6, waiting for transfers between devices, exchange(): return lax.all_to_all(sent, AXES, 0, 0, tiled=True)  29.9 us
    ppermute x26, waiting for transfers between devices, across(): lax.ppermute(part, axis, [(at, at ^ k) for at in range(size)])  29.9 us
    pallas_call x4, Pallas kernels, weight_grad(): pl.pallas_call(weight_grad_stage, grid_spec=pltpu.PrefetchScalarGridSpec(...  17.9 us
  transfers between devices with their start and end apart: 40, of which 21 were waited for; matrix products, arithmetic and copies ran while one was open for 5% of the time, Pallas kernels for 15%

profile of v2, /device:TPU:0, one launch (start us, length us, event | category | flops | bytes accessed | tf_op | source)
XLA Modules:
  0.0 488.7 jit_solution(345725254667506263)
XLA Ops:
  10.7 4.2 enter_stage.1
  16.0 15.5 %all_to_all.114 = f32[32,1,1152]{2,1,0:T(1,128)S(1)} all-to-all(f32[32,1,1152]{2,1,0:T(1,128)S(1)} %copy.81), channel_id=1, replica_groups=mesh['node'=4,'chip'=4,'core'=2] {'node','chip','core'}, dimensions={0} | all-to-all | bytes 294912 | tf_op jit(solution)/shard_map/all_to_all | solution.py:922
  32.2 4.9 %first_stage.1 = (bf16[896,512]{1,0:T(8,128)(2,1)}, f32[896,512]{1,0:T(8,128)}, f32[32,1024]{1,0:T(8,128)}, f32[8,512]{1,0:T(8,128)}) custom-call(s32[4]{0:T(128)} %refs_0_.27, f32[32,1152]{1,0:T(8,128)} %bitcast.64, f32[7,512]{1,0:T(8,128)} %refs_3_.12, f32[7,512]{1,0:T(8,128)} %refs_4_.12, ...), custom_call_target="tpu_custom_call" | custom-call | bytes 4517904 | tf_op jit(solution)/shard_map/first_stage/pallas_call | solution.py:869
  41.4 5.6 %kernel_waves_stage.1 = (f32[736,512]{1,0:T(8,128)}, f32[736,512]{1,0:T(8,128)}) custom-call(bf16[31,31,512]{2,1,0:T(8,128)(2,1)} %refs_0_.16, bf16[5,5,512]{2,1,0:T(8,128)(2,1)} %refs_1_.2, bf16[736,992]{1,0:T(8,128)(2,1)} %constant.62.clone.refs_2_, bf16[736,992]{1,0:T(8,128)(2,1)} %constant.63.clone.refs_3_, bf16[736,80]{1,0:T(8,128)(2,1)} %constant.64.clone.refs_4_, ...), custom_call_target="tpu_custom_call" | custom-call | bytes 7180288 | tf_op jit(solution)/shard_map/kernel_waves_stage/pallas_call | solution.py:869
  46.9 2.6 all-to-all-done.1
  50.3 16.8 %mixer_stage.1 = (bf16[896,512]{1,0:T(8,128)(2,1)}, f32[896,512]{1,0:T(8,128)}, f32[896,512]{1,0:T(8,128)}, f32[32,2048]{1,0:T(8,128)}, f32[8,512]{1,0:T(8,128)}) custom-call(s32[4]{0:T(128)} %refs_0_.27, f32[32,1024]{1,0:T(8,128)} %bitcast.67, f32[8,512]{1,0:T(8,128)} %get-tuple-element.134.refs_2_, f32[7,512]{1,0:T(8,128)} %refs_3_.12, f32[7,512]{1,0:T(8,128)} %refs_4_.12, ...), custom_call_target="tpu_custom_call" | custom-call | bytes 11210768 | tf_op jit(solution)/shard_map/mixer_stage/pallas_call | solution.py:869
  68.3 13.6 %all_to_all.115 = f32[32,1,2048]{2,1,0:T(1,128)S(1)} all-to-all(f32[32,1,2048]{2,1,0:T(1,128)S(1)} %copy.83), channel_id=1, replica_groups=mesh['node'=4,'chip'=4,'core'=2] {'node','chip','core'}, dimensions={0} | all-to-all | bytes 524288 | tf_op jit(solution)/shard_map/all_to_all | solution.py:922
  82.6 6.6 %merge_stage.1 = (bf16[896,512]{1,0:T(8,128)(2,1)}, f32[896,512]{1,0:T(8,128)}, f32[32,2048]{1,0:T(8,128)}, f32[8,512]{1,0:T(8,128)}) custom-call(s32[4]{0:T(128)} %refs_0_.27, f32[32,2048]{1,0:T(8,128)} %bitcast.59, f32[8,512]{1,0:T(8,128)} %get-tuple-element.134.refs_2_, f32[7,512]{1,0:T(8,128)} %refs_3_.12, f32[7,512]{1,0:T(8,128)} %refs_4_.12, ...), custom_call_target="tpu_custom_call" | custom-call | bytes 9367568 | tf_op jit(solution)/shard_map/merge_stage/pallas_call | solution.py:869
  91.2 2.6 all-to-all-start.3
  93.8 10.6 %all-to-all-done.3 = f32[32,1,2048]{2,1,0:T(1,128)S(1)} async-done(((f32[32,1,2048]{2,1,0:T(1,128)}), f32[32,1,2048]{2,1,0:T(1,128)S(1)}, u32[]{:S(2)}, u32[]{:S(2)}) %all-to-all-start.3) | async-done | bytes 262176 | tf_op jit(solution)/shard_map/all_to_all | solution.py:922
  105.2 9.9 %widen_stage.1 = (bf16[896,512]{1,0:T(8,128)(2,1)}, f32[896,2048]{1,0:T(8,128)}, f32[2,2048]{1,0:T(2,128)}, f32[8,512]{1,0:T(8,128)}) custom-call(s32[4]{0:T(128)} %refs_0_.27, f32[32,2048]{1,0:T(8,128)} %bitcast.61, f32[8,512]{1,0:T(8,128)} %get-tuple-element.134.refs_2_, f32[7,512]{1,0:T(8,128)} %refs_3_.12, f32[7,512]{1,0:T(8,128)} %refs_4_.12, ...), custom_call_target="tpu_custom_call" | custom-call | bytes 13447184 | tf_op jit(solution)/shard_map/widen_stage/pallas_call | solution.py:869
  117.2 10.9 %all_to_all.116 = f32[16,1,2048]{2,1,0:T(1,128)S(1)} all-to-all(f32[16,1,2048]{2,1,0:T(1,128)S(1)} %broadcast_in_dim.14), channel_id=1, replica_groups=mesh['node'=4,'chip'=4,'core'=2] {'node','chip'}, dimensions={0} | all-to-all | bytes 262144 | tf_op jit(solution)/shard_map/all_to_all | solution.py:935
  130.1 10.3 %narrow_stage.1 = (bf16[896,2048]{1,0:T(8,128)(2,1)}, f32[896,512]{1,0:T(8,128)}, f32[32,2048]{1,0:T(8,128)}, f32[8,2048]{1,0:T(8,128)}) custom-call(s32[4]{0:T(128)} %refs_0_.27, f32[2,2048]{1,0:T(2,128)} %maximum_select_fusion.refs_1_, f32[8,512]{1,0:T(8,128)} %get-tuple-element.134.refs_2_, f32[1,2048]{1,0:T(1,128)} %bitcast.81, f32[1,2048]{1,0:T(1,128)} %bitcast.89, ...), custom_call_target="tpu_custom_call" | custom-call | bytes 16236560 | tf_op jit(solution)/shard_map/narrow_stage/pallas_call | solution.py:869
  144.9 3.9 copy.87
  148.9 6.7 %all-to-all-done.5 = f32[32,1,2048]{2,1,0:T(1,128)S(1)} async-done(((f32[32,1,2048]{2,1,0:T(1,128)}), f32[32,1,2048]{2,1,0:T(1,128)S(1)}, u32[]{:S(2)}, u32[]{:S(2)}) %all-to-all-start.5) | async-done | bytes 262176 | tf_op jit(solution)/shard_map/all_to_all | solution.py:922
  156.3 16.5 %wide_back_stage.1 = (bf16[896,512]{1,0:T(8,128)(2,1)}, f32[896,2048]{1,0:T(8,128)}, f32[2,2048]{1,0:T(2,128)}, f32[8,512]{1,0:T(8,128)}) custom-call(s32[4]{0:T(128)} %refs_0_.27, f32[32,2048]{1,0:T(8,128)} %bitcast.60, f32[8,512]{1,0:T(8,128)} %get-tuple-element.134.refs_2_, f32[8,2048]{1,0:T(8,128)} %get-tuple-element.148.refs_3_.refs_2_, ...), custom_call_target="tpu_custom_call" | custom-call | bytes 20852752 | tf_op jit(solution)/shard_map/wide_back_stage/pallas_call | solution.py:869
  175.6 3.7 all-to-all-start.6
  179.3 3.9 copy.89
  183.3 3.9 all-to-all-done.6
  187.3 6.3 %weight_grad_stage.4 = f32[2048,512]{1,0:T(8,128)} custom-call(s32[1]{0:T(128)} %constant.56.clone.1.place, bf16[896,2048]{1,0:T(8,128)(2,1)} %get-tuple-element.153.inputs, bf16[896,512]{1,0:T(8,128)(2,1)} %get-tuple-element.154.gradient), custom_call_target="tpu_custom_call" | custom-call | flops 1879048192 | bytes 8781824 | tf_op jit(solution)/shard_map/weight_grad_stage/pallas_call | solution.py:897
  194.3 11.9 %narrow_back_stage.1 = (bf16[896,2048]{1,0:T(8,128)(2,1)}, f32[896,512]{1,0:T(8,128)}, f32[32,1536]{1,0:T(8,128)}, f32[8,2048]{1,0:T(8,128)}) custom-call(s32[4]{0:T(128)} %refs_0_.27, f32[2,2048]{1,0:T(2,128)} %maximum_select_fusion.1.refs_1_, f32[8,2048]{1,0:T(8,128)} %get-tuple-element.148.refs_3_.refs_2_, f32[1,2048]{1,0:T(1,128)} %bitcast.82, ...), custom_call_target="tpu_custom_call" | custom-call | bytes 25387024 | tf_op jit(solution)/shard_map/narrow_back_stage/pallas_call | solution.py:869
  211.7 6.3 %weight_grad_stage.5 = f32[512,2048]{1,0:T(8,128)} custom-call(s32[1]{0:T(128)} %constant.56.clone.1.place, bf16[896,512]{1,0:T(8,128)(2,1)} %get-tuple-element.158.inputs, bf16[896,2048]{1,0:T(8,128)(2,1)} %get-tuple-element.159.gradient), custom_call_target="tpu_custom_call" | custom-call | flops 1879048192 | bytes 8781824 | tf_op jit(solution)/shard_map/weight_grad_stage/pallas_call | solution.py:897
  220.2 8.8 %mid_back_stage.1 = (f32[896,512]{1,0:T(8,128)}, bf16[896,512]{1,0:T(8,128)(2,1)}, f32[896,512]{1,0:T(8,128)}, f32[32,1536]{1,0:T(8,128)}, f32[8,512]{1,0:T(8,128)}) custom-call(s32[4]{0:T(128)} %refs_0_.27, f32[32,1536]{1,0:T(8,128)} %bitcast.63, f32[8,512]{1,0:T(8,128)} %get-tuple-element.134.refs_2_, f32[8,512]{1,0:T(8,128)} %get-tuple-element.161.refs_3_, ...), custom_call_target="tpu_custom_call" | custom-call | bytes 14790672 | tf_op jit(solution)/shard_map/mid_back_stage/pallas_call | solution.py:869
  230.1 13.0 %all_to_all.117 = f32[32,1,1536]{2,1,0:T(1,128)S(1)} all-to-all(f32[32,1,1536]{2,1,0:T(1,128)S(1)} %copy.92), channel_id=1, replica_groups=mesh['node'=4,'chip'=4,'core'=2] {'node','chip','core'}, dimensions={0} | all-to-all | bytes 393216 | tf_op jit(solution)/shard_map/all_to_all | solution.py:922
  243.8 16.6 %mixer_back_stage.1 = (bf16[896,512]{1,0:T(8,128)(2,1)}, bf16[896,512]{1,0:T(8,128)(2,1)}, f32[896,512]{1,0:T(8,128)}, f32[32,1024]{1,0:T(8,128)}, f32[8,512]{1,0:T(8,128)}) custom-call(s32[4]{0:T(128)} %refs_0_.27, f32[32,1536]{1,0:T(8,128)} %bitcast.62, f32[8,512]{1,0:T(8,128)} %get-tuple-element.134.refs_2_, f32[8,512]{1,0:T(8,128)} %get-tuple-element.161.refs_3_, ...), custom_call_target="tpu_custom_call" | custom-call | bytes 15765520 | tf_op jit(solution)/shard_map/mixer_back_stage/pallas_call | solution.py:869
  260.4 19.1 %kernel_grad_stage.1 = (f32[768,512]{1,0:T(8,128)}, f32[768,512]{1,0:T(8,128)}) custom-call(s32[1]{0:T(128)} %bitcast.13.refs_0_.place, bf16[896,512]{1,0:T(8,128)(2,1)} %get-tuple-element.167.refs_1_, bf16[896,512]{1,0:T(8,128)(2,1)} %get-tuple-element.168.refs_2_, bf16[896,512]{1,0:T(8,128)(2,1)} %get-tuple-element.169.refs_3_, ...), custom_call_target="tpu_custom_call" | custom-call | bytes 11054084 | tf_op jit(solution)/shard_map/kernel_grad_stage/pallas_call | solution.py:869
  281.2 2.7 all-to-all-start.9
  285.0 8.4 %all-to-all-done.9 = f32[32,1,1024]{2,1,0:T(1,128)S(1)} async-done(((f32[32,1,1024]{2,1,0:T(1,128)}), f32[32,1,1024]{2,1,0:T(1,128)S(1)}, u32[]{:S(2)}, u32[]{:S(2)}) %all-to-all-start.9) | async-done | bytes 131104 | tf_op jit(solution)/shard_map/all_to_all | solution.py:922
  295.2 3.8 sum_and_cut.6
  299.0 5.8 %first_back_stage.1 = (bf16[896,512]{1,0:T(8,128)(2,1)}, f32[896,512]{1,0:T(8,128)}, f32[32,1024]{1,0:T(8,128)}, f32[8,512]{1,0:T(8,128)}) custom-call(s32[4]{0:T(128)} %refs_0_.27, f32[32,1024]{1,0:T(8,128)} %bitcast.66, f32[8,512]{1,0:T(8,128)} %get-tuple-element.134.refs_2_, f32[8,512]{1,0:T(8,128)} %get-tuple-element.164.refs_4_.refs_3_, ...), custom_call_target="tpu_custom_call" | custom-call | bytes 8189968 | tf_op jit(solution)/shard_map/first_back_stage/pallas_call | solution.py:869
  304.8 2.7 weight_grad_stage.6
  315.7 2.8 all-to-all-start.10
  321.0 9.0 %collective-permute-done.7.refs_2_ = f32[192,512]{1,0:T(8,128)S(1)} collective-permute-done((f32[192,512]{1,0:T(8,128)}, f32[192,512]{1,0:T(8,128)S(1)}, u32[]{:S(2)}, u32[]{:S(2)}) %collective-permute-start.7) | collective-permute-done | bytes 393248 | tf_op jit(solution)/shard_map/ppermute | solution.py:1004
  330.9 3.1 sum_and_cut.7
  335.5 3.2 sum_and_cut.8
  340.1 3.3 collective-permute-start.14
  345.8 4.3 block_out_stage.1
  363.1 4.6 leave_stage.1
  378.7 2.9 collective-permute-start.17
  381.6 2.8 collective-permute-done.17.refs_3_
  386.5 5.8 %collective-permute-done.25.refs_2_ = f32[192,512]{1,0:T(8,128)S(1)} collective-permute-done((f32[192,512]{1,0:T(8,128)}, f32[192,512]{1,0:T(8,128)S(1)}, u32[]{:S(2)}, u32[]{:S(2)}) %collective-permute-start.25) | collective-permute-done | bytes 393248 | tf_op jit(solution)/shard_map/ppermute | solution.py:1004
  393.8 3.0 join.7.refs_0_
  413.4 3.8 join.9.refs_0_
  417.3 3.0 collective-permute-done.29.refs_3_
  428.1 3.7 copy.97
  433.8 3.9 kernel_grad_out_stage.1
  440.8 34.1 %all-reduce.3.cloned.1.call-done = (f32[512,2048]{1,0:T(8,128)}, f32[2048,512]{1,0:T(8,128)}) async-done(((f32[512,2048]{1,0:T(8,128)}, f32[2048,512]{1,0:T(8,128)}), (f32[512,2048]{1,0:T(8,128)}, f32[2048,512]{1,0:T(8,128)})) %all-reduce.3.cloned.1.call-update) | async-done | bytes 8388624 | tf_op jit(solution)/shard_map/psum | solution.py:1183
  474.9 4.8 copy.129
  (193 shorter events, 117.5 us)
Async XLA Ops:
  38.8 10.8 %all-to-all-start.1 = ((f32[32,1,1024]{2,1,0:T(1,128)}), f32[32,1,1024]{2,1,0:T(1,128)S(1)}, u32[]{:S(2)}, u32[]{:S(2)}) async-start(f32[32,1,1024]{2,1,0:T(1,128)} %copy.82), calls=%async_computation.1 | async-start | bytes 262144 | tf_op jit(solution)/shard_map/all_to_all | solution.py:922
  91.2 13.2 %all-to-all-start.3 = ((f32[32,1,2048]{2,1,0:T(1,128)}), f32[32,1,2048]{2,1,0:T(1,128)S(1)}, u32[]{:S(2)}, u32[]{:S(2)}) async-start(f32[32,1,2048]{2,1,0:T(1,128)} %copy.84), calls=%async_computation.3 | async-start | bytes 524288 | tf_op jit(solution)/shard_map/all_to_all | solution.py:922
  115.9 1.2 collective-permute-start
  128.2 1.2 collective-permute-start.1
  142.3 13.2 %all-to-all-start.5 = ((f32[32,1,2048]{2,1,0:T(1,128)}), f32[32,1,2048]{2,1,0:T(1,128)S(1)}, u32[]{:S(2)}, u32[]{:S(2)}) async-start(f32[32,1,2048]{2,1,0:T(1,128)} %copy.86), calls=%async_computation.5 | async-start | bytes 524288 | tf_op jit(solution)/shard_map/all_to_all | solution.py:922
  173.7 1.2 collective-permute-start.2
  175.6 11.5 %all-to-all-start.6 = ((f32[16,1,2048]{2,1,0:T(1,128)}), f32[16,1,2048]{2,1,0:T(1,128)S(1)}, u32[]{:S(2)}, u32[]{:S(2)}) async-start(f32[16,1,2048]{2,1,0:T(1,128)} %broadcast_in_dim.19), calls=%async_computation.6 | async-start | bytes 262144 | tf_op jit(solution)/shard_map/all_to_all | solution.py:935
  187.3 6.4 %collective-permute-start.3 = (f32[2048]{0:T(1024)S(1)}, f32[2048]{0:T(1024)S(1)}, u32[]{:S(2)}, u32[]{:S(2)}) collective-permute-start(f32[2048]{0:T(1024)S(1)} %reduce_sum.19), channel_id=1, source_target_pairs={{0,1},{1,0},{2,3},{3,2},{4,5},{5,4},{6,7},{7,6},{8,9},{9,8},{10,11... | collective-permute-start | bytes 24584 | tf_op jit(solution)/shard_map/ppermute | solution.py:936
  194.3 16.4 %copy-start.2 = (bf16[512,512]{1,0:T(8,128)(2,1)S(1)}, bf16[512,512]{1,0:T(8,128)(2,1)}, u32[]{:S(2)}) copy-start(bf16[512,512]{1,0:T(8,128)(2,1)} %refs_9_.3) | copy-start | bytes 1572868
  208.0 11.5 %all-to-all-start.7 = ((f32[32,1,1536]{2,1,0:T(1,128)}), f32[32,1,1536]{2,1,0:T(1,128)S(1)}, u32[]{:S(2)}, u32[]{:S(2)}) async-start(f32[32,1,1536]{2,1,0:T(1,128)} %copy.90), calls=%async_computation.7 | async-start | bytes 393216 | tf_op jit(solution)/shard_map/all_to_all | solution.py:922
  210.6 264.3 %all-reduce.3.cloned.1.call-start = ((), (), s32[]{:S(2)}) async-start(), calls=%async_computation.11 | async-start | bytes 16777216 | tf_op jit(solution)/shard_map/psum | solution.py:1183
  279.6 14.5 %collective-permute-start.4 = (f32[768,512]{1,0:T(8,128)}, f32[768,512]{1,0:T(8,128)S(1)}, u32[]{:S(2)}, u32[]{:S(2)}) collective-permute-start(f32[768,512]{1,0:T(8,128)} %get-tuple-element.173), channel_id=1, source_target_pairs={{0,1},{1,0},{2,3},{3,2},{4,5},{5,4},{6,7},{7,6},{8,9},{9,8},{10,11... | collective-permute-start | bytes 4718600 | tf_op jit(solution)/shard_map/ppermute | solution.py:1019
  281.2 12.1 %all-to-all-start.9 = ((f32[32,1,1024]{2,1,0:T(1,128)}), f32[32,1,1024]{2,1,0:T(1,128)S(1)}, u32[]{:S(2)}, u32[]{:S(2)}) async-start(f32[32,1,1024]{2,1,0:T(1,128)} %copy.93), calls=%async_computation.9 | async-start | bytes 262144 | tf_op jit(solution)/shard_map/all_to_all | solution.py:922
  304.8 10.1 %copy-start.18 = (f32[32,1024]{1,0:T(8,128)S(1)}, f32[32,1024]{1,0:T(8,128)}, u32[]{:S(2)}) copy-start(f32[32,1024]{1,0:T(8,128)} %get-tuple-element.195) | copy-start | bytes 393220
  307.5 27.1 %collective-permute-start.5 = (f32[256,512]{1,0:T(8,128)}, f32[256,512]{1,0:T(8,128)S(1)}, u32[]{:S(2)}, u32[]{:S(2)}) collective-permute-start(f32[256,512]{1,0:T(8,128)} %weight_grad_stage.6), channel_id=1, source_target_pairs={{0,1},{1,0},{2,3},{3,2},{4,5},{5,4},{6,7},{7,6},{8,9},{9,8},{10,11... | collective-permute-start | bytes 1572872 | tf_op jit(solution)/shard_map/ppermute | solution.py:1019
  308.8 12.2 %collective-permute-start.6 = (f32[192,512]{1,0:T(8,128)}, f32[192,512]{1,0:T(8,128)S(1)}, u32[]{:S(2)}, u32[]{:S(2)}) collective-permute-start(f32[192,512]{1,0:T(8,128)} %get-tuple-element.182), channel_id=1, source_target_pairs={{0,2},{2,0},{4,6},{6,4},{1,3},{3,1},{5,7},{7,5},{8,10},{10,8},{12,... | collective-permute-start | bytes 1179656 | tf_op jit(solution)/shard_map/ppermute | solution.py:1004
  308.9 21.1 %collective-permute-start.7 = (f32[192,512]{1,0:T(8,128)}, f32[192,512]{1,0:T(8,128)S(1)}, u32[]{:S(2)}, u32[]{:S(2)}) collective-permute-start(f32[192,512]{1,0:T(8,128)} %get-tuple-element.183), channel_id=1, source_target_pairs={{0,4},{2,6},{4,0},{6,2},{1,5},{3,7},{5,1},{7,3},{8,12},{10,14},{12... | collective-permute-start | bytes 1179656 | tf_op jit(solution)/shard_map/ppermute | solution.py:1004
  309.8 20.3 %collective-permute-start.8 = (f32[192,512]{1,0:T(8,128)}, f32[192,512]{1,0:T(8,128)S(1)}, u32[]{:S(2)}, u32[]{:S(2)}) collective-permute-start(f32[192,512]{1,0:T(8,128)} %get-tuple-element.184), channel_id=1, source_target_pairs={{0,6},{2,4},{4,2},{6,0},{1,7},{3,5},{5,3},{7,1},{8,14},{10,12},{12... | collective-permute-start | bytes 1179656 | tf_op jit(solution)/shard_map/ppermute | solution.py:1004
  315.7 43.0 %all-to-all-start.10 = ((f32[32,1,1024]{2,1,0:T(1,128)}), f32[32,1,1024]{2,1,0:T(1,128)S(1)}, u32[]{:S(2)}, u32[]{:S(2)}) async-start(f32[32,1,1024]{2,1,0:T(1,128)} %copy.95), calls=%async_computation.10 | async-start | bytes 262144 | tf_op jit(solution)/shard_map/all_to_all | solution.py:922
  334.1 11.1 %collective-permute-start.12 = (f32[48,512]{1,0:T(8,128)}, f32[48,512]{1,0:T(8,128)S(1)}, u32[]{:S(2)}, u32[]{:S(2)}) collective-permute-start(f32[48,512]{1,0:T(8,128)} %get-tuple-element.199), channel_id=1, source_target_pairs={{0,8},{8,0},{16,24},{24,16},{1,9},{9,1},{17,25},{25,17},{2,10},{10... | collective-permute-start | bytes 294920 | tf_op jit(solution)/shard_map/ppermute | solution.py:1004
  338.6 18.6 %collective-permute-start.10 = (f32[64,512]{1,0:T(8,128)}, f32[64,512]{1,0:T(8,128)S(1)}, u32[]{:S(2)}, u32[]{:S(2)}) collective-permute-start(f32[64,512]{1,0:T(8,128)} %get-tuple-element.197), channel_id=1, source_target_pairs={{0,4},{2,6},{4,0},{6,2},{1,5},{3,7},{5,1},{7,3},{8,12},{10,14},{12... | collective-permute-start | bytes 393224 | tf_op jit(solution)/shard_map/ppermute | solution.py:1004
  339.9 11.0 %collective-permute-start.13 = (f32[48,512]{1,0:T(8,128)}, f32[48,512]{1,0:T(8,128)S(1)}, u32[]{:S(2)}, u32[]{:S(2)}) collective-permute-start(f32[48,512]{1,0:T(8,128)} %get-tuple-element.200), channel_id=1, source_target_pairs={{0,16},{8,24},{16,0},{24,8},{1,17},{9,25},{17,1},{25,9},{2,18},{10... | collective-permute-start | bytes 294920 | tf_op jit(solution)/shard_map/ppermute | solution.py:1004
  340.1 10.8 %collective-permute-start.14 = (f32[48,512]{1,0:T(8,128)}, f32[48,512]{1,0:T(8,128)S(1)}, u32[]{:S(2)}, u32[]{:S(2)}) collective-permute-start(f32[48,512]{1,0:T(8,128)} %get-tuple-element.201), channel_id=1, source_target_pairs={{0,24},{8,16},{16,8},{24,0},{1,25},{9,17},{17,9},{25,1},{2,26},{10... | collective-permute-start | bytes 294920 | tf_op jit(solution)/shard_map/ppermute | solution.py:1004
  343.4 16.0 %collective-permute-start.11 = (f32[64,512]{1,0:T(8,128)}, f32[64,512]{1,0:T(8,128)S(1)}, u32[]{:S(2)}, u32[]{:S(2)}) collective-permute-start(f32[64,512]{1,0:T(8,128)} %get-tuple-element.198), channel_id=1, source_target_pairs={{0,6},{2,4},{4,2},{6,0},{1,7},{3,5},{5,3},{7,1},{8,14},{10,12},{12... | collective-permute-start | bytes 393224 | tf_op jit(solution)/shard_map/ppermute | solution.py:1004
  345.2 14.2 %collective-permute-start.9 = (f32[64,512]{1,0:T(8,128)}, f32[64,512]{1,0:T(8,128)S(1)}, u32[]{:S(2)}, u32[]{:S(2)}) collective-permute-start(f32[64,512]{1,0:T(8,128)} %get-tuple-element.196), channel_id=1, source_target_pairs={{0,2},{2,0},{4,6},{6,4},{1,3},{3,1},{5,7},{7,5},{8,10},{10,8},{12,... | collective-permute-start | bytes 393224 | tf_op jit(solution)/shard_map/ppermute | solution.py:1004
  353.9 13.8 %collective-permute-start.18 = (f32[48,512]{1,0:T(8,128)}, f32[48,512]{1,0:T(8,128)S(1)}, u32[]{:S(2)}, u32[]{:S(2)}) collective-permute-start(f32[48,512]{1,0:T(8,128)} %sum_and_cut.9.refs_0_), channel_id=1, source_target_pairs={{0,8},{8,0},{16,24},{24,16},{1,9},{9,1},{17,25},{25,17},{2,10},{10... | collective-permute-start | bytes 294920 | tf_op jit(solution)/shard_map/ppermute | solution.py:1004
  355.5 12.2 %collective-permute-start.19 = (f32[48,512]{1,0:T(8,128)}, f32[48,512]{1,0:T(8,128)S(1)}, u32[]{:S(2)}, u32[]{:S(2)}) collective-permute-start(f32[48,512]{1,0:T(8,128)} %sum_and_cut.9.refs_0_), channel_id=1, source_target_pairs={{0,16},{8,24},{16,0},{24,8},{1,17},{9,25},{17,1},{25,9},{2,18},{10... | collective-permute-start | bytes 294920 | tf_op jit(solution)/shard_map/ppermute | solution.py:1004
  357.2 10.6 %collective-permute-start.20 = (f32[48,512]{1,0:T(8,128)}, f32[48,512]{1,0:T(8,128)S(1)}, u32[]{:S(2)}, u32[]{:S(2)}) collective-permute-start(f32[48,512]{1,0:T(8,128)} %sum_and_cut.9.refs_0_), channel_id=1, source_target_pairs={{0,24},{8,16},{16,8},{24,0},{1,25},{9,17},{17,9},{25,1},{2,26},{10... | collective-permute-start | bytes 294920 | tf_op jit(solution)/shard_map/ppermute | solution.py:1004
  363.1 11.6 %copy-start.38 = (f32[16,512]{1,0:T(8,128)S(1)}, f32[16,512]{1,0:T(8,128)}, u32[]{:S(2)}) copy-start(f32[16,512]{1,0:T(8,128)} %get-tuple-element.215) | copy-start | bytes 98308
  363.1 13.3 %copy-start.37 = (f32[16,512]{1,0:T(8,128)S(1)}, f32[16,512]{1,0:T(8,128)}, u32[]{:S(2)}) copy-start(f32[16,512]{1,0:T(8,128)} %get-tuple-element.216) | copy-start | bytes 98308
  363.1 15.6 %copy-start.36 = (f32[16,512]{1,0:T(8,128)S(1)}, f32[16,512]{1,0:T(8,128)}, u32[]{:S(2)}) copy-start(f32[16,512]{1,0:T(8,128)} %get-tuple-element.217) | copy-start | bytes 98308
  370.8 15.7 %collective-permute-start.24 = (f32[192,512]{1,0:T(8,128)}, f32[192,512]{1,0:T(8,128)S(1)}, u32[]{:S(2)}, u32[]{:S(2)}) collective-permute-start(f32[192,512]{1,0:T(8,128)} %join.6.refs_0_), channel_id=1, source_target_pairs={{0,2},{2,0},{4,6},{6,4},{1,3},{3,1},{5,7},{7,5},{8,10},{10,8},{12,... | collective-permute-start | bytes 1179656 | tf_op jit(solution)/shard_map/ppermute | solution.py:1004
  371.9 20.4 %collective-permute-start.25 = (f32[192,512]{1,0:T(8,128)}, f32[192,512]{1,0:T(8,128)S(1)}, u32[]{:S(2)}, u32[]{:S(2)}) collective-permute-start(f32[192,512]{1,0:T(8,128)} %join.6.refs_0_), channel_id=1, source_target_pairs={{0,4},{2,6},{4,0},{6,2},{1,5},{3,7},{5,1},{7,3},{8,12},{10,14},{12... | collective-permute-start | bytes 1179656 | tf_op jit(solution)/shard_map/ppermute | solution.py:1004
  374.3 18.5 %collective-permute-start.26 = (f32[192,512]{1,0:T(8,128)}, f32[192,512]{1,0:T(8,128)S(1)}, u32[]{:S(2)}, u32[]{:S(2)}) collective-permute-start(f32[192,512]{1,0:T(8,128)} %join.6.refs_0_), channel_id=1, source_target_pairs={{0,6},{2,4},{4,2},{6,0},{1,7},{3,5},{5,3},{7,1},{8,14},{10,12},{12... | collective-permute-start | bytes 1179656 | tf_op jit(solution)/shard_map/ppermute | solution.py:1004
  374.7 4.0 collective-permute-start.15
  376.5 5.1 %collective-permute-start.16 = (f32[16,512]{1,0:T(8,128)S(1)}, f32[16,512]{1,0:T(8,128)S(1)}, u32[]{:S(2)}, u32[]{:S(2)}) collective-permute-start(f32[16,512]{1,0:T(8,128)S(1)} %copy-done.37), channel_id=1, source_target_pairs={{0,16},{8,24},{16,0},{24,8},{1,17},{9,25},{17,1},{25,9},{2,18},{10... | collective-permute-start | bytes 98312 | tf_op jit(solution)/shard_map/ppermute | solution.py:1004
  378.7 5.7 %collective-permute-start.17 = (f32[16,512]{1,0:T(8,128)S(1)}, f32[16,512]{1,0:T(8,128)S(1)}, u32[]{:S(2)}, u32[]{:S(2)}) collective-permute-start(f32[16,512]{1,0:T(8,128)S(1)} %copy-done.36), channel_id=1, source_target_pairs={{0,24},{8,16},{16,8},{24,0},{1,25},{9,17},{17,9},{25,1},{2,26},{10... | collective-permute-start | bytes 98312 | tf_op jit(solution)/shard_map/ppermute | solution.py:1004
  386.5 10.4 %copy-start.19 = (f32[16,512]{1,0:T(8,128)S(1)}, f32[16,512]{1,0:T(8,128)}, u32[]{:S(2)}) copy-start(f32[16,512]{1,0:T(8,128)} %sum_and_cut.11.refs_0_) | copy-start | bytes 98308
  396.9 16.5 %collective-permute-start.30 = (f32[768,512]{1,0:T(8,128)}, f32[768,512]{1,0:T(8,128)}, u32[]{:S(2)}, u32[]{:S(2)}) collective-permute-start(f32[768,512]{1,0:T(8,128)} %join.7.refs_0_), channel_id=1, source_target_pairs={{0,1},{1,0},{2,3},{3,2},{4,5},{5,4},{6,7},{7,6},{8,9},{9,8},{10,11... | collective-permute-start | bytes 4718600 | tf_op jit(solution)/shard_map/ppermute | solution.py:1004
  396.9 4.5 collective-permute-start.21
  398.6 5.0 %collective-permute-start.22 = (f32[16,512]{1,0:T(8,128)S(1)}, f32[16,512]{1,0:T(8,128)S(1)}, u32[]{:S(2)}, u32[]{:S(2)}) collective-permute-start(f32[16,512]{1,0:T(8,128)S(1)} %copy-done.19), channel_id=1, source_target_pairs={{0,16},{8,24},{16,0},{24,8},{1,17},{9,25},{17,1},{25,9},{2,18},{10... | collective-permute-start | bytes 98312 | tf_op jit(solution)/shard_map/ppermute | solution.py:1004
  400.0 5.7 %collective-permute-start.23 = (f32[16,512]{1,0:T(8,128)S(1)}, f32[16,512]{1,0:T(8,128)S(1)}, u32[]{:S(2)}, u32[]{:S(2)}) collective-permute-start(f32[16,512]{1,0:T(8,128)S(1)} %copy-done.19), channel_id=1, source_target_pairs={{0,24},{8,16},{16,8},{24,0},{1,25},{9,17},{17,9},{25,1},{2,26},{10... | collective-permute-start | bytes 98312 | tf_op jit(solution)/shard_map/ppermute | solution.py:1004
  408.4 8.9 %collective-permute-start.27 = (f32[64,512]{1,0:T(8,128)}, f32[64,512]{1,0:T(8,128)S(1)}, u32[]{:S(2)}, u32[]{:S(2)}) collective-permute-start(f32[64,512]{1,0:T(8,128)} %join.8.refs_0_), channel_id=1, source_target_pairs={{0,2},{2,0},{4,6},{6,4},{1,3},{3,1},{5,7},{7,5},{8,10},{10,8},{12,... | collective-permute-start | bytes 393224 | tf_op jit(solution)/shard_map/ppermute | solution.py:1004
  410.2 7.2 %collective-permute-start.28 = (f32[64,512]{1,0:T(8,128)}, f32[64,512]{1,0:T(8,128)S(1)}, u32[]{:S(2)}, u32[]{:S(2)}) collective-permute-start(f32[64,512]{1,0:T(8,128)} %join.8.refs_0_), channel_id=1, source_target_pairs={{0,4},{2,6},{4,0},{6,2},{1,5},{3,7},{5,1},{7,3},{8,12},{10,14},{12... | collective-permute-start | bytes 393224 | tf_op jit(solution)/shard_map/ppermute | solution.py:1004
  412.5 7.8 %collective-permute-start.29 = (f32[64,512]{1,0:T(8,128)}, f32[64,512]{1,0:T(8,128)S(1)}, u32[]{:S(2)}, u32[]{:S(2)}) collective-permute-start(f32[64,512]{1,0:T(8,128)} %join.8.refs_0_), channel_id=1, source_target_pairs={{0,6},{2,4},{4,2},{6,0},{1,7},{3,5},{5,3},{7,1},{8,14},{10,12},{12... | collective-permute-start | bytes 393224 | tf_op jit(solution)/shard_map/ppermute | solution.py:1004
  413.3 11.7 %copy-start.35 = (f32[8,512]{1,0:T(8,128)S(1)}, f32[8,512]{1,0:T(8,128)}, u32[]{:S(2)}) copy-start(f32[8,512]{1,0:T(8,128)} %get-tuple-element.248) | copy-start | bytes 49156
  413.3 13.2 %copy-start.1 = (bf16[4,14,14,512]{3,2,1,0:T(8,128)(2,1)S(1)}, bf16[4,14,14,512]{3,2,1,0:T(8,128)(2,1)}, u32[]{:S(2)}) copy-start(bf16[4,14,14,512]{3,2,1,0:T(8,128)(2,1)} %block_out_stage.1) | copy-start | bytes 2408452
  423.5 14.2 %collective-permute-start.31 = (f32[256,512]{1,0:T(8,128)}, f32[256,512]{1,0:T(8,128)S(1)}, u32[]{:S(2)}, u32[]{:S(2)}) collective-permute-start(f32[256,512]{1,0:T(8,128)} %join.10.refs_0_), channel_id=1, source_target_pairs={{0,1},{1,0},{2,3},{3,2},{4,5},{5,4},{6,7},{7,6},{8,9},{9,8},{10,11... | collective-permute-start | bytes 1572872 | tf_op jit(solution)/shard_map/ppermute | solution.py:1004
  (31 other events, 68.4 us)
Sparse Core Ops, SparseCore 0:
  280.4 194.5 all-reduce.2

commit v3 on v2

--- a/solution.py
+++ b/solution.py
@@ -57,9 +57,11 @@
         keep = keep & (np.arange(row) < side)[None, :]
         return table(offsets_h, offsets_w, keep.reshape(-1).astype(np.float64), 1.0)
 
-    def taps_back(side, row):
+    def taps_back(side):
         first, count = used_rows(side, canvas)
-        return taps(side, row)[:, first * row : (first + count) * row]
+        every = taps(side, side).reshape(2 * half, side, side)
+        used = every[:, first : first + count, first : first + count].reshape(2 * half, -1)
+        return np.pad(used, ((0, 0), (0, -used.shape[1] % 8)))
 
     def tap_row(side):
         return -(-side // 16) * 16
@@ -74,8 +76,8 @@
         back=split((cells * share).T),
         large=split(large),
         small=split(small),
-        large_back=split((taps_back(side_large, 32) * turn * share).T),
-        small_back=split((taps_back(side_small, 8) * turn * share).T),
+        large_back=split((taps_back(side_large) * turn * share).T),
+        small_back=split((taps_back(side_small) * turn * share).T),
     )
 
 
@@ -139,9 +141,20 @@
     return pl.program_id(0) == pl.num_programs(0) - 1
 
 
-def received(sent, width):
-    summed = jnp.sum(sent[...], axis=0, keepdims=True)
-    return [summed[:, at : at + width] for at in range(0, summed.shape[1], width)]
+def to_tiles(parts):
+    lines = [part[:, at : at + 128] for part in parts for at in range(0, part.shape[1], 128)]
+    lines += [jnp.zeros_like(lines[0])] * (-len(lines) % 8)
+    return jnp.concatenate(lines, axis=0)
+
+
+def from_tiles(tiles, count, width):
+    tiles = [tiles[at : at + 1] for at in range(count * width // 128)]
+    many = width // 128
+    return [jnp.concatenate(tiles[at * many : (at + 1) * many], axis=1) for at in range(count)]
+
+
+def received(sent, count, width):
+    return from_tiles(jnp.sum(sent[...], axis=0), count, width)
 
 
 def keep(coefs, values):
@@ -169,7 +182,7 @@
     def _():
         parts = [jnp.sum(sums[at], axis=0, keepdims=True) for at in range(sums.shape[0])]
         parts += list(extra)
-        out[...] = jnp.broadcast_to(jnp.concatenate(parts, axis=1), out.shape)
+        out[...] = jnp.broadcast_to(to_tiles(parts)[None], out.shape)
 
 
 def norm_coefs(column_sum, square, count, scaling, offsets):
@@ -210,7 +223,7 @@
         u_out[rows(at), :] = u.astype(BF16)
         return carry[0] + fold(x), carry[1] + fold(x * x)
 
-    add_sums(sums, lax.fori_loop(0, canvas, step, zeros(2, channels), unroll=7))
+    add_sums(sums, lax.fori_loop(0, canvas, step, zeros(2, channels), unroll=14))
     count = jnp.int32(0)
     for at in range(sides.shape[0]):
         count += sides[at] * sides[at]
@@ -224,8 +237,8 @@
 
     @pl.when(first_step())
     def _():
-        parts = received(came, 128)
         tiles = channels // 128
+        parts = received(came, 2 * tiles + 1, 128)
         column_sum = jnp.concatenate(parts[:tiles], axis=1)
         square = jnp.concatenate(parts[tiles : 2 * tiles], axis=1)
         count = jnp.concatenate([parts[2 * tiles]] * tiles, axis=1)
@@ -241,14 +254,14 @@
         low_out[rows(at), :] = (mask * (factor * x_in[rows(at), :].astype(F32) + constant)).astype(BF16)
         return carry
 
-    lax.fori_loop(0, canvas, step, 0, unroll=7)
+    lax.fori_loop(0, canvas, step, 0, unroll=14)
     pre_out[...] = dot(low_out[...], weight[...])
 
     def measure(at, carry):
         pre = pre_out[rows(at), :]
         return carry[0] + fold(pre), carry[1] + fold(pre * pre)
 
-    add_sums(sums, lax.fori_loop(0, canvas, measure, zeros(2, channels), unroll=7))
+    add_sums(sums, lax.fori_loop(0, canvas, measure, zeros(2, channels), unroll=14))
     publish(sums, sent)
 
 
@@ -261,6 +274,14 @@
     return real, imag, a * c - b * d, a * d + b * c
 
 
+def ahead_once(tables, values):
+    return dot(tables[0][...], values)
+
+
+def back_once(tables, values):
+    return dot(tables[0][...], values.astype(BF16))
+
+
 def ahead(tables, values):
     return dot(tables[0][...], values) + dot(tables[1][...], values)
 
@@ -271,7 +292,7 @@
 
 def mixer_stage(
     sides, came, seen, scale, offset, pre_in, ahead_t, back_t, large_w, small_w,
-    low_out, large_out, small_out, sent, noted, coefs, sums, spectrum, high, low,
+    low_out, large_out, small_out, waves_out, sent, noted, coefs, sums, spectrum, high, low,
 ):
     channels = pre_in.shape[1]
     canvas = pre_in.shape[0] // ROW
@@ -281,7 +302,7 @@
     @pl.when(first_step())
     def _():
         mean, reciprocal, factor, constant = norm_coefs(
-            *received(came, channels), seen[0:1], scale[1:2], offset[1:2]
+            *received(came, 2, channels), seen[0:1], scale[1:2], offset[1:2]
         )
         keep(coefs, [factor, constant])
         note(noted, [mean, reciprocal])
@@ -294,8 +315,9 @@
         low_out[rows(at), :] = gelu(mask * (factor * pre_in[rows(at), :] + constant)).astype(BF16)
         return carry
 
-    lax.fori_loop(0, canvas, step, 0, unroll=7)
+    lax.fori_loop(0, canvas, step, 0, unroll=14)
     spectrum[...] = ahead(ahead_t, low_out[...])
+    waves_out[...] = spectrum[...].astype(BF16)
     parts = ()
     for kernel, out in ((large_w, large_out), (small_w, small_out)):
 
@@ -313,7 +335,7 @@
             out[rows(at), :] = conv
             return carry[0] + fold(conv), carry[1] + fold(conv * conv)
 
-        parts += lax.fori_loop(0, canvas, measure, zeros(2, channels), unroll=7)
+        parts += lax.fori_loop(0, canvas, measure, zeros(2, channels), unroll=14)
     add_sums(sums, parts)
     publish(sums, sent)
 
@@ -328,7 +350,7 @@
 
     @pl.when(first_step())
     def _():
-        large_sum, large_square, small_sum, small_square = received(came, channels)
+        large_sum, large_square, small_sum, small_square = received(came, 4, channels)
         large = norm_coefs(large_sum, large_square, seen[0:1], scale[2:3], offset[2:3])
         small = norm_coefs(small_sum, small_square, seen[0:1], scale[3:4], offset[3:4])
         keep(coefs, [large[2], small[2], large[3] + small[3]])
@@ -343,7 +365,7 @@
         low_out[rows(at), :] = gelu(merged).astype(BF16)
         return carry
 
-    lax.fori_loop(0, canvas, step, 0, unroll=7)
+    lax.fori_loop(0, canvas, step, 0, unroll=14)
     proj_out[...] = dot(low_out[...], weight[...])
 
     def measure(at, carry):
@@ -352,12 +374,13 @@
         parts = (proj, proj * proj, proj * x, proj * u)
         return tuple(old + fold(part) for old, part in zip(carry, parts))
 
-    add_sums(sums, lax.fori_loop(0, canvas, measure, zeros(4, channels), unroll=2))
+    add_sums(sums, lax.fori_loop(0, canvas, measure, zeros(4, channels), unroll=7))
     publish(sums, sent)
 
 
 def widen_stage(
-    sides, came, seen, scale, offset, x_in, proj_in, weight, low_out, hidden_out, sent, noted, coefs, sums
+    sides, core, came, seen, scale, offset, x_in, proj_in, weight,
+    low_out, hidden_out, mine, other, noted, coefs, sums, found,
 ):
     channels = x_in.shape[1]
     canvas = x_in.shape[0] // ROW
@@ -365,7 +388,7 @@
 
     @pl.when(first_step())
     def _():
-        proj_sum, proj_square, cross, _ = parts = received(came, channels)
+        proj_sum, proj_square, cross, _ = parts = received(came, 4, channels)
         count, x_mean, x_sum, x_square = seen[0:1], seen[1:2], seen[3:4], seen[4:5]
         mean, reciprocal, factor, constant = norm_coefs(
             proj_sum, proj_square, count, scale[4:5], offset[4:5]
@@ -389,31 +412,43 @@
         low_out[rows(at), :] = (mask * (from_x * x + from_proj * proj_in[rows(at), :] + constant)).astype(BF16)
         return carry
 
-    lax.fori_loop(0, canvas, step, 0, unroll=7)
+    lax.fori_loop(0, canvas, step, 0, unroll=14)
     parts = [[], []]
     for at_block in range(hidden_out.shape[1] // channels):
         block = slice(at_block * channels, (at_block + 1) * channels)
-        hidden_out[:, block] = dot(low_out[...], weight[:, block])
+        found[...] = dot(low_out[...], weight[:, block])
 
         def measure(at, carry):
-            hidden = hidden_out[rows(at), block]
+            hidden = found[rows(at), :]
+            hidden_out[rows(at), block] = hidden.astype(BF16)
             return carry[0] + fold(hidden), carry[1] + fold(hidden * hidden)
 
-        found = lax.fori_loop(0, canvas, measure, zeros(2, channels), unroll=7)
-        parts[0].append(found[0])
-        parts[1].append(found[1])
+        pair = lax.fori_loop(0, canvas, measure, zeros(2, channels), unroll=14)
+        parts[0].append(pair[0])
+        parts[1].append(pair[1])
     add_sums(sums, [jnp.concatenate(part, axis=1) for part in parts])
-    hand_over(sums, sent)
-
-
-def hand_over(sums, out):
+    hand_over(sums, core, mine, other)
+
+
+def hand_over(sums, core, mine, other):
     @pl.when(last_step())
     def _():
-        out[...] = jnp.concatenate([jnp.sum(sums[at], axis=0, keepdims=True) for at in range(2)], axis=0)
+        first, second = (to_tiles([jnp.sum(sums[at], axis=0, keepdims=True)]) for at in range(2))
+        mine[...] = jnp.where(core[0] == 0, first, second)
+        other[...] = jnp.where(core[0] == 0, second, first)
+
+
+def taken_over(core, came):
+    mine, other = came[0][...], came[1][...]
+    wide = mine.size
+    first = jnp.where(core[0] == 0, mine, other)
+    second = jnp.where(core[0] == 0, other, mine)
+    return from_tiles(first, 1, wide)[0], from_tiles(second, 1, wide)[0]
 
 
 def narrow_stage(
-    sides, came, seen, wide_scale, wide_offset, hidden_in, u_in, weight, low_out, proj_out, sent, noted, coefs, sums
+    sides, core, came, seen, wide_scale, wide_offset, hidden_in, u_in, weight,
+    low_out, proj_out, sent, noted, coefs, sums,
 ):
     channels = u_in.shape[1]
     canvas = u_in.shape[0] // ROW
@@ -424,7 +459,7 @@
     def _():
         count = jnp.concatenate([seen[0:1]] * (wide // channels), axis=1)
         mean, reciprocal, factor, constant = norm_coefs(
-            came[0:1], came[1:2], count, wide_scale[...], wide_offset[...]
+            *taken_over(core, came), count, wide_scale[...], wide_offset[...]
         )
         keep(coefs, [factor, constant])
         note(noted, [mean, reciprocal, factor, constant, count])
@@ -434,10 +469,11 @@
         factor, constant = twice(coefs[0, :, block]), twice(coefs[1, :, block])
 
         def step(at, carry):
-            low_out[rows(at), block] = gelu(factor * hidden_in[rows(at), block] + constant).astype(BF16)
+            hidden = hidden_in[rows(at), block].astype(F32)
+            low_out[rows(at), block] = gelu(factor * hidden + constant).astype(BF16)
             return carry
 
-        lax.fori_loop(0, canvas, step, 0, unroll=7)
+        lax.fori_loop(0, canvas, step, 0, unroll=14)
     proj_out[...] = dot(low_out[...], weight[...])
     inside = columns_inside(side, channels)
 
@@ -448,13 +484,13 @@
         parts = (proj, proj * proj, proj * u, u)
         return tuple(old + fold(part) for old, part in zip(carry, parts))
 
-    add_sums(sums, lax.fori_loop(0, canvas, measure, zeros(4, channels), unroll=2))
+    add_sums(sums, lax.fori_loop(0, canvas, measure, zeros(4, channels), unroll=7))
     publish(sums, sent)
 
 
 def wide_back_stage(
-    sides, came, seen, wide_seen, scale, offset, proj_in, u_in, hidden_in, weight,
-    down_out, grad_out, sent, noted, coefs, sums,
+    sides, core, came, seen, wide_seen, scale, offset, proj_in, u_in, hidden_in, weight,
+    down_out, grad_out, mine, other, noted, coefs, sums, found,
 ):
     channels = u_in.shape[1]
     canvas = u_in.shape[0] // ROW
@@ -463,7 +499,7 @@
 
     @pl.when(first_step())
     def _():
-        proj_sum, proj_square, cross, u_sum = received(came, channels)
+        proj_sum, proj_square, cross, u_sum = received(came, 4, channels)
         count = seen[0:1]
         mean, reciprocal, factor, constant = norm_coefs(
             proj_sum, proj_square, count, scale[6:7], offset[6:7]
@@ -481,29 +517,29 @@
         down_out[rows(at), :] = (mask * (factor * u - constant - slope * proj_in[rows(at), :])).astype(BF16)
         return carry
 
-    lax.fori_loop(0, canvas, step, 0, unroll=7)
+    lax.fori_loop(0, canvas, step, 0, unroll=14)
     parts = [[], []]
     for at_block in range(wide // channels):
         block = slice(at_block * channels, (at_block + 1) * channels)
-        grad_out[:, block] = dot(down_out[...], weight[:, block])
+        found[...] = dot(down_out[...], weight[:, block])
         wide_factor = jnp.broadcast_to(wide_seen[2:3, block], (ROW, channels))
         wide_constant = jnp.broadcast_to(wide_seen[3:4, block], (ROW, channels))
 
         def measure(at, carry):
-            hidden = hidden_in[rows(at), block]
-            grad = grad_out[rows(at), block] * gelu_slope(wide_factor * hidden + wide_constant)
-            grad_out[rows(at), block] = grad
+            hidden = hidden_in[rows(at), block].astype(F32)
+            grad = found[rows(at), :] * gelu_slope(wide_factor * hidden + wide_constant)
+            grad_out[rows(at), block] = grad.astype(BF16)
             return carry[0] + fold(grad), carry[1] + fold(grad * hidden)
 
-        found = lax.fori_loop(0, canvas, measure, zeros(2, channels))
-        parts[0].append(found[0])
-        parts[1].append(found[1])
+        pair = lax.fori_loop(0, canvas, measure, zeros(2, channels), unroll=7)
+        parts[0].append(pair[0])
+        parts[1].append(pair[1])
     add_sums(sums, [jnp.concatenate(part, axis=1) for part in parts])
-    hand_over(sums, sent)
+    hand_over(sums, core, mine, other)
 
 
 def narrow_back_stage(
-    sides, came, wide_seen, wide_scale, grad_in, hidden_in, x_in, proj_in, weight,
+    sides, core, came, wide_seen, wide_scale, grad_in, hidden_in, x_in, proj_in, weight,
     up_out, ffn_out, sent, noted, coefs, sums,
 ):
     channels = x_in.shape[1]
@@ -514,8 +550,8 @@
     @pl.when(first_step())
     def _():
         mean, reciprocal, count = wide_seen[0:1], wide_seen[1:2], wide_seen[4:5]
-        shift_sum = came[0:1]
-        gain_sum = reciprocal * (came[1:2] - mean * shift_sum)
+        shift_sum, with_hidden = taken_over(core, came)
+        gain_sum = reciprocal * (with_hidden - mean * shift_sum)
         keep(coefs, back_coefs(shift_sum, gain_sum, count, mean, reciprocal, wide_scale[...]))
         note(noted, [gain_sum, shift_sum])
 
@@ -524,11 +560,12 @@
         factor, constant, slope = (twice(coefs[at, :, block]) for at in range(3))
 
         def step(at, carry):
-            grad = factor * grad_in[rows(at), block] - constant - slope * hidden_in[rows(at), block]
+            grad = factor * grad_in[rows(at), block].astype(F32) - constant
+            grad = grad - slope * hidden_in[rows(at), block].astype(F32)
             up_out[rows(at), block] = grad.astype(BF16)
             return carry
 
-        lax.fori_loop(0, canvas, step, 0, unroll=7)
+        lax.fori_loop(0, canvas, step, 0, unroll=14)
     ffn_out[...] = dot(up_out[...], weight[...])
     inside = columns_inside(side, channels)
 
@@ -538,7 +575,7 @@
         parts = (grad, grad * x_in[rows(at), :].astype(F32), grad * proj_in[rows(at), :])
         return tuple(old + fold(part) for old, part in zip(carry, parts))
 
-    add_sums(sums, lax.fori_loop(0, canvas, measure, zeros(3, channels), unroll=2))
+    add_sums(sums, lax.fori_loop(0, canvas, measure, zeros(3, channels), unroll=7))
     publish(sums, sent)
 
 
@@ -553,7 +590,7 @@
 
     @pl.when(first_step())
     def _():
-        ffn_sum, ffn_x, ffn_proj = received(came, channels)
+        ffn_sum, ffn_x, ffn_proj = received(came, 3, channels)
         count, u_sum = seen[0:1], last_seen[2:3]
         mean, reciprocal, mid_mean, mid_reciprocal = (mid_seen[at : at + 1] for at in range(4))
         proj_sum, proj_square, cross, proj_u = (mid_seen[at : at + 1] for at in range(4, 8))
@@ -583,7 +620,7 @@
         back_out[rows(at), :] = (mask * down).astype(BF16)
         return carry
 
-    lax.fori_loop(0, canvas, step, 0)
+    lax.fori_loop(0, canvas, step, 0, unroll=14)
     grad_out[...] = dot(back_out[...], weight[...])
     large = jnp.broadcast_to(merge_seen[4:5], (ROW, channels))
     small = jnp.broadcast_to(merge_seen[5:6], (ROW, channels))
@@ -596,14 +633,14 @@
         parts = (grad, grad * large_conv, grad * small_conv)
         return tuple(old + fold(part) for old, part in zip(carry, parts))
 
-    add_sums(sums, lax.fori_loop(0, canvas, measure, zeros(3, channels), unroll=2))
+    add_sums(sums, lax.fori_loop(0, canvas, measure, zeros(3, channels), unroll=7))
     publish(sums, sent)
 
 
 def mixer_back_stage(
-    sides, came, seen, merge_seen, first_seen, scale, offset, large_in, small_in, grad_in, pre_in,
+    sides, came, seen, merge_seen, first_seen, scale, offset, large_in, small_in, grad_in, pre_in, waves_in,
     ahead_t, back_t, large_w, small_w,
-    large_out, small_out, grad_out, sent, noted, coefs, sums, large_s, small_s, high, low,
+    grad_out, large_sum, small_sum, sent, noted, coefs, sums, large_out, small_out, large_s, small_s, summed,
 ):
     channels = pre_in.shape[1]
     canvas = pre_in.shape[0] // ROW
@@ -612,7 +649,7 @@
 
     @pl.when(first_step())
     def _():
-        shift_sum, with_large, with_small = received(came, channels)
+        shift_sum, with_large, with_small = received(came, 3, channels)
         count = seen[0:1]
         large_mean, large_r, small_mean, small_r = (merge_seen[at : at + 1] for at in range(4))
         large_gain = large_r * (with_large - large_mean * shift_sum)
@@ -637,19 +674,29 @@
         small_out[rows(at), :] = (mask * small).astype(BF16)
         return carry
 
-    lax.fori_loop(0, canvas, step, 0)
-    large_s[...] = ahead(ahead_t, large_out[...])
-    small_s[...] = ahead(ahead_t, small_out[...])
+    lax.fori_loop(0, canvas, step, 0, unroll=14)
+    large_s[...] = ahead_once(ahead_t, large_out[...])
+    small_s[...] = ahead_once(ahead_t, small_out[...])
 
     def product(at, carry):
         real, imag, one_real, one_imag = times(large_s, large_w, half, at, True)
         _, _, two_real, two_imag = times(small_s, small_w, half, at, True)
-        high[real, :], low[real, :] = halves(one_real + two_real)
-        high[imag, :], low[imag, :] = halves(one_imag + two_imag)
+        summed[real, :] = (one_real + two_real).astype(BF16)
+        summed[imag, :] = (one_imag + two_imag).astype(BF16)
+        a, b = waves_in[real, :].astype(F32), waves_in[imag, :].astype(F32)
+        for total, spectrum in ((large_sum, large_s), (small_sum, small_s)):
+            c, d = spectrum[real, :], spectrum[imag, :]
+            total[real, :] += a * c + b * d
+            total[imag, :] += b * c - a * d
         return carry
 
+    @pl.when(first_step())
+    def _():
+        large_sum[...] = jnp.zeros_like(large_sum)
+        small_sum[...] = jnp.zeros_like(small_sum)
+
     lax.fori_loop(0, half // 16, product, 0, unroll=4)
-    grad_out[...] = back(back_t, high[...], low[...])
+    grad_out[...] = back_once(back_t, summed[...])
     reciprocal = first_seen[1:2]
     factor = scale[1:2] * reciprocal
     constant = jnp.broadcast_to(offset[1:2] - first_seen[0:1] * factor, (ROW, channels))
@@ -662,7 +709,7 @@
         grad_out[rows(at), :] = grad
         return carry[0] + fold(grad), carry[1] + fold(grad * pre)
 
-    add_sums(sums, lax.fori_loop(0, canvas, measure, zeros(2, channels)))
+    add_sums(sums, lax.fori_loop(0, canvas, measure, zeros(2, channels), unroll=7))
     publish(sums, sent)
 
 
@@ -676,7 +723,7 @@
 
     @pl.when(first_step())
     def _():
-        shift_sum, with_pre = received(came, channels)
+        shift_sum, with_pre = received(came, 2, channels)
         mean, reciprocal = first_seen[0:1], first_seen[1:2]
         gain_sum = reciprocal * (with_pre - mean * shift_sum)
         keep(coefs, back_coefs(shift_sum, gain_sum, seen[0:1], mean, reciprocal, scale[1:2]))
@@ -691,14 +738,14 @@
         low_out[rows(at), :] = (mask * grad).astype(BF16)
         return carry
 
-    lax.fori_loop(0, canvas, step, 0, unroll=7)
+    lax.fori_loop(0, canvas, step, 0, unroll=14)
     grad_out[...] = dot(low_out[...], weight[...])
 
     def measure(at, carry):
         grad = grad_out[rows(at), :]
         return carry[0] + fold(grad), carry[1] + fold(grad * x_in[rows(at), :].astype(F32))
 
-    add_sums(sums, lax.fori_loop(0, canvas, measure, zeros(2, channels), unroll=7))
+    add_sums(sums, lax.fori_loop(0, canvas, measure, zeros(2, channels), unroll=14))
     publish(sums, sent)
 
 
@@ -709,7 +756,7 @@
 
     @pl.when(first_step())
     def _():
-        shift_sum, with_x = received(came, channels)
+        shift_sum, with_x = received(came, 2, channels)
         count, mean, reciprocal = (seen[at : at + 1] for at in range(3))
         gain_sum = reciprocal * (with_x - mean * shift_sum)
         keep(coefs, back_coefs(shift_sum, gain_sum, count, mean, reciprocal, scale[0:1]))
@@ -724,7 +771,7 @@
         image_out[0, at] = (mask * (resid_in[rows(at), :] + grad))[:canvas]
         return carry
 
-    lax.fori_loop(0, canvas, step, 0, unroll=7)
+    lax.fori_loop(0, canvas, step, 0, unroll=14)
 
 
 def block_out_stage(sides, mid_seen, last_seen, scale, offset, x_in, mid_in, last_in, out):
@@ -744,7 +791,7 @@
         out[0, at] = (x_in[rows(at), :].astype(F32) + mask * added)[:canvas].astype(BF16)
         return carry
 
-    lax.fori_loop(0, canvas, step, 0, unroll=7)
+    lax.fori_loop(0, canvas, step, 0, unroll=14)
 
 
 def kernel_waves_stage(large, small, large_t, small_t, large_out, small_out, large_rows, small_rows):
@@ -761,54 +808,20 @@
 
 
 def kernel_grad_stage(
-    place, mixer, large, small, merged, merged_grad, ahead_t, large_t, small_t, other_out, mine_out,
-    mixer_s, grad_s, large_sum, small_sum, flat, proj_sum,
+    place, merged, merged_grad, large_sum, small_sum, large_t, small_t, other_out, mine_out, flat, proj_sum
 ):
-    half = mixer_s.shape[0] // 2
-    at_crop = pl.program_id(0)
-    proj = dot_tn(merged[...], merged_grad[...])
-
-    @pl.when(at_crop == 0)
-    def _():
-        proj_sum[...] = proj
-
-    @pl.when(at_crop != 0)
-    def _():
-        proj_sum[...] += proj
-
-    mixer_s[...] = ahead(ahead_t, mixer[...])
-    for grad, total in ((large, large_sum), (small, small_sum)):
-        grad_s[...] = ahead(ahead_t, grad[...])
-
-        def product(at, carry):
-            real, imag, new_real, new_imag = times(mixer_s, grad_s, half, at, True)
-
-            @pl.when(at_crop == 0)
-            def _():
-                total[real, :] = new_real
-                total[imag, :] = new_imag
-
-            @pl.when(at_crop != 0)
-            def _():
-                total[real, :] += new_real
-                total[imag, :] += new_imag
-
-            return carry
-
-        lax.fori_loop(0, half // 16, product, 0, unroll=4)
-
-    @pl.when(last_step())
-    def _():
-        start = 0
-        for total, table in ((large_sum, large_t), (small_sum, small_t)):
-            size = table[0].shape[0]
-            flat[start : start + size, :] = back(table, *halves(total[...]))
-            start += size
+    proj_sum[...] = dot_tn(merged[...], merged_grad[...])
+    start = 0
+    for total, table in ((large_sum, large_t), (small_sum, small_t)):
+        size = table[0].shape[0]
+        flat[start : start + size, :] = back(table, *halves(total[...]))
+        start += size
+    if start < flat.shape[0]:
         flat[start:, :] = jnp.zeros((flat.shape[0] - start, flat.shape[1]), F32)
-        size, rest = flat.shape[0] // 2, proj_sum.shape[0] // 2
-        for out, core in ((mine_out, place[0]), (other_out, 1 - place[0])):
-            out[:size, :] = flat[pl.ds(pl.multiple_of(core * size, 8), size), :]
-            out[size:, :] = proj_sum[pl.ds(pl.multiple_of(core * rest, 8), rest), :]
+    size, rest = flat.shape[0] // 2, proj_sum.shape[0] // 2
+    for out, core in ((mine_out, place[0]), (other_out, 1 - place[0])):
+        out[:size, :] = flat[pl.ds(pl.multiple_of(core * size, 8), size), :]
+        out[size:, :] = proj_sum[pl.ds(pl.multiple_of(core * rest, 8), rest), :]
 
 
 def kernel_grad_out_stage(settled, large_out, small_out, proj_out, flat, *, canvas):
@@ -819,15 +832,14 @@
         flat[core * size : (core + 1) * size, :] = settled[start : start + size, :]
         proj_out[core * rest : (core + 1) * rest, :] = settled[start + size : start + size + rest, :]
     start = 0
-    for out, row in ((large_out, 32), (small_out, 8)):
+    for out in (large_out, small_out):
         side = out.shape[0]
         first, count = used_rows(side, canvas)
-        for at in range(side):
-            if first <= at < first + count:
-                out[at] = flat[start : start + side, :]
-                start += row
-            else:
-                out[at] = jnp.zeros(out.shape[1:], F32)
+        out[...] = jnp.zeros_like(out)
+        for at in range(first, first + count):
+            out[at, first : first + count, :] = flat[start : start + count, :]
+            start += count
+        start = -(-start // 8) * 8
 
 
 def weight_grad_stage(place, inputs, gradient, out):
@@ -841,7 +853,7 @@
     return pl.BlockSpec(shape, lambda at: (0,) * len(shape))
 
 
-VMEM = 62 * 1024 * 1024
+VMEM = 36 * 1024 * 1024
 
 
 def call(kernel, crops, ins, outs, scratch):
@@ -859,6 +871,8 @@
         group = value if isinstance(value, tuple) else (value,)
         places.append((len(flat), len(group) if isinstance(value, tuple) else 0))
         for part in group:
+            if kind == "rows":
+                part = pltpu.with_memory_space_constraint(part, pltpu.HBM)
             flat.append(part)
             specs.append(spec(part.shape, kind))
 
@@ -871,14 +885,16 @@
         grid=(crops,),
         in_specs=specs,
         out_specs=[spec(shape, kind) for shape, _, kind in outs],
-        out_shape=[jax.ShapeDtypeStruct(shape, dtype) for shape, dtype, _ in outs],
+        out_shape=[
+            (pltpu.HBM if kind == "rows" else jax.ShapeDtypeStruct)(shape, dtype) for shape, dtype, kind in outs
+        ],
         scratch_shapes=[pltpu.VMEM(shape, dtype) for shape, dtype in scratch],
         compiler_params=pltpu.CompilerParams(
             dimension_semantics=("arbitrary",), vmem_limit_bytes=VMEM
         ),
         cost_estimate=pl.CostEstimate(
             flops=0,
-            bytes_accessed=sum(part.size * part.dtype.itemsize for part in flat)
+            bytes_accessed=sum(math.prod(part.shape) * part.dtype.itemsize for part in flat)
             + sum(math.prod(shape) * jnp.dtype(dtype).itemsize for shape, dtype, _ in outs),
             transcendentals=0,
         ),
@@ -889,8 +905,11 @@
 def weight_grad(inputs, gradient, place=None):
     deep, high = inputs.shape
     wide = gradient.shape[1]
-    if place is None:
+    large = place is None
+    if large:
         place = jnp.zeros((1,), jnp.int32)
+        inputs = pltpu.with_memory_space_constraint(inputs, pltpu.HBM)
+        gradient = pltpu.with_memory_space_constraint(gradient, pltpu.HBM)
     else:
         high = high // 2
     block, across = min(high, 512), min(wide, 512)
@@ -905,7 +924,7 @@
             ],
             out_specs=pl.BlockSpec((block, across), lambda i, j, place: (i, j)),
         ),
-        out_shape=jax.ShapeDtypeStruct((high, wide), F32),
+        out_shape=pltpu.HBM((high, wide), F32) if large else jax.ShapeDtypeStruct((high, wide), F32),
         compiler_params=pltpu.CompilerParams(
             dimension_semantics=("arbitrary", "arbitrary"), vmem_limit_bytes=VMEM
         ),
@@ -925,16 +944,12 @@
 SWAP = [(0, 1), (1, 0)]
 
 
-def wide_exchange(sums):
-    core = lax.axis_index("core")
-    mine = lax.dynamic_index_in_dim(sums, core, 0, False)
-    other = lax.dynamic_index_in_dim(sums, 1 - core, 0, False)
+def wide_exchange(mine, other, *beside):
     mine = mine + lax.ppermute(other, "core", SWAP)
     chips = lax.axis_size(("node", "chip"))
     copies = jnp.broadcast_to(mine[None], (chips,) + mine.shape)
-    mine = jnp.sum(lax.all_to_all(copies, ("node", "chip"), 0, 0, tiled=True), axis=0)
-    other = lax.ppermute(mine, "core", SWAP)
-    return jnp.where(core == 0, jnp.stack([mine, other]), jnp.stack([other, mine]))
+    mine = jnp.sum(together(lax.all_to_all(copies, ("node", "chip"), 0, 0, tiled=True), *beside), axis=0)
+    return mine, lax.ppermute(mine, "core", SWAP)
 
 
 def sum_and_cut(arrays, place, ways):
@@ -1071,6 +1086,10 @@
     return Settle(other, mine, steps)
 
 
+def turned(token, *weights):
+    return [weight.T for weight in lax.optimization_barrier((weights, token))[0]]
+
+
 def together(value, *tokens):
     return lax.optimization_barrier((value, tokens))[0]
 
@@ -1094,11 +1113,13 @@
     scale, offset = (norm_gain, "whole"), (norm_shift, "whole")
     wide_scale, wide_offset = (wide_gain[None], "whole"), (wide_shift[None], "whole")
     full, full_low = ((cells, channels), F32, "rows"), ((cells, channels), BF16, "rows")
-    wide_full, wide_low = ((cells, wide), F32, "rows"), ((cells, wide), BF16, "rows")
+    wide_low = ((cells, wide), BF16, "rows")
+    wide_half = ((wide // 128, 128), F32, "whole")
+    core = (place_on("core"), "smem")
     seen_out, wide_seen_out = ((8, channels), F32, "whole"), ((8, wide), F32, "whole")
 
     def send(count):
-        return ((devices, count), F32, "whole")
+        return ((devices, -(-count // 1024) * 8, 128), F32, "whole")
 
     def coefs(count, width=channels):
         return ((count, 8, width), F32)
@@ -1130,6 +1151,7 @@
             ((tables["small"][0].shape[1], channels), BF16),
         ],
     )
+    came = together(came, large_w, small_w)
     pre_low, pre, sent, seen = run(
         first_stage,
         [sides, w(came), scale, offset, r(x), w(proj_in)],
@@ -1138,42 +1160,48 @@
     )
     spectrum = ((2 * half, channels), F32)
     spectrum_low = ((2 * half, channels), BF16)
-    mixer_low, large, small, sent, first_seen = run(
+    down_t, out_t = turned(sent, proj_down, proj_out)
+    came = together(exchange(sent), down_t, out_t)
+    mixer_low, large, small, mixer_waves, sent, first_seen = run(
         mixer_stage,
-        [sides, w(exchange(sent)), w(seen), scale, offset, r(pre), w(ahead_t), w(back_t), w(large_w), w(small_w)],
-        [full_low, full, full, send(4 * channels), seen_out],
+        [sides, w(came), w(seen), scale, offset, r(pre), w(ahead_t), w(back_t), w(large_w), w(small_w)],
+        [full_low, full, full, ((crops * 2 * half, channels), BF16, "rows"), send(4 * channels), seen_out],
         [coefs(2), coefs(4), spectrum, spectrum_low, spectrum_low],
     )
+    up_t, in_t = turned(sent, proj_up, proj_in)
+    came = together(exchange(sent), up_t, in_t)
     merged_low, proj, sent, merge_seen = run(
         merge_stage,
-        [sides, w(exchange(sent)), w(seen), scale, offset, r(large), r(small), r(x), r(u), w(proj_out)],
+        [sides, w(came), w(seen), scale, offset, r(large), r(small), r(x), r(u), w(proj_out)],
         [full_low, full, send(4 * channels), seen_out],
         [coefs(3), coefs(4)],
     )
-    ffn_low, hidden, sent, mid_seen = run(
+    ffn_low, hidden, mine, other, mid_seen = run(
         widen_stage,
-        [sides, w(exchange(sent)), w(seen), scale, offset, r(x), r(proj), w(proj_up)],
-        [full_low, wide_full, ((2, wide), F32, "whole"), seen_out],
-        [coefs(3), coefs(2, wide)],
+        [sides, core, w(exchange(sent)), w(seen), scale, offset, r(x), r(proj), w(proj_up)],
+        [full_low, wide_low, wide_half, wide_half, seen_out],
+        [coefs(3), coefs(2, wide), ((canvas * ROW, channels), F32)],
     )
     hidden_low, last, sent, wide_seen = run(
         narrow_stage,
-        [sides, w(wide_exchange(sent)), w(seen), wide_scale, wide_offset, r(hidden), r(u), w(proj_down)],
+        [sides, core, w(wide_exchange(mine, other)), w(seen), wide_scale, wide_offset, r(hidden), r(u), w(proj_down)],
         [wide_low, full, send(4 * channels), wide_seen_out],
         [coefs(2, wide), coefs(4)],
     )
-    down_low, hidden_grad, sent, last_seen = run(
+    down_low, hidden_grad, mine, other, last_seen = run(
         wide_back_stage,
-        [sides, w(exchange(sent)), w(seen), w(wide_seen), scale, offset, r(last), r(u), r(hidden), w(proj_down.T)],
-        [full_low, wide_full, ((2, wide), F32, "whole"), seen_out],
-        [coefs(3), coefs(2, wide)],
-    )
-    came = wide_exchange(sent)
+        [
+            sides, core, w(exchange(sent)), w(seen), w(wide_seen), scale, offset,
+            r(last), r(u), r(hidden), w(down_t),
+        ],
+        [full_low, wide_low, wide_half, wide_half, seen_out],
+        [coefs(3), coefs(2, wide), ((canvas * ROW, channels), F32)],
+    )
     grad_down = weight_grad(hidden_low, down_low)
-    came = together(came, grad_down)
+    came = wide_exchange(mine, other, grad_down)
     up_low, ffn_grad, sent, wide_noted = run(
         narrow_back_stage,
-        [sides, w(came), w(wide_seen), wide_scale, r(hidden_grad), r(hidden), r(x), r(proj), w(proj_up.T)],
+        [sides, core, w(came), w(wide_seen), wide_scale, r(hidden_grad), r(hidden), r(x), r(proj), w(up_t)],
         [wide_low, full, send(3 * channels), wide_seen_out],
         [coefs(3, wide), coefs(3)],
     )
@@ -1185,40 +1213,41 @@
         mid_back_stage,
         [
             sides, w(came), w(seen), w(merge_seen), w(mid_seen), w(last_seen), scale, offset,
-            r(x), r(u), r(proj), r(ffn_grad), r(large), r(small), w(proj_out.T),
+            r(x), r(u), r(proj), r(ffn_grad), r(large), r(small), w(out_t),
         ],
         [full, full_low, full, send(3 * channels), seen_out],
         [coefs(7), coefs(3)],
     )
     came = exchange(sent)
-    large_low, small_low, mixer_grad, sent, mixer_noted = run(
+    mixer_grad, large_sum, small_sum, sent, mixer_noted = run(
         mixer_back_stage,
         [
             sides, w(came), w(seen), w(merge_seen), w(first_seen), scale, offset,
-            r(large), r(small), r(merged_grad), r(pre), w(ahead_t), w(back_t), w(large_w), w(small_w),
+            r(large), r(small), r(merged_grad), r(pre), r(mixer_waves), w(ahead_t), w(back_t), w(large_w), w(small_w),
         ],
-        [full_low, full_low, full, send(2 * channels), seen_out],
-        [coefs(6), coefs(2), spectrum, spectrum, spectrum_low, spectrum_low],
+        [full, spectrum_out, spectrum_out, send(2 * channels), seen_out],
+        [
+            coefs(6), coefs(2), ((canvas * ROW, channels), BF16), ((canvas * ROW, channels), BF16),
+            spectrum, spectrum, spectrum_low,
+        ],
     )
     came = exchange(sent)
     taps_t = (const("large_back"), const("small_back"))
     tap_rows = sum(table[0].shape[0] for table in taps_t)
-    tap_rows = -(-tap_rows // (16 * devices)) * 16 * devices
+    tap_rows = -(-tap_rows // (8 * devices)) * 8 * devices
     half_taps = (((tap_rows + channels) // 2, channels), F32, "whole")
-    other, mine = run(
+    other, mine = call(
         kernel_grad_stage,
-        [
-            (place_on("core"), "smem"), r(mixer_low), r(large_low), r(small_low), r(merged_low), r(back_low),
-            w(ahead_t), w(taps_t[0]), w(taps_t[1]),
-        ],
+        1,
+        [core, w(merged_low), w(back_low), w(large_sum), w(small_sum), w(taps_t[0]), w(taps_t[1])],
         [half_taps, half_taps],
-        [spectrum, spectrum, spectrum, spectrum, ((tap_rows, channels), F32), ((channels, channels), F32)],
-    )
+        [((tap_rows, channels), F32), ((channels, channels), F32)],
+    )
+    came = together(came, other, mine)
     settle_taps = Settle(other, mine, BY_PERMUTES)
-    came = together(came, settle_taps.step(sent))
     pre_round, first_grad, sent, first_noted = run(
         first_back_stage,
-        [sides, w(came), w(seen), w(first_seen), scale, r(mixer_grad), r(pre), r(x), w(proj_in.T)],
+        [sides, w(came), w(seen), w(first_seen), scale, r(mixer_grad), r(pre), r(x), w(in_t)],
         [full_low, full, send(2 * channels), seen_out],
         [coefs(3), coefs(2)],
     )

time: 492 us -> 411 us (0.84)
  Pallas kernels: 199 us -> 128 us
  blocking collectives: 53 us -> 39 us
  local copies, waits for them, and re-layouts: 62.6 us -> 51.2 us
  waiting for transfers between devices: 101 us -> 110 us
  starting transfers between devices: 56.4 us -> 65.1 us
    pallas_call x16, Pallas kernels: 150 us -> 103 us  [call(): pl.pallas_call(body, grid=(crops,), in_specs=specs, out_specs=[spec(shape...]
    all_to_all x3 -> x2, blocking collectives: 42.1 us -> 28 us  [exchange(): return lax.all_to_all(sent, AXES, 0, 0, tiled=True)]
    pallas_call x6, Pallas kernels: 16 us -> 3.14 us  [join(): pl.pallas_call(body, grid_spec=pltpu.PrefetchScalarGridSpec(num_scalar_pr...]
    all_to_all x9 -> x0, local copies, waits for them, and re-layouts: 12.4 us -> none  [exchange(): return lax.all_to_all(sent, AXES, 0, 0, tiled=True)]
    all_to_all x6 -> x7, starting transfers between devices: 15.8 us -> 26.2 us  [exchange(): return lax.all_to_all(sent, AXES, 0, 0, tiled=True)]
    optimization_barrier x0 -> x4, local copies, waits for them, and re-layouts: none -> 9.19 us  [turned(): lax.optimization_barrier((weights, token))[0]]
    pallas_call x6, Pallas kernels: 15.6 us -> 7.8 us  [sum_and_cut(): pl.pallas_call(body, grid_spec=pltpu.PrefetchScalarGridSpec(num_scalar_pr...]
    all_to_all x6 -> x7, waiting for transfers between devices: 29.9 us -> 37.4 us  [exchange(): return lax.all_to_all(sent, AXES, 0, 0, tiled=True)]
  transfers between devices with their start and end apart: 40 -> 41, of which waited for: 21 -> 21; matrix products, arithmetic and copies ran while one was open for 5% -> 4% of each run, Pallas kernels for 15% -> 16%
where the time goes in v3:
time: 411 us; the launch traced here: 408 us
  Pallas kernels  128 us (31%)
  waiting for transfers between devices  110 us (27%)
  starting transfers between devices  65.1 us (16%)
  local copies, waits for them, and re-layouts  51.2 us (12%)
  blocking collectives  39 us (9%)
  between operations  14.9 us (4%)
    pallas_call x16, Pallas kernels, call(): pl.pallas_call(body, grid=(crops,), in_specs=specs, out_specs=[spec(shape...  103 us
    all_to_all x7, waiting for transfers between devices, exchange(): return lax.all_to_all(sent, AXES, 0, 0, tiled=True)  37.4 us
    unnamed x134, local copies, waits for them, and re-layouts  37.1 us
    ppermute x26, starting transfers between devices, across(): lax.ppermute(part, axis, [(at, at ^ k) for at in range(size)])  33.7 us
    ppermute x26, waiting for transfers between devices, across(): lax.ppermute(part, axis, [(at, at ^ k) for at in range(size)])  33.7 us
    psum x1, waiting for transfers between devices, local(): grad_down, grad_up = lax.psum((grad_down, grad_up), AXES)  33 us
    all_to_all x2, blocking collectives, exchange(): return lax.all_to_all(sent, AXES, 0, 0, tiled=True)  28 us
    all_to_all x7, starting transfers between devices, exchange(): return lax.all_to_all(sent, AXES, 0, 0, tiled=True)  26.2 us
  transfers between devices with their start and end apart: 41, of which 21 were waited for; matrix products, arithmetic and copies ran while one was open for 4% of the time, Pallas kernels for 16%

profile of v3, /device:TPU:0, one launch (start us, length us, event | category | flops | bytes accessed | tf_op | source)
XLA Modules:
  0.0 408.1 jit_solution(370672218085351900)
XLA Ops:
  8.9 2.8 enter_stage.1
  11.7 7.3 %all-to-all-start = ((f32[32,16,128]{2,1,0:T(8,128)}), f32[32,16,128]{2,1,0:T(8,128)S(1)}, u32[]{:S(2)}, u32[]{:S(2)}) async-start(f32[32,16,128]{2,1,0:T(8,128)} %get-tuple-element.140), calls=%async_computation | async-start | bytes 524288 | tf_op jit(solution)/shard_map/all_to_all | solution.py:941
  26.0 3.6 all-to-all-done.refs_1_
  29.6 4.4 %first_stage.1 = (bf16[896,512]{1,0:T(8,128)(2,1)}, f32[896,512]{1,0:T(8,128)}, f32[32,8,128]{2,1,0:T(8,128)}, f32[8,512]{1,0:T(8,128)S(1)}) custom-call(s32[4]{0:T(128)S(1)} %copy-done.41, f32[32,16,128]{2,1,0:T(8,128)S(1)} %all-to-all-done.refs_1_, f32[7,512]{1,0:T(8,128)S(1)} %copy-done.15, f32[7,512]{1,0:T(8,128)S(1)} %copy-done.29, ...), custom_call_target="tpu_custom_call" | custom-call | bytes 4632592 | tf_op jit(solution)/shard_map/first_stage/pallas_call | solution.py:883
  34.0 3.3 all-to-all-start.1
  37.3 3.0 copy.39
  40.6 4.9 %all-to-all-done.1.refs_1_ = f32[32,8,128]{2,1,0:T(8,128)} async-done(((f32[32,8,128]{2,1,0:T(8,128)}), f32[32,8,128]{2,1,0:T(8,128)}, u32[]{:S(2)}, u32[]{:S(2)}) %all-to-all-start.1) | async-done | bytes 131104 | tf_op jit(solution)/shard_map/all_to_all | solution.py:941
  52.6 14.6 %mixer_stage.1 = (bf16[896,512]{1,0:T(8,128)(2,1)}, f32[896,512]{1,0:T(8,128)}, f32[896,512]{1,0:T(8,128)}, bf16[2944,512]{1,0:T(8,128)(2,1)}, f32[32,16,128]{2,1,0:T(8,128)S(1)}, /*index=5*/f32[8,512]{1,0:T(8,128)S(1)}) custom-call(s32[4]{0:T(128)S(1)} %copy-done.42, f32[32,8,128]{2,1,0:T(8,128)} %all-to-all-done.1.refs_1_, ...), custom_call_target="tpu_custom_call" | custom-call | bytes 14225424 | tf_op jit(solution)/shard_map/mixer_stage/pallas_call | solution.py:883
  68.5 3.3 all-to-all-start.2
  71.8 3.9 copy.41
  77.8 4.6 %all-to-all-done.2.refs_1_ = f32[32,16,128]{2,1,0:T(8,128)} async-done(((f32[32,16,128]{2,1,0:T(8,128)}), f32[32,16,128]{2,1,0:T(8,128)}, u32[]{:S(2)}, u32[]{:S(2)}) %all-to-all-start.2) | async-done | bytes 262176 | tf_op jit(solution)/shard_map/all_to_all | solution.py:941
  83.8 5.9 %merge_stage.1 = (bf16[896,512]{1,0:T(8,128)(2,1)}, f32[896,512]{1,0:T(8,128)}, f32[32,16,128]{2,1,0:T(8,128)S(1)}, f32[8,512]{1,0:T(8,128)S(1)}) custom-call(s32[4]{0:T(128)S(1)} %copy-done.43, f32[32,16,128]{2,1,0:T(8,128)} %all-to-all-done.2.refs_1_, f32[8,512]{1,0:T(8,128)S(1)} %get-tuple-element.149.refs_2_.refs_3_.refs_4_, f32[7,512]{1,0:T(8,128)S(1)} %copy-done.15, ...), custom_call_target="tpu_custom_call" | custom-call | bytes 9367568 | tf_op jit(solution)/shard_map/merge_stage/pallas_call | solution.py:883
  91.0 2.6 all-to-all-start.3
  93.6 10.6 %all-to-all-done.3.refs_2_ = f32[32,16,128]{2,1,0:T(8,128)S(1)} async-done(((f32[32,16,128]{2,1,0:T(8,128)}), f32[32,16,128]{2,1,0:T(8,128)S(1)}, u32[]{:S(2)}, u32[]{:S(2)}) %all-to-all-start.3) | async-done | bytes 262176 | tf_op jit(solution)/shard_map/all_to_all | solution.py:941
  107.2 6.0 %widen_stage.1 = (bf16[896,512]{1,0:T(8,128)(2,1)}, bf16[896,2048]{1,0:T(8,128)(2,1)}, f32[16,128]{1,0:T(8,128)S(1)}, f32[16,128]{1,0:T(8,128)S(1)}, f32[8,512]{1,0:T(8,128)S(1)}) custom-call(s32[4]{0:T(128)S(1)} %copy-done.44, s32[1]{0:T(128)} %bitcast.refs_1_.refs_0_.place, f32[32,16,128]{2,1,0:T(8,128)S(1)} %all-to-all-done.3.refs_2_, ...), custom_call_target="tpu_custom_call" | custom-call | bytes 9777172 | tf_op jit(solution)/shard_map/widen_stage/pallas_call | solution.py:883
  114.4 10.9 %all_to_all.55 = f32[16,16,128]{2,1,0:T(8,128)S(1)} all-to-all(f32[16,16,128]{2,1,0:T(8,128)S(1)} %broadcast_in_dim.15), channel_id=1, replica_groups=mesh['node'=4,'chip'=4,'core'=2] {'node','chip'}, dimensions={0} | all-to-all | bytes 262144 | tf_op jit(solution)/shard_map/all_to_all | solution.py:951
  128.2 7.5 %narrow_stage.1 = (bf16[896,2048]{1,0:T(8,128)(2,1)}, f32[896,512]{1,0:T(8,128)}, f32[32,16,128]{2,1,0:T(8,128)S(1)}, f32[8,2048]{1,0:T(8,128)S(1)}) custom-call(s32[4]{0:T(128)S(1)} %copy-done.45, s32[1]{0:T(128)} %bitcast.refs_1_.refs_0_.place, f32[16,128]{1,0:T(8,128)S(1)} %reduce_sum.18.refs_2_, f32[16,128]{1,0:T(8,128)S(1)} %collective-permute-done.1.refs_3_, ...), custom_call_target="tpu_custom_call" | custom-call | bytes 12566548 | tf_op jit(solution)/shard_map/narrow_stage/pallas_call | solution.py:883
  135.7 12.5 %all_to_all.56.refs_2_ = f32[32,16,128]{2,1,0:T(8,128)S(1)} all-to-all(f32[32,16,128]{2,1,0:T(8,128)S(1)} %get-tuple-element.164), channel_id=1, replica_groups=mesh['node'=4,'chip'=4,'core'=2] {'node','chip','core'}, dimensions={0} | all-to-all | bytes 524288 | tf_op jit(solution)/shard_map/all_to_all | solution.py:941
  148.2 13.1 %wide_back_stage.1 = (bf16[896,512]{1,0:T(8,128)(2,1)}, bf16[896,2048]{1,0:T(8,128)(2,1)}, f32[16,128]{1,0:T(8,128)S(1)}, f32[16,128]{1,0:T(8,128)S(1)}, f32[8,512]{1,0:T(8,128)S(1)}) custom-call(s32[4]{0:T(128)S(1)} %copy-done.45, s32[1]{0:T(128)} %bitcast.refs_1_.refs_0_.place, f32[32,16,128]{2,1,0:T(8,128)S(1)} %all_to_all.56.refs_2_, ...), custom_call_target="tpu_custom_call" | custom-call | bytes 13512724 | tf_op jit(solution)/shard_map/wide_back_stage/pallas_call | solution.py:883
  163.2 3.7 all-to-all-start.6
  166.9 6.4 %weight_grad_stage.4 = f32[2048,512]{1,0:T(8,128)} custom-call(s32[1]{0:T(128)} %constant.39.clone.1.place, bf16[896,2048]{1,0:T(8,128)(2,1)} %get-tuple-element.171.inputs, bf16[896,512]{1,0:T(8,128)(2,1)} %get-tuple-element.172.gradient), custom_call_target="tpu_custom_call" | custom-call | flops 1879048192 | bytes 8781824 | tf_op jit(solution)/shard_map/weight_grad_stage/pallas_call | solution.py:916
  176.0 8.0 %narrow_back_stage.1 = (bf16[896,2048]{1,0:T(8,128)(2,1)}, f32[896,512]{1,0:T(8,128)}, f32[32,16,128]{2,1,0:T(8,128)}, f32[8,2048]{1,0:T(8,128)S(1)}) custom-call(s32[4]{0:T(128)S(1)} %copy-done.45, s32[1]{0:T(128)} %bitcast.refs_1_.refs_0_.place, f32[16,128]{1,0:T(8,128)S(1)} %reduce_sum.19.refs_2_, f32[16,128]{1,0:T(8,128)S(1)} %collective-permute-done.3.refs_3_, ...), custom_call_target="tpu_custom_call" | custom-call | bytes 18112532 | tf_op jit(solution)/shard_map/narrow_back_stage/pallas_call | solution.py:883
  184.0 4.3 %all-to-all-start.7 = ((f32[32,16,128]{2,1,0:T(8,128)}), f32[32,16,128]{2,1,0:T(8,128)S(1)}, u32[]{:S(2)}, u32[]{:S(2)}) async-start(f32[32,16,128]{2,1,0:T(8,128)} %get-tuple-element.175), calls=%async_computation.7 | async-start | bytes 524288 | tf_op jit(solution)/shard_map/all_to_all | solution.py:941
  188.4 6.3 %weight_grad_stage.5 = f32[512,2048]{1,0:T(8,128)} custom-call(s32[1]{0:T(128)} %constant.39.clone.1.place, bf16[896,512]{1,0:T(8,128)(2,1)} %get-tuple-element.176.inputs, bf16[896,2048]{1,0:T(8,128)(2,1)} %get-tuple-element.177.gradient), custom_call_target="tpu_custom_call" | custom-call | flops 1879048192 | bytes 8781824 | tf_op jit(solution)/shard_map/weight_grad_stage/pallas_call | solution.py:916
  194.7 4.2 %all-to-all-done.7.refs_1_ = f32[32,16,128]{2,1,0:T(8,128)S(1)} async-done(((f32[32,16,128]{2,1,0:T(8,128)}), f32[32,16,128]{2,1,0:T(8,128)S(1)}, u32[]{:S(2)}, u32[]{:S(2)}) %all-to-all-start.7) | async-done | bytes 262176 | tf_op jit(solution)/shard_map/all_to_all | solution.py:941
  199.1 8.4 %mid_back_stage.1 = (f32[896,512]{1,0:T(8,128)}, bf16[896,512]{1,0:T(8,128)(2,1)}, f32[896,512]{1,0:T(8,128)}, f32[32,16,128]{2,1,0:T(8,128)S(1)}, f32[8,512]{1,0:T(8,128)S(1)}) custom-call(s32[4]{0:T(128)S(1)} %copy-done.45, f32[32,16,128]{2,1,0:T(8,128)S(1)} %all-to-all-done.7.refs_1_, f32[8,512]{1,0:T(8,128)S(1)} %get-tuple-element.149.refs_2_.refs_3_.refs_4_, ...), custom_call_target="tpu_custom_call" | custom-call | bytes 14921744 | tf_op jit(solution)/shard_map/mid_back_stage/pallas_call | solution.py:883
  207.4 15.5 %all_to_all.57.refs_1_ = f32[32,16,128]{2,1,0:T(8,128)S(1)} all-to-all(f32[32,16,128]{2,1,0:T(8,128)S(1)} %get-tuple-element.181), channel_id=1, replica_groups=mesh['node'=4,'chip'=4,'core'=2] {'node','chip','core'}, dimensions={0} | all-to-all | bytes 524288 | tf_op jit(solution)/shard_map/all_to_all | solution.py:941
  223.1 12.6 %mixer_back_stage.1 = (f32[896,512]{1,0:T(8,128)}, f32[736,512]{1,0:T(8,128)S(1)}, f32[736,512]{1,0:T(8,128)S(1)}, f32[32,8,128]{2,1,0:T(8,128)}, f32[8,512]{1,0:T(8,128)S(1)}) custom-call(s32[4]{0:T(128)S(1)} %copy-done.45, f32[32,16,128]{2,1,0:T(8,128)S(1)} %all_to_all.57.refs_1_, f32[8,512]{1,0:T(8,128)S(1)} %get-tuple-element.149.refs_2_.refs_3_.refs_4_, ...), custom_call_target="tpu_custom_call" | custom-call | bytes 20025360 | tf_op jit(solution)/shard_map/mixer_back_stage/pallas_call | solution.py:883
  235.8 4.0 kernel_grad_stage.1
  244.8 9.5 %all-to-all-done.9.refs_1_ = f32[32,8,128]{2,1,0:T(8,128)S(1)} async-done(((f32[32,8,128]{2,1,0:T(8,128)}), f32[32,8,128]{2,1,0:T(8,128)S(1)}, u32[]{:S(2)}, u32[]{:S(2)}) %all-to-all-start.9) | async-done | bytes 131104 | tf_op jit(solution)/shard_map/all_to_all | solution.py:941
  254.2 5.1 %first_back_stage.1 = (bf16[896,512]{1,0:T(8,128)(2,1)}, f32[896,512]{1,0:T(8,128)}, f32[32,8,128]{2,1,0:T(8,128)}, f32[8,512]{1,0:T(8,128)S(1)}) custom-call(s32[4]{0:T(128)S(1)} %copy-done.45, f32[32,8,128]{2,1,0:T(8,128)S(1)} %all-to-all-done.9.refs_1_, f32[8,512]{1,0:T(8,128)S(1)} %get-tuple-element.149.refs_2_.refs_3_.refs_4_, f32[8,512]{1,0:T(8,128)S(1)} %copy-done.50, ...), custom_call_target="tpu_custom_call" | custom-call | bytes 8189968 | tf_op jit(solution)/shard_map/first_back_stage/pallas_call | solution.py:883
  263.5 3.0 sum_and_cut.6
  270.0 2.8 all-to-all-start.10
  277.8 10.3 %collective-permute-done.10.refs_2_ = f32[160,512]{1,0:T(8,128)S(1)} collective-permute-done((f32[160,512]{1,0:T(8,128)S(1)}, f32[160,512]{1,0:T(8,128)S(1)}, u32[]{:S(2)}, u32[]{:S(2)}) %collective-permute-start.10) | collective-permute-done | bytes 327712 | tf_op jit(solution)/shard_map/ppermute | solution.py:1019
  289.3 3.3 block_out_stage.1
  292.6 2.6 sum_and_cut.8
  295.7 3.9 collective-permute-start.17
  299.8 3.3 leave_stage.1
  304.5 2.7 collective-permute-start.22
  308.9 2.7 collective-permute-start.13
  311.6 3.6 collective-permute-done.12.refs_1_
  317.2 3.7 collective-permute-done.14.refs_3_
  331.9 3.3 collective-permute-done.20.refs_3_
  335.3 3.5 collective-permute-done.29.refs_3_
  342.7 2.8 collective-permute-done.24.refs_1_
  345.5 3.1 collective-permute-done.25.refs_2_
  361.4 33.0 %all-reduce.3.cloned.1.call-done = (f32[512,2048]{1,0:T(8,128)}, f32[2048,512]{1,0:T(8,128)}) async-done(((f32[512,2048]{1,0:T(8,128)}, f32[2048,512]{1,0:T(8,128)}), (f32[512,2048]{1,0:T(8,128)}, f32[2048,512]{1,0:T(8,128)})) %all-reduce.3.cloned.1.call-update) | async-done | bytes 8388624 | tf_op jit(solution)/shard_map/psum | solution.py:1211
  394.4 4.8 %copy.47 = f32[512,2048]{1,0:T(8,128)} copy(f32[512,2048]{1,0:T(8,128)} %get-tuple-element.302) | data formatting | bytes 8388608
  (222 shorter events, 87.8 us)
Async XLA Ops:
  11.7 17.9 %all-to-all-start = ((f32[32,16,128]{2,1,0:T(8,128)}), f32[32,16,128]{2,1,0:T(8,128)S(1)}, u32[]{:S(2)}, u32[]{:S(2)}) async-start(f32[32,16,128]{2,1,0:T(8,128)} %get-tuple-element.140), calls=%async_computation | async-start | bytes 524288 | tf_op jit(solution)/shard_map/all_to_all | solution.py:941
  34.0 11.5 %all-to-all-start.1 = ((f32[32,8,128]{2,1,0:T(8,128)}), f32[32,8,128]{2,1,0:T(8,128)}, u32[]{:S(2)}, u32[]{:S(2)}) async-start(f32[32,8,128]{2,1,0:T(8,128)} %get-tuple-element.145), calls=%async_computation.1 | async-start | bytes 262144 | tf_op jit(solution)/shard_map/all_to_all | solution.py:941
  68.5 13.9 %all-to-all-start.2 = ((f32[32,16,128]{2,1,0:T(8,128)}), f32[32,16,128]{2,1,0:T(8,128)}, u32[]{:S(2)}, u32[]{:S(2)}) async-start(f32[32,16,128]{2,1,0:T(8,128)} %copy-done.37), calls=%async_computation.2 | async-start | bytes 524288 | tf_op jit(solution)/shard_map/all_to_all | solution.py:941
  91.0 13.2 %all-to-all-start.3 = ((f32[32,16,128]{2,1,0:T(8,128)}), f32[32,16,128]{2,1,0:T(8,128)S(1)}, u32[]{:S(2)}, u32[]{:S(2)}) async-start(f32[32,16,128]{2,1,0:T(8,128)} %copy-done.38), calls=%async_computation.3 | async-start | bytes 524288 | tf_op jit(solution)/shard_map/all_to_all | solution.py:941
  113.2 85.8 %copy-start.46 = (f32[8,512]{1,0:T(8,128)}, f32[8,512]{1,0:T(8,128)S(1)}, u32[]{:S(2)}) copy-start(f32[8,512]{1,0:T(8,128)S(1)} %get-tuple-element.160.refs_4_.refs_1_) | copy-start | bytes 49156
  113.2 1.2 collective-permute-start
  125.3 1.2 collective-permute-start.1
  161.3 1.2 collective-permute-start.2
  163.2 11.5 %all-to-all-start.6 = ((f32[16,16,128]{2,1,0:T(8,128)}), f32[16,16,128]{2,1,0:T(8,128)S(1)}, u32[]{:S(2)}, u32[]{:S(2)}) async-start(f32[16,16,128]{2,1,0:T(8,128)} %broadcast_in_dim.19), calls=%async_computation.6 | async-start | bytes 262144 | tf_op jit(solution)/shard_map/all_to_all | solution.py:951
  174.7 1.2 collective-permute-start.3
  184.0 14.9 %all-to-all-start.7 = ((f32[32,16,128]{2,1,0:T(8,128)}), f32[32,16,128]{2,1,0:T(8,128)S(1)}, u32[]{:S(2)}, u32[]{:S(2)}) async-start(f32[32,16,128]{2,1,0:T(8,128)} %get-tuple-element.175), calls=%async_computation.7 | async-start | bytes 524288 | tf_op jit(solution)/shard_map/all_to_all | solution.py:941
  188.3 206.1 %all-reduce.3.cloned.1.call-start = ((), (), s32[]{:S(2)}) async-start(), calls=%async_computation.11 | async-start | bytes 16777216 | tf_op jit(solution)/shard_map/psum | solution.py:1211
  199.0 24.0 %copy-start.5 = (f32[736,512]{1,0:T(8,128)S(1)}, f32[736,512]{1,0:T(8,128)}, u32[]{:S(2)}) copy-start(f32[736,512]{1,0:T(8,128)} %copy-done.3) | copy-start | bytes 4521988
  199.0 24.0 %copy-start.8 = (f32[736,512]{1,0:T(8,128)S(1)}, f32[736,512]{1,0:T(8,128)}, u32[]{:S(2)}) copy-start(f32[736,512]{1,0:T(8,128)} %copy-done.6) | copy-start | bytes 4521988
  199.0 23.9 %copy-start.20 = (bf16[736,224]{1,0:T(8,128)(2,1)S(1)}, bf16[736,224]{1,0:T(8,128)(2,1)}, u32[]{:S(2)}) copy-start(bf16[736,224]{1,0:T(8,128)(2,1)} %constant.42.clone.refs_7_.refs_13_) | copy-start | bytes 989188
  199.0 23.9 %copy-start.22 = (bf16[224,736]{1,0:T(8,128)(2,1)S(1)}, bf16[224,736]{1,0:T(8,128)(2,1)}, u32[]{:S(2)}) copy-start(bf16[224,736]{1,0:T(8,128)(2,1)} %constant.43.clone.refs_8_.refs_14_) | copy-start | bytes 989188
  199.0 23.9 %copy-start.24 = (bf16[224,736]{1,0:T(8,128)(2,1)S(1)}, bf16[224,736]{1,0:T(8,128)(2,1)}, u32[]{:S(2)}) copy-start(bf16[224,736]{1,0:T(8,128)(2,1)} %constant.44.clone.refs_9_.refs_15_) | copy-start | bytes 989188
  240.9 21.2 %collective-permute-start.5 = (f32[640,512]{1,0:T(8,128)}, f32[640,512]{1,0:T(8,128)}, u32[]{:S(2)}, u32[]{:S(2)}) collective-permute-start(f32[640,512]{1,0:T(8,128)} %get-tuple-element.190), channel_id=1, source_target_pairs={{0,1},{1,0},{2,3},{3,2},{4,5},{5,4},{6,7},{7,6},{8,9},{9,8},{10,11... | collective-permute-start | bytes 3932168 | tf_op jit(solution)/shard_map/ppermute | solution.py:1034
  242.2 12.1 %all-to-all-start.9 = ((f32[32,8,128]{2,1,0:T(8,128)}), f32[32,8,128]{2,1,0:T(8,128)S(1)}, u32[]{:S(2)}, u32[]{:S(2)}) async-start(f32[32,8,128]{2,1,0:T(8,128)} %get-tuple-element.185), calls=%async_computation.9 | async-start | bytes 262144 | tf_op jit(solution)/shard_map/all_to_all | solution.py:941
  261.0 11.8 %collective-permute-start.4 = (f32[256,512]{1,0:T(8,128)S(1)}, f32[256,512]{1,0:T(8,128)}, u32[]{:S(2)}, u32[]{:S(2)}) collective-permute-start(f32[256,512]{1,0:T(8,128)S(1)} %weight_grad_stage.6), channel_id=1, source_target_pairs={{0,1},{1,0},{2,3},{3,2},{4,5},{5,4},{6,7},{7,6},{8,9},{9,8},{10,11... | collective-permute-start | bytes 1572872 | tf_op jit(solution)/shard_map/ppermute | solution.py:1034
  263.5 25.9 %copy-start.47 = (f32[8,512]{1,0:T(8,128)S(1)}, f32[8,512]{1,0:T(8,128)}, u32[]{:S(2)}) copy-start(f32[8,512]{1,0:T(8,128)} %copy-done.46) | copy-start | bytes 49156
  266.5 21.6 %collective-permute-start.10 = (f32[160,512]{1,0:T(8,128)S(1)}, f32[160,512]{1,0:T(8,128)S(1)}, u32[]{:S(2)}, u32[]{:S(2)}) collective-permute-start(f32[160,512]{1,0:T(8,128)S(1)} %get-tuple-element.210), channel_id=1, source_target_pairs={{0,4},{2,6},{4,0},{6,2},{1,5},{3,7},{5,1},{7,3},{8,12},{10,14},{12... | collective-permute-start | bytes 983048 | tf_op jit(solution)/shard_map/ppermute | solution.py:1019
  267.4 25.2 %collective-permute-start.11 = (f32[160,512]{1,0:T(8,128)}, f32[160,512]{1,0:T(8,128)S(1)}, u32[]{:S(2)}, u32[]{:S(2)}) collective-permute-start(f32[160,512]{1,0:T(8,128)} %get-tuple-element.211), channel_id=1, source_target_pairs={{0,6},{2,4},{4,2},{6,0},{1,7},{3,5},{5,3},{7,1},{8,14},{10,12},{12... | collective-permute-start | bytes 983048 | tf_op jit(solution)/shard_map/ppermute | solution.py:1019
  268.4 24.2 %collective-permute-start.9 = (f32[160,512]{1,0:T(8,128)}, f32[160,512]{1,0:T(8,128)}, u32[]{:S(2)}, u32[]{:S(2)}) collective-permute-start(f32[160,512]{1,0:T(8,128)} %get-tuple-element.209), channel_id=1, source_target_pairs={{0,2},{2,0},{4,6},{6,4},{1,3},{3,1},{5,7},{7,5},{8,10},{10,8},{12,... | collective-permute-start | bytes 983048 | tf_op jit(solution)/shard_map/ppermute | solution.py:1019
  270.0 29.8 %all-to-all-start.10 = ((f32[32,8,128]{2,1,0:T(8,128)}), f32[32,8,128]{2,1,0:T(8,128)S(1)}, u32[]{:S(2)}, u32[]{:S(2)}) async-start(f32[32,8,128]{2,1,0:T(8,128)} %get-tuple-element.205), calls=%async_computation.10 | async-start | bytes 262144 | tf_op jit(solution)/shard_map/all_to_all | solution.py:941
  274.8 20.9 %collective-permute-start.6 = (f32[64,512]{1,0:T(8,128)S(1)}, f32[64,512]{1,0:T(8,128)S(1)}, u32[]{:S(2)}, u32[]{:S(2)}) collective-permute-start(f32[64,512]{1,0:T(8,128)S(1)} %get-tuple-element.206), channel_id=1, source_target_pairs={{0,2},{2,0},{4,6},{6,4},{1,3},{3,1},{5,7},{7,5},{8,10},{10,8},{12,... | collective-permute-start | bytes 393224 | tf_op jit(solution)/shard_map/ppermute | solution.py:1019
  276.3 23.3 %collective-permute-start.7 = (f32[64,512]{1,0:T(8,128)S(1)}, f32[64,512]{1,0:T(8,128)S(1)}, u32[]{:S(2)}, u32[]{:S(2)}) collective-permute-start(f32[64,512]{1,0:T(8,128)S(1)} %get-tuple-element.207), channel_id=1, source_target_pairs={{0,4},{2,6},{4,0},{6,2},{1,5},{3,7},{5,1},{7,3},{8,12},{10,14},{12... | collective-permute-start | bytes 393224 | tf_op jit(solution)/shard_map/ppermute | solution.py:1019
  288.1 11.5 %collective-permute-start.8 = (f32[64,512]{1,0:T(8,128)S(1)}, f32[64,512]{1,0:T(8,128)S(1)}, u32[]{:S(2)}, u32[]{:S(2)}) collective-permute-start(f32[64,512]{1,0:T(8,128)S(1)} %get-tuple-element.208), channel_id=1, source_target_pairs={{0,6},{2,4},{4,2},{6,0},{1,7},{3,5},{5,3},{7,1},{8,14},{10,12},{12... | collective-permute-start | bytes 393224 | tf_op jit(solution)/shard_map/ppermute | solution.py:1019
  295.2 7.8 %collective-permute-start.15 = (f32[40,512]{1,0:T(8,128)}, f32[40,512]{1,0:T(8,128)S(1)}, u32[]{:S(2)}, u32[]{:S(2)}) collective-permute-start(f32[40,512]{1,0:T(8,128)} %get-tuple-element.229), channel_id=1, source_target_pairs={{0,8},{8,0},{16,24},{24,16},{1,9},{9,1},{17,25},{25,17},{2,10},{10... | collective-permute-start | bytes 245768 | tf_op jit(solution)/shard_map/ppermute | solution.py:1019
  295.2 7.8 %collective-permute-start.16 = (f32[40,512]{1,0:T(8,128)}, f32[40,512]{1,0:T(8,128)S(1)}, u32[]{:S(2)}, u32[]{:S(2)}) collective-permute-start(f32[40,512]{1,0:T(8,128)} %get-tuple-element.230), channel_id=1, source_target_pairs={{0,16},{8,24},{16,0},{24,8},{1,17},{9,25},{17,1},{25,9},{2,18},{10... | collective-permute-start | bytes 245768 | tf_op jit(solution)/shard_map/ppermute | solution.py:1019
  295.7 8.7 %collective-permute-start.17 = (f32[40,512]{1,0:T(8,128)S(1)}, f32[40,512]{1,0:T(8,128)S(1)}, u32[]{:S(2)}, u32[]{:S(2)}) collective-permute-start(f32[40,512]{1,0:T(8,128)S(1)} %get-tuple-element.231), channel_id=1, source_target_pairs={{0,24},{8,16},{16,8},{24,0},{1,25},{9,17},{17,9},{25,1},{2,26},{10... | collective-permute-start | bytes 245768 | tf_op jit(solution)/shard_map/ppermute | solution.py:1019
  304.4 16.5 %collective-permute-start.21 = (f32[40,512]{1,0:T(8,128)S(1)}, f32[40,512]{1,0:T(8,128)S(1)}, u32[]{:S(2)}, u32[]{:S(2)}) collective-permute-start(f32[40,512]{1,0:T(8,128)S(1)} %sum_and_cut.10.refs_0_), channel_id=1, source_target_pairs={{0,8},{8,0},{16,24},{24,16},{1,9},{9,1},{17,25},{25,17},{2,10},{10... | collective-permute-start | bytes 245768 | tf_op jit(solution)/shard_map/ppermute | solution.py:1019
  304.5 16.4 %collective-permute-start.22 = (f32[40,512]{1,0:T(8,128)S(1)}, f32[40,512]{1,0:T(8,128)S(1)}, u32[]{:S(2)}, u32[]{:S(2)}) collective-permute-start(f32[40,512]{1,0:T(8,128)S(1)} %sum_and_cut.10.refs_0_), channel_id=1, source_target_pairs={{0,16},{8,24},{16,0},{24,8},{1,17},{9,25},{17,1},{25,9},{2,18},{10... | collective-permute-start | bytes 245768 | tf_op jit(solution)/shard_map/ppermute | solution.py:1019
  307.2 13.7 %collective-permute-start.23 = (f32[40,512]{1,0:T(8,128)S(1)}, f32[40,512]{1,0:T(8,128)S(1)}, u32[]{:S(2)}, u32[]{:S(2)}) collective-permute-start(f32[40,512]{1,0:T(8,128)S(1)} %sum_and_cut.10.refs_0_), channel_id=1, source_target_pairs={{0,24},{8,16},{16,8},{24,0},{1,25},{9,17},{17,9},{25,1},{2,26},{10... | collective-permute-start | bytes 245768 | tf_op jit(solution)/shard_map/ppermute | solution.py:1019
  308.9 6.3 %collective-permute-start.12 = (f32[16,512]{1,0:T(8,128)S(1)}, f32[16,512]{1,0:T(8,128)S(1)}, u32[]{:S(2)}, u32[]{:S(2)}) collective-permute-start(f32[16,512]{1,0:T(8,128)S(1)} %get-tuple-element.226), channel_id=1, source_target_pairs={{0,8},{8,0},{16,24},{24,16},{1,9},{9,1},{17,25},{25,17},{2,10},{10... | collective-permute-start | bytes 98312 | tf_op jit(solution)/shard_map/ppermute | solution.py:1019
  308.9 8.3 %collective-permute-start.13 = (f32[16,512]{1,0:T(8,128)S(1)}, f32[16,512]{1,0:T(8,128)S(1)}, u32[]{:S(2)}, u32[]{:S(2)}) collective-permute-start(f32[16,512]{1,0:T(8,128)S(1)} %get-tuple-element.227), channel_id=1, source_target_pairs={{0,16},{8,24},{16,0},{24,8},{1,17},{9,25},{17,1},{25,9},{2,18},{10... | collective-permute-start | bytes 98312 | tf_op jit(solution)/shard_map/ppermute | solution.py:1019
  315.2 5.7 %collective-permute-start.14 = (f32[16,512]{1,0:T(8,128)S(1)}, f32[16,512]{1,0:T(8,128)S(1)}, u32[]{:S(2)}, u32[]{:S(2)}) collective-permute-start(f32[16,512]{1,0:T(8,128)S(1)} %get-tuple-element.228), channel_id=1, source_target_pairs={{0,24},{8,16},{16,8},{24,0},{1,25},{9,17},{17,9},{25,1},{2,26},{10... | collective-permute-start | bytes 98312 | tf_op jit(solution)/shard_map/ppermute | solution.py:1019
  321.1 14.2 %collective-permute-start.27 = (f32[160,512]{1,0:T(8,128)S(1)}, f32[160,512]{1,0:T(8,128)S(1)}, u32[]{:S(2)}, u32[]{:S(2)}) collective-permute-start(f32[160,512]{1,0:T(8,128)S(1)} %join.6.refs_0_), channel_id=1, source_target_pairs={{0,2},{2,0},{4,6},{6,4},{1,3},{3,1},{5,7},{7,5},{8,10},{10,8},{12,... | collective-permute-start | bytes 983048 | tf_op jit(solution)/shard_map/ppermute | solution.py:1019
  323.0 12.4 %collective-permute-start.28 = (f32[160,512]{1,0:T(8,128)S(1)}, f32[160,512]{1,0:T(8,128)S(1)}, u32[]{:S(2)}, u32[]{:S(2)}) collective-permute-start(f32[160,512]{1,0:T(8,128)S(1)} %join.6.refs_0_), channel_id=1, source_target_pairs={{0,4},{2,6},{4,0},{6,2},{1,5},{3,7},{5,1},{7,3},{8,12},{10,14},{12... | collective-permute-start | bytes 983048 | tf_op jit(solution)/shard_map/ppermute | solution.py:1019
  325.2 13.6 %collective-permute-start.29 = (f32[160,512]{1,0:T(8,128)S(1)}, f32[160,512]{1,0:T(8,128)S(1)}, u32[]{:S(2)}, u32[]{:S(2)}) collective-permute-start(f32[160,512]{1,0:T(8,128)S(1)} %join.6.refs_0_), channel_id=1, source_target_pairs={{0,6},{2,4},{4,2},{6,0},{1,7},{3,5},{5,3},{7,1},{8,14},{10,12},{12... | collective-permute-start | bytes 983048 | tf_op jit(solution)/shard_map/ppermute | solution.py:1019
  325.2 4.3 %collective-permute-start.18 = (f32[16,512]{1,0:T(8,128)S(1)}, f32[16,512]{1,0:T(8,128)S(1)}, u32[]{:S(2)}, u32[]{:S(2)}) collective-permute-start(f32[16,512]{1,0:T(8,128)S(1)} %sum_and_cut.11.refs_0_), channel_id=1, source_target_pairs={{0,8},{8,0},{16,24},{24,16},{1,9},{9,1},{17,25},{25,17},{2,10},{10... | collective-permute-start | bytes 98312 | tf_op jit(solution)/shard_map/ppermute | solution.py:1019
  325.2 6.7 %collective-permute-start.19 = (f32[16,512]{1,0:T(8,128)S(1)}, f32[16,512]{1,0:T(8,128)S(1)}, u32[]{:S(2)}, u32[]{:S(2)}) collective-permute-start(f32[16,512]{1,0:T(8,128)S(1)} %sum_and_cut.11.refs_0_), channel_id=1, source_target_pairs={{0,16},{8,24},{16,0},{24,8},{1,17},{9,25},{17,1},{25,9},{2,18},{10... | collective-permute-start | bytes 98312 | tf_op jit(solution)/shard_map/ppermute | solution.py:1019
  329.5 5.7 %collective-permute-start.20 = (f32[16,512]{1,0:T(8,128)S(1)}, f32[16,512]{1,0:T(8,128)S(1)}, u32[]{:S(2)}, u32[]{:S(2)}) collective-permute-start(f32[16,512]{1,0:T(8,128)S(1)} %sum_and_cut.11.refs_0_), channel_id=1, source_target_pairs={{0,24},{8,16},{16,8},{24,0},{1,25},{9,17},{17,9},{25,1},{2,26},{10... | collective-permute-start | bytes 98312 | tf_op jit(solution)/shard_map/ppermute | solution.py:1019
  339.0 17.8 %collective-permute-start.31 = (f32[640,512]{1,0:T(8,128)S(1)}, f32[640,512]{1,0:T(8,128)}, u32[]{:S(2)}, u32[]{:S(2)}) collective-permute-start(f32[640,512]{1,0:T(8,128)S(1)} %join.8.refs_0_), channel_id=1, source_target_pairs={{0,1},{1,0},{2,3},{3,2},{4,5},{5,4},{6,7},{7,6},{8,9},{9,8},{10,11... | collective-permute-start | bytes 3932168 | tf_op jit(solution)/shard_map/ppermute | solution.py:1019
  339.1 6.4 %collective-permute-start.24 = (f32[64,512]{1,0:T(8,128)S(1)}, f32[64,512]{1,0:T(8,128)S(1)}, u32[]{:S(2)}, u32[]{:S(2)}) collective-permute-start(f32[64,512]{1,0:T(8,128)S(1)} %join.7.refs_0_), channel_id=1, source_target_pairs={{0,2},{2,0},{4,6},{6,4},{1,3},{3,1},{5,7},{7,5},{8,10},{10,8},{12,... | collective-permute-start | bytes 393224 | tf_op jit(solution)/shard_map/ppermute | solution.py:1019
  340.2 8.4 %collective-permute-start.25 = (f32[64,512]{1,0:T(8,128)S(1)}, f32[64,512]{1,0:T(8,128)S(1)}, u32[]{:S(2)}, u32[]{:S(2)}) collective-permute-start(f32[64,512]{1,0:T(8,128)S(1)} %join.7.refs_0_), channel_id=1, source_target_pairs={{0,4},{2,6},{4,0},{6,2},{1,5},{3,7},{5,1},{7,3},{8,12},{10,14},{12... | collective-permute-start | bytes 393224 | tf_op jit(solution)/shard_map/ppermute | solution.py:1019
  340.6 7.9 %collective-permute-start.26 = (f32[64,512]{1,0:T(8,128)S(1)}, f32[64,512]{1,0:T(8,128)S(1)}, u32[]{:S(2)}, u32[]{:S(2)}) collective-permute-start(f32[64,512]{1,0:T(8,128)S(1)} %join.7.refs_0_), channel_id=1, source_target_pairs={{0,6},{2,4},{4,2},{6,0},{1,7},{3,5},{5,3},{7,1},{8,14},{10,12},{12... | collective-permute-start | bytes 393224 | tf_op jit(solution)/shard_map/ppermute | solution.py:1019
  348.7 11.7 %collective-permute-start.30 = (f32[256,512]{1,0:T(8,128)S(1)}, f32[256,512]{1,0:T(8,128)S(1)}, u32[]{:S(2)}, u32[]{:S(2)}) collective-permute-start(f32[256,512]{1,0:T(8,128)S(1)} %join.9.refs_0_), channel_id=1, source_target_pairs={{0,1},{1,0},{2,3},{3,2},{4,5},{5,4},{6,7},{7,6},{8,9},{9,8},{10,11... | collective-permute-start | bytes 1572872 | tf_op jit(solution)/shard_map/ppermute | solution.py:1019
  (57 other events, 393.0 us)
Sparse Core Ops, SparseCore 0:
  199.1 195.2 all-reduce.2

commit v4 on v3

--- a/solution.py
+++ b/solution.py
@@ -108,6 +108,14 @@
     return values * (0.5 + 0.5 * jnp.tanh(inner))
 
 
+def gelu_and_slope(values):
+    square = values * values
+    bend = jnp.tanh(values * (ROOT + (ROOT * CUBIC) * square))
+    slope = ROOT + (3.0 * ROOT * CUBIC) * square
+    half = 0.5 + 0.5 * bend
+    return values * half, half * (1.0 + values * slope * (1.0 - bend))
+
+
 def gelu_slope(values):
     square = values * values
     bend = jnp.tanh(values * (ROOT + (ROOT * CUBIC) * square))
@@ -292,7 +300,7 @@
 
 def mixer_stage(
     sides, came, seen, scale, offset, pre_in, ahead_t, back_t, large_w, small_w,
-    low_out, large_out, small_out, waves_out, sent, noted, coefs, sums, spectrum, high, low,
+    low_out, large_out, small_out, waves_out, sent, noted, coefs, sums, spectrum, high,
 ):
     channels = pre_in.shape[1]
     canvas = pre_in.shape[0] // ROW
@@ -323,12 +331,12 @@
 
         def product(at, carry):
             real, imag, new_real, new_imag = times(spectrum, kernel, half, at, False)
-            high[real, :], low[real, :] = halves(new_real)
-            high[imag, :], low[imag, :] = halves(new_imag)
+            high[real, :] = new_real.astype(BF16)
+            high[imag, :] = new_imag.astype(BF16)
             return carry
 
         lax.fori_loop(0, half // 16, product, 0, unroll=4)
-        out[...] = back(back_t, high[...], low[...])
+        out[...] = ahead(back_t, high[...])
 
         def measure(at, carry):
             conv = jnp.where(at < side, inside, 0.0) * out[rows(at), :]
@@ -448,7 +456,7 @@
 
 def narrow_stage(
     sides, core, came, seen, wide_scale, wide_offset, hidden_in, u_in, weight,
-    low_out, proj_out, sent, noted, coefs, sums,
+    low_out, slope_out, proj_out, sent, noted, coefs, sums,
 ):
     channels = u_in.shape[1]
     canvas = u_in.shape[0] // ROW
@@ -470,7 +478,9 @@
 
         def step(at, carry):
             hidden = hidden_in[rows(at), block].astype(F32)
-            low_out[rows(at), block] = gelu(factor * hidden + constant).astype(BF16)
+            value, slope = gelu_and_slope(factor * hidden + constant)
+            low_out[rows(at), block] = value.astype(BF16)
+            slope_out[rows(at), block] = slope.astype(BF16)
             return carry
 
         lax.fori_loop(0, canvas, step, 0, unroll=14)
@@ -489,7 +499,7 @@
 
 
 def wide_back_stage(
-    sides, core, came, seen, wide_seen, scale, offset, proj_in, u_in, hidden_in, weight,
+    sides, core, came, seen, scale, offset, proj_in, u_in, hidden_in, slope_in, weight,
     down_out, grad_out, mine, other, noted, coefs, sums, found,
 ):
     channels = u_in.shape[1]
@@ -522,12 +532,10 @@
     for at_block in range(wide // channels):
         block = slice(at_block * channels, (at_block + 1) * channels)
         found[...] = dot(down_out[...], weight[:, block])
-        wide_factor = jnp.broadcast_to(wide_seen[2:3, block], (ROW, channels))
-        wide_constant = jnp.broadcast_to(wide_seen[3:4, block], (ROW, channels))
 
         def measure(at, carry):
             hidden = hidden_in[rows(at), block].astype(F32)
-            grad = found[rows(at), :] * gelu_slope(wide_factor * hidden + wide_constant)
+            grad = found[rows(at), :] * slope_in[rows(at), block].astype(F32)
             grad_out[rows(at), block] = grad.astype(BF16)
             return carry[0] + fold(grad), carry[1] + fold(grad * hidden)
 
@@ -871,7 +879,7 @@
         group = value if isinstance(value, tuple) else (value,)
         places.append((len(flat), len(group) if isinstance(value, tuple) else 0))
         for part in group:
-            if kind == "rows":
+            if kind in ("rows", "apart"):
                 part = pltpu.with_memory_space_constraint(part, pltpu.HBM)
             flat.append(part)
             specs.append(spec(part.shape, kind))
@@ -1110,8 +1118,8 @@
 
     ahead_t, back_t = const("ahead"), const("back")
     sides = (crop_sides, "smem")
-    scale, offset = (norm_gain, "whole"), (norm_shift, "whole")
-    wide_scale, wide_offset = (wide_gain[None], "whole"), (wide_shift[None], "whole")
+    scale, offset = (norm_gain, "apart"), (norm_shift, "apart")
+    wide_scale, wide_offset = (wide_gain[None], "apart"), (wide_shift[None], "apart")
     full, full_low = ((cells, channels), F32, "rows"), ((cells, channels), BF16, "rows")
     wide_low = ((cells, wide), BF16, "rows")
     wide_half = ((wide // 128, 128), F32, "whole")
@@ -1133,6 +1141,9 @@
     def w(value):
         return (value, "whole")
 
+    def apart(value):
+        return (value, "apart")
+
     x, u, sent = run(
         enter_stage,
         [sides, (image, "map"), (cotangent, "map")],
@@ -1144,7 +1155,7 @@
     large_w, small_w = call(
         kernel_waves_stage,
         1,
-        [w(kernel_large), w(kernel_small), w(const("large")), w(const("small"))],
+        [apart(kernel_large), apart(kernel_small), apart(const("large")), apart(const("small"))],
         [spectrum_out, spectrum_out],
         [
             ((tables["large"][0].shape[1], channels), BF16),
@@ -1154,7 +1165,7 @@
     came = together(came, large_w, small_w)
     pre_low, pre, sent, seen = run(
         first_stage,
-        [sides, w(came), scale, offset, r(x), w(proj_in)],
+        [sides, w(came), scale, offset, r(x), apart(proj_in)],
         [full_low, full, send(2 * channels), seen_out],
         [coefs(2), coefs(2)],
     )
@@ -1164,35 +1175,35 @@
     came = together(exchange(sent), down_t, out_t)
     mixer_low, large, small, mixer_waves, sent, first_seen = run(
         mixer_stage,
-        [sides, w(came), w(seen), scale, offset, r(pre), w(ahead_t), w(back_t), w(large_w), w(small_w)],
+        [sides, w(came), w(seen), scale, offset, r(pre), apart(ahead_t), apart(back_t), apart(large_w), apart(small_w)],
         [full_low, full, full, ((crops * 2 * half, channels), BF16, "rows"), send(4 * channels), seen_out],
-        [coefs(2), coefs(4), spectrum, spectrum_low, spectrum_low],
+        [coefs(2), coefs(4), spectrum, spectrum_low],
     )
     up_t, in_t = turned(sent, proj_up, proj_in)
     came = together(exchange(sent), up_t, in_t)
     merged_low, proj, sent, merge_seen = run(
         merge_stage,
-        [sides, w(came), w(seen), scale, offset, r(large), r(small), r(x), r(u), w(proj_out)],
+        [sides, w(came), w(seen), scale, offset, r(large), r(small), r(x), r(u), apart(proj_out)],
         [full_low, full, send(4 * channels), seen_out],
         [coefs(3), coefs(4)],
     )
     ffn_low, hidden, mine, other, mid_seen = run(
         widen_stage,
-        [sides, core, w(exchange(sent)), w(seen), scale, offset, r(x), r(proj), w(proj_up)],
+        [sides, core, w(exchange(sent)), w(seen), scale, offset, r(x), r(proj), apart(proj_up)],
         [full_low, wide_low, wide_half, wide_half, seen_out],
         [coefs(3), coefs(2, wide), ((canvas * ROW, channels), F32)],
     )
-    hidden_low, last, sent, wide_seen = run(
+    hidden_low, hidden_slope, last, sent, wide_seen = run(
         narrow_stage,
-        [sides, core, w(wide_exchange(mine, other)), w(seen), wide_scale, wide_offset, r(hidden), r(u), w(proj_down)],
-        [wide_low, full, send(4 * channels), wide_seen_out],
+        [sides, core, w(wide_exchange(mine, other)), w(seen), wide_scale, wide_offset, r(hidden), r(u), apart(proj_down)],
+        [wide_low, wide_low, full, send(4 * channels), wide_seen_out],
         [coefs(2, wide), coefs(4)],
     )
     down_low, hidden_grad, mine, other, last_seen = run(
         wide_back_stage,
         [
-            sides, core, w(exchange(sent)), w(seen), w(wide_seen), scale, offset,
-            r(last), r(u), r(hidden), w(down_t),
+            sides, core, w(exchange(sent)), w(seen), scale, offset,
+            r(last), r(u), r(hidden), r(hidden_slope), apart(down_t),
         ],
         [full_low, wide_low, wide_half, wide_half, seen_out],
         [coefs(3), coefs(2, wide), ((canvas * ROW, channels), F32)],
@@ -1201,7 +1212,7 @@
     came = wide_exchange(mine, other, grad_down)
     up_low, ffn_grad, sent, wide_noted = run(
         narrow_back_stage,
-        [sides, core, w(came), w(wide_seen), wide_scale, r(hidden_grad), r(hidden), r(x), r(proj), w(up_t)],
+        [sides, core, w(came), w(wide_seen), wide_scale, r(hidden_grad), r(hidden), r(x), r(proj), apart(up_t)],
         [wide_low, full, send(3 * channels), wide_seen_out],
         [coefs(3, wide), coefs(3)],
     )
@@ -1213,7 +1224,7 @@
         mid_back_stage,
         [
             sides, w(came), w(seen), w(merge_seen), w(mid_seen), w(last_seen), scale, offset,
-            r(x), r(u), r(proj), r(ffn_grad), r(large), r(small), w(out_t),
+            r(x), r(u), r(proj), r(ffn_grad), r(large), r(small), apart(out_t),
         ],
         [full, full_low, full, send(3 * channels), seen_out],
         [coefs(7), coefs(3)],
@@ -1223,7 +1234,7 @@
         mixer_back_stage,
         [
             sides, w(came), w(seen), w(merge_seen), w(first_seen), scale, offset,
-            r(large), r(small), r(merged_grad), r(pre), r(mixer_waves), w(ahead_t), w(back_t), w(large_w), w(small_w),
+            r(large), r(small), r(merged_grad), r(pre), r(mixer_waves), apart(ahead_t), apart(back_t), apart(large_w), apart(small_w),
         ],
         [full, spectrum_out, spectrum_out, send(2 * channels), seen_out],
         [
@@ -1239,7 +1250,7 @@
     other, mine = call(
         kernel_grad_stage,
         1,
-        [core, w(merged_low), w(back_low), w(large_sum), w(small_sum), w(taps_t[0]), w(taps_t[1])],
+        [core, w(merged_low), w(back_low), w(large_sum), w(small_sum), apart(taps_t[0]), apart(taps_t[1])],
         [half_taps, half_taps],
         [((tap_rows, channels), F32), ((channels, channels), F32)],
     )
@@ -1247,7 +1258,7 @@
     settle_taps = Settle(other, mine, BY_PERMUTES)
     pre_round, first_grad, sent, first_noted = run(
         first_back_stage,
-        [sides, w(came), w(seen), w(first_seen), scale, r(mixer_grad), r(pre), r(x), w(in_t)],
+        [sides, w(came), w(seen), w(first_seen), scale, r(mixer_grad), r(pre), r(x), apart(in_t)],
         [full_low, full, send(2 * channels), seen_out],
         [coefs(3), coefs(2)],
     )

time: 411 us -> 394 us (0.959)
  local copies, waits for them, and re-layouts: 51.2 us -> 31.1 us
  Pallas kernels: 128 us -> 134 us
    unnamed x134 -> x42, local copies, waits for them, and re-layouts: 37.1 us -> 19.1 us
    pallas_call x16, Pallas kernels: 103 us -> 111 us  [call(): pl.pallas_call(body, grid=(crops,), in_specs=specs, out_specs=[spec(shape...]
    psum x1, waiting for transfers between devices: 33 us -> 28.3 us  [local(): grad_down, grad_up = lax.psum((grad_down, grad_up), AXES)]
  transfers between devices with their start and end apart: 41 -> 41, of which waited for: 21 -> 23; matrix products, arithmetic and copies ran while one was open for 4% -> 4% of each run, Pallas kernels for 16% -> 18%
where the time goes in v4:
time: 394 us; the launch traced here: 392 us
  Pallas kernels  134 us (34%)
  waiting for transfers between devices  109 us (28%)
  starting transfers between devices  64.4 us (16%)
  blocking collectives  39.2 us (10%)
  local copies, waits for them, and re-layouts  31.1 us (8%)
  between operations  14.6 us (4%)
    pallas_call x16, Pallas kernels, call(): pl.pallas_call(body, grid=(crops,), in_specs=specs, out_specs=[spec(shape...  111 us
    all_to_all x7, waiting for transfers between devices, exchange(): return lax.all_to_all(sent, AXES, 0, 0, tiled=True)  38.6 us
    ppermute x26, waiting for transfers between devices, across(): lax.ppermute(part, axis, [(at, at ^ k) for at in range(size)])  35.7 us
    ppermute x26, starting transfers between devices, across(): lax.ppermute(part, axis, [(at, at ^ k) for at in range(size)])  34.4 us
    psum x1, waiting for transfers between devices, local(): grad_down, grad_up = lax.psum((grad_down, grad_up), AXES)  28.3 us
    all_to_all x2, blocking collectives, exchange(): return lax.all_to_all(sent, AXES, 0, 0, tiled=True)  28.2 us
    all_to_all x7, starting transfers between devices, exchange(): return lax.all_to_all(sent, AXES, 0, 0, tiled=True)  24.6 us
    unnamed x42, local copies, waits for them, and re-layouts  19.1 us
  transfers between devices with their start and end apart: 41, of which 23 were waited for; matrix products, arithmetic and copies ran while one was open for 4% of the time, Pallas kernels for 18%

profile of v4, /device:TPU:0, one launch (start us, length us, event | category | flops | bytes accessed | tf_op | source)
XLA Modules:
  0.0 391.8 jit_solution(2256734680121766164)
XLA Ops:
  8.8 2.8 enter_stage.1
  11.6 7.3 %all-to-all-start = ((f32[32,16,128]{2,1,0:T(8,128)}), f32[32,16,128]{2,1,0:T(8,128)S(1)}, u32[]{:S(2)}, u32[]{:S(2)}) async-start(f32[32,16,128]{2,1,0:T(8,128)} %get-tuple-element.141), calls=%async_computation | async-start | bytes 524288 | tf_op jit(solution)/shard_map/all_to_all | solution.py:949
  19.0 4.5 %kernel_waves_stage.1 = (f32[736,512]{1,0:T(8,128)S(1)}, f32[736,512]{1,0:T(8,128)S(1)}) custom-call(bf16[31,31,512]{2,1,0:T(8,128)(2,1)} %refs_0_.15, bf16[5,5,512]{2,1,0:T(8,128)(2,1)} %refs_1_.2, bf16[736,992]{1,0:T(8,128)(2,1)} %constant.45.clone.refs_2_, bf16[736,992]{1,0:T(8,128)(2,1)} %constant.46.clone.refs_3_, ...), custom_call_target="tpu_custom_call" | custom-call | bytes 7180288 | tf_op jit(solution)/shard_map/kernel_waves_stage/pallas_call | solution.py:891
  25.7 3.8 all-to-all-done.refs_1_
  29.6 4.6 %first_stage.1 = (bf16[896,512]{1,0:T(8,128)(2,1)}, f32[896,512]{1,0:T(8,128)}, f32[32,8,128]{2,1,0:T(8,128)}, f32[8,512]{1,0:T(8,128)S(1)}) custom-call(s32[4]{0:T(128)S(1)} %copy-done.9, f32[32,16,128]{2,1,0:T(8,128)S(1)} %all-to-all-done.refs_1_, f32[7,512]{1,0:T(8,128)} %refs_3_.10, f32[7,512]{1,0:T(8,128)} %refs_4_.12, ...), custom_call_target="tpu_custom_call" | custom-call | bytes 4632592 | tf_op jit(solution)/shard_map/first_stage/pallas_call | solution.py:891
  34.2 2.6 all-to-all-start.1
  36.8 2.5 copy.39
  40.3 4.7 %all-to-all-done.1.refs_1_ = f32[32,8,128]{2,1,0:T(8,128)S(1)} async-done(((f32[32,8,128]{2,1,0:T(8,128)}), f32[32,8,128]{2,1,0:T(8,128)S(1)}, u32[]{:S(2)}, u32[]{:S(2)}) %all-to-all-start.1) | async-done | bytes 131104 | tf_op jit(solution)/shard_map/all_to_all | solution.py:949
  45.0 13.6 %mixer_stage.1 = (bf16[896,512]{1,0:T(8,128)(2,1)}, f32[896,512]{1,0:T(8,128)}, f32[896,512]{1,0:T(8,128)}, bf16[2944,512]{1,0:T(8,128)(2,1)}, f32[32,16,128]{2,1,0:T(8,128)}, /*index=5*/f32[8,512]{1,0:T(8,128)S(1)}) custom-call(s32[4]{0:T(128)S(1)} %copy-done.9, f32[32,8,128]{2,1,0:T(8,128)S(1)} %all-to-all-done.1.refs_1_, ...), custom_call_target="tpu_custom_call" | custom-call | bytes 14225424 | tf_op jit(solution)/shard_map/mixer_stage/pallas_call | solution.py:891
  58.6 2.6 all-to-all-start.2
  61.3 2.6 copy.41
  64.9 6.9 %all-to-all-done.2.refs_1_ = f32[32,16,128]{2,1,0:T(8,128)S(1)} async-done(((f32[32,16,128]{2,1,0:T(8,128)}), f32[32,16,128]{2,1,0:T(8,128)S(1)}, u32[]{:S(2)}, u32[]{:S(2)}) %all-to-all-start.2) | async-done | bytes 262176 | tf_op jit(solution)/shard_map/all_to_all | solution.py:949
  71.8 6.1 %merge_stage.1 = (bf16[896,512]{1,0:T(8,128)(2,1)}, f32[896,512]{1,0:T(8,128)}, f32[32,16,128]{2,1,0:T(8,128)}, f32[8,512]{1,0:T(8,128)S(1)}) custom-call(s32[4]{0:T(128)S(1)} %copy-done.9, f32[32,16,128]{2,1,0:T(8,128)S(1)} %all-to-all-done.2.refs_1_, f32[8,512]{1,0:T(8,128)S(1)} %get-tuple-element.150.refs_2_.refs_3_.refs_4_, f32[7,512]{1,0:T(8,128)} %refs_3_.10, ...), custom_call_target="tpu_custom_call" | custom-call | bytes 9367568 | tf_op jit(solution)/shard_map/merge_stage/pallas_call | solution.py:891
  77.9 2.6 all-to-all-start.3
  80.5 10.6 %all-to-all-done.3.refs_2_ = f32[32,16,128]{2,1,0:T(8,128)S(1)} async-done(((f32[32,16,128]{2,1,0:T(8,128)}), f32[32,16,128]{2,1,0:T(8,128)S(1)}, u32[]{:S(2)}, u32[]{:S(2)}) %all-to-all-start.3) | async-done | bytes 262176 | tf_op jit(solution)/shard_map/all_to_all | solution.py:949
  91.1 6.8 %widen_stage.1 = (bf16[896,512]{1,0:T(8,128)(2,1)}, bf16[896,2048]{1,0:T(8,128)(2,1)}, f32[16,128]{1,0:T(8,128)S(1)}, f32[16,128]{1,0:T(8,128)S(1)}, f32[8,512]{1,0:T(8,128)S(1)}) custom-call(s32[4]{0:T(128)S(1)} %copy-done.9, s32[1]{0:T(128)} %bitcast.refs_1_.refs_0_.place, f32[32,16,128]{2,1,0:T(8,128)S(1)} %all-to-all-done.3.refs_2_, ...), custom_call_target="tpu_custom_call" | custom-call | bytes 9777172 | tf_op jit(solution)/shard_map/widen_stage/pallas_call | solution.py:891
  99.1 10.9 %all_to_all.55 = f32[16,16,128]{2,1,0:T(8,128)S(1)} all-to-all(f32[16,16,128]{2,1,0:T(8,128)S(1)} %broadcast_in_dim.15), channel_id=1, replica_groups=mesh['node'=4,'chip'=4,'core'=2] {'node','chip'}, dimensions={0} | all-to-all | bytes 262144 | tf_op jit(solution)/shard_map/all_to_all | solution.py:959
  111.3 10.2 %narrow_stage.1 = (bf16[896,2048]{1,0:T(8,128)(2,1)}, bf16[896,2048]{1,0:T(8,128)(2,1)}, f32[896,512]{1,0:T(8,128)}, f32[32,16,128]{2,1,0:T(8,128)S(1)}, f32[8,2048]{1,0:T(8,128)S(1)}) custom-call(s32[4]{0:T(128)S(1)} %copy-done.9, s32[1]{0:T(128)} %bitcast.refs_1_.refs_0_.place, f32[16,128]{1,0:T(8,128)S(1)} %reduce_sum.18.refs_2_, ...), custom_call_target="tpu_custom_call" | custom-call | bytes 16236564 | tf_op jit(solution)/shard_map/narrow_stage/pallas_call | solution.py:891
  121.4 12.5 %all_to_all.56.refs_2_ = f32[32,16,128]{2,1,0:T(8,128)S(1)} all-to-all(f32[32,16,128]{2,1,0:T(8,128)S(1)} %get-tuple-element.165), channel_id=1, replica_groups=mesh['node'=4,'chip'=4,'core'=2] {'node','chip','core'}, dimensions={0} | all-to-all | bytes 524288 | tf_op jit(solution)/shard_map/all_to_all | solution.py:949
  133.9 10.8 %wide_back_stage.1 = (bf16[896,512]{1,0:T(8,128)(2,1)}, bf16[896,2048]{1,0:T(8,128)(2,1)}, f32[16,128]{1,0:T(8,128)S(1)}, f32[16,128]{1,0:T(8,128)S(1)}, f32[8,512]{1,0:T(8,128)S(1)}) custom-call(s32[4]{0:T(128)S(1)} %copy-done.9, s32[1]{0:T(128)} %bitcast.refs_1_.refs_0_.place, f32[32,16,128]{2,1,0:T(8,128)S(1)} %all_to_all.56.refs_2_, ...), custom_call_target="tpu_custom_call" | custom-call | bytes 17117204 | tf_op jit(solution)/shard_map/wide_back_stage/pallas_call | solution.py:891
  146.6 3.7 all-to-all-start.6
  150.3 6.3 %weight_grad_stage.4 = f32[2048,512]{1,0:T(8,128)} custom-call(s32[1]{0:T(128)} %constant.39.clone.1.place, bf16[896,2048]{1,0:T(8,128)(2,1)} %get-tuple-element.172.inputs, bf16[896,512]{1,0:T(8,128)(2,1)} %get-tuple-element.173.gradient), custom_call_target="tpu_custom_call" | custom-call | flops 1879048192 | bytes 8781824 | tf_op jit(solution)/shard_map/weight_grad_stage/pallas_call | solution.py:924
  159.4 9.0 %narrow_back_stage.1 = (bf16[896,2048]{1,0:T(8,128)(2,1)}, f32[896,512]{1,0:T(8,128)}, f32[32,16,128]{2,1,0:T(8,128)}, f32[8,2048]{1,0:T(8,128)S(1)}) custom-call(s32[4]{0:T(128)S(1)} %copy-done.9, s32[1]{0:T(128)} %bitcast.refs_1_.refs_0_.place, f32[16,128]{1,0:T(8,128)S(1)} %reduce_sum.19.refs_2_, f32[16,128]{1,0:T(8,128)S(1)} %collective-permute-done.3.refs_3_, ...), custom_call_target="tpu_custom_call" | custom-call | bytes 18112532 | tf_op jit(solution)/shard_map/narrow_back_stage/pallas_call | solution.py:891
  168.4 4.2 %all-to-all-start.7 = ((f32[32,16,128]{2,1,0:T(8,128)}), f32[32,16,128]{2,1,0:T(8,128)S(1)}, u32[]{:S(2)}, u32[]{:S(2)}) async-start(f32[32,16,128]{2,1,0:T(8,128)} %get-tuple-element.177), calls=%async_computation.7 | async-start | bytes 524288 | tf_op jit(solution)/shard_map/all_to_all | solution.py:949
  172.6 6.3 %weight_grad_stage.5 = f32[512,2048]{1,0:T(8,128)} custom-call(s32[1]{0:T(128)} %constant.39.clone.1.place, bf16[896,512]{1,0:T(8,128)(2,1)} %get-tuple-element.178.inputs, bf16[896,2048]{1,0:T(8,128)(2,1)} %get-tuple-element.179.gradient), custom_call_target="tpu_custom_call" | custom-call | flops 1879048192 | bytes 8781824 | tf_op jit(solution)/shard_map/weight_grad_stage/pallas_call | solution.py:924
  178.9 4.2 %all-to-all-done.7.refs_1_ = f32[32,16,128]{2,1,0:T(8,128)S(1)} async-done(((f32[32,16,128]{2,1,0:T(8,128)}), f32[32,16,128]{2,1,0:T(8,128)S(1)}, u32[]{:S(2)}, u32[]{:S(2)}) %all-to-all-start.7) | async-done | bytes 262176 | tf_op jit(solution)/shard_map/all_to_all | solution.py:949
  183.2 8.4 %mid_back_stage.1 = (f32[896,512]{1,0:T(8,128)}, bf16[896,512]{1,0:T(8,128)(2,1)}, f32[896,512]{1,0:T(8,128)}, f32[32,16,128]{2,1,0:T(8,128)S(1)}, f32[8,512]{1,0:T(8,128)S(1)}) custom-call(s32[4]{0:T(128)S(1)} %copy-done.9, f32[32,16,128]{2,1,0:T(8,128)S(1)} %all-to-all-done.7.refs_1_, f32[8,512]{1,0:T(8,128)S(1)} %get-tuple-element.150.refs_2_.refs_3_.refs_4_, ...), custom_call_target="tpu_custom_call" | custom-call | bytes 14921744 | tf_op jit(solution)/shard_map/mid_back_stage/pallas_call | solution.py:891
  191.6 15.7 %all_to_all.57.refs_1_ = f32[32,16,128]{2,1,0:T(8,128)S(1)} all-to-all(f32[32,16,128]{2,1,0:T(8,128)S(1)} %get-tuple-element.183), channel_id=1, replica_groups=mesh['node'=4,'chip'=4,'core'=2] {'node','chip','core'}, dimensions={0} | all-to-all | bytes 524288 | tf_op jit(solution)/shard_map/all_to_all | solution.py:949
  207.3 14.7 %mixer_back_stage.1 = (f32[896,512]{1,0:T(8,128)}, f32[736,512]{1,0:T(8,128)S(1)}, f32[736,512]{1,0:T(8,128)S(1)}, f32[32,8,128]{2,1,0:T(8,128)}, f32[8,512]{1,0:T(8,128)S(1)}) custom-call(s32[4]{0:T(128)S(1)} %copy-done.9, f32[32,16,128]{2,1,0:T(8,128)S(1)} %all_to_all.57.refs_1_, f32[8,512]{1,0:T(8,128)S(1)} %get-tuple-element.150.refs_2_.refs_3_.refs_4_, ...), custom_call_target="tpu_custom_call" | custom-call | bytes 20025360 | tf_op jit(solution)/shard_map/mixer_back_stage/pallas_call | solution.py:891
  222.1 5.7 %kernel_grad_stage.1 = (f32[640,512]{1,0:T(8,128)}, f32[640,512]{1,0:T(8,128)S(1)}) custom-call(s32[1]{0:T(128)} %bitcast.refs_1_.refs_0_.place, bf16[896,512]{1,0:T(8,128)(2,1)S(1)} %copy-done.7, bf16[896,512]{1,0:T(8,128)(2,1)S(1)} %copy-done.8, f32[736,512]{1,0:T(8,128)S(1)} %get-tuple-element.190.refs_3_, f32[736,512]{1,0:T(8,128)S(1)} %get-tuple-element.191.refs_4_, ...), custom_call_target="tpu_custom_call" | custom-call | bytes 9732100 | tf_op jit(solution)/shard_map/kernel_grad_stage/pallas_call | solution.py:891
  230.0 2.6 all-to-all-start.9
  232.6 8.2 %all-to-all-done.9.refs_1_ = f32[32,8,128]{2,1,0:T(8,128)S(1)} async-done(((f32[32,8,128]{2,1,0:T(8,128)}), f32[32,8,128]{2,1,0:T(8,128)S(1)}, u32[]{:S(2)}, u32[]{:S(2)}) %all-to-all-start.9) | async-done | bytes 131104 | tf_op jit(solution)/shard_map/all_to_all | solution.py:949
  240.8 5.4 %first_back_stage.1 = (bf16[896,512]{1,0:T(8,128)(2,1)}, f32[896,512]{1,0:T(8,128)}, f32[32,8,128]{2,1,0:T(8,128)}, f32[8,512]{1,0:T(8,128)S(1)}) custom-call(s32[4]{0:T(128)S(1)} %copy-done.9, f32[32,8,128]{2,1,0:T(8,128)S(1)} %all-to-all-done.9.refs_1_, f32[8,512]{1,0:T(8,128)S(1)} %get-tuple-element.150.refs_2_.refs_3_.refs_4_, ...), custom_call_target="tpu_custom_call" | custom-call | bytes 8189968 | tf_op jit(solution)/shard_map/first_back_stage/pallas_call | solution.py:891
  251.0 3.1 sum_and_cut.6
  257.6 2.8 all-to-all-start.10
  264.3 11.3 %collective-permute-done.10.refs_2_ = f32[160,512]{1,0:T(8,128)S(1)} collective-permute-done((f32[160,512]{1,0:T(8,128)S(1)}, f32[160,512]{1,0:T(8,128)S(1)}, u32[]{:S(2)}, u32[]{:S(2)}) %collective-permute-start.10) | collective-permute-done | bytes 327712 | tf_op jit(solution)/shard_map/ppermute | solution.py:1027
  276.6 3.3 block_out_stage.1
  283.6 2.7 collective-permute-start.17
  286.5 3.2 leave_stage.1
  291.6 6.8 %collective-permute-start.21 = (f32[40,512]{1,0:T(8,128)S(1)}, f32[40,512]{1,0:T(8,128)S(1)}, u32[]{:S(2)}, u32[]{:S(2)}) collective-permute-start(f32[40,512]{1,0:T(8,128)S(1)} %sum_and_cut.10.refs_0_), channel_id=1, source_target_pairs={{0,8},{8,0},{16,24},{24,16},{1,9},{9,1},{17,25},{25,17},{2,10},{10... | collective-permute-start | bytes 245768 | tf_op jit(solution)/shard_map/ppermute | solution.py:1027
  302.8 2.6 collective-permute-done.12.refs_1_
  306.7 5.2 %collective-permute-done.14.refs_3_ = f32[16,512]{1,0:T(8,128)S(1)} collective-permute-done((f32[16,512]{1,0:T(8,128)S(1)}, f32[16,512]{1,0:T(8,128)S(1)}, u32[]{:S(2)}, u32[]{:S(2)}) %collective-permute-start.14) | collective-permute-done | bytes 32800 | tf_op jit(solution)/shard_map/ppermute | solution.py:1027
  321.1 4.1 %collective-permute-done.20.refs_3_ = f32[16,512]{1,0:T(8,128)S(1)} collective-permute-done((f32[16,512]{1,0:T(8,128)S(1)}, f32[16,512]{1,0:T(8,128)S(1)}, u32[]{:S(2)}, u32[]{:S(2)}) %collective-permute-start.20) | collective-permute-done | bytes 32800 | tf_op jit(solution)/shard_map/ppermute | solution.py:1027
  325.4 2.5 collective-permute-done.29.refs_3_
  331.7 2.8 collective-permute-done.24.refs_1_
  334.5 2.6 collective-permute-done.25.refs_2_
  349.7 28.3 %all-reduce.3.cloned.1.call-done = (f32[512,2048]{1,0:T(8,128)}, f32[2048,512]{1,0:T(8,128)}) async-done(((f32[512,2048]{1,0:T(8,128)}, f32[2048,512]{1,0:T(8,128)}), (f32[512,2048]{1,0:T(8,128)}, f32[2048,512]{1,0:T(8,128)})) %all-reduce.3.cloned.1.call-update) | async-done | bytes 8388624 | tf_op jit(solution)/shard_map/psum | solution.py:1222
  378.1 4.8 %copy.47 = f32[512,2048]{1,0:T(8,128)} copy(f32[512,2048]{1,0:T(8,128)} %get-tuple-element.304) | data formatting | bytes 8388608
  (130 shorter events, 67.6 us)
Async XLA Ops:
  11.6 17.9 %all-to-all-start = ((f32[32,16,128]{2,1,0:T(8,128)}), f32[32,16,128]{2,1,0:T(8,128)S(1)}, u32[]{:S(2)}, u32[]{:S(2)}) async-start(f32[32,16,128]{2,1,0:T(8,128)} %get-tuple-element.141), calls=%async_computation | async-start | bytes 524288 | tf_op jit(solution)/shard_map/all_to_all | solution.py:949
  19.0 17.8 %copy-start.13 = (bf16[2048,512]{1,0:T(8,128)(2,1)S(1)}, bf16[2048,512]{1,0:T(8,128)(2,1)}, u32[]{:S(2)}) copy-start(bf16[2048,512]{1,0:T(8,128)(2,1)} %refs_9_.4) | copy-start | bytes 6291460
  34.2 10.8 %all-to-all-start.1 = ((f32[32,8,128]{2,1,0:T(8,128)}), f32[32,8,128]{2,1,0:T(8,128)S(1)}, u32[]{:S(2)}, u32[]{:S(2)}) async-start(f32[32,8,128]{2,1,0:T(8,128)} %get-tuple-element.146), calls=%async_computation.1 | async-start | bytes 262144 | tf_op jit(solution)/shard_map/all_to_all | solution.py:949
  45.0 16.2 %copy-start.12 = (bf16[512,2048]{1,0:T(8,128)(2,1)S(1)}, bf16[512,2048]{1,0:T(8,128)(2,1)}, u32[]{:S(2)}) copy-start(bf16[512,2048]{1,0:T(8,128)(2,1)} %refs_8_.3) | copy-start | bytes 6291460
  58.6 13.2 %all-to-all-start.2 = ((f32[32,16,128]{2,1,0:T(8,128)}), f32[32,16,128]{2,1,0:T(8,128)S(1)}, u32[]{:S(2)}, u32[]{:S(2)}) async-start(f32[32,16,128]{2,1,0:T(8,128)} %get-tuple-element.152), calls=%async_computation.2 | async-start | bytes 524288 | tf_op jit(solution)/shard_map/all_to_all | solution.py:949
  77.9 13.2 %all-to-all-start.3 = ((f32[32,16,128]{2,1,0:T(8,128)}), f32[32,16,128]{2,1,0:T(8,128)S(1)}, u32[]{:S(2)}, u32[]{:S(2)}) async-start(f32[32,16,128]{2,1,0:T(8,128)} %get-tuple-element.159), calls=%async_computation.3 | async-start | bytes 524288 | tf_op jit(solution)/shard_map/all_to_all | solution.py:949
  97.9 1.2 collective-permute-start
  110.0 1.2 collective-permute-start.1
  144.7 1.2 collective-permute-start.2
  146.6 11.5 %all-to-all-start.6 = ((f32[16,16,128]{2,1,0:T(8,128)}), f32[16,16,128]{2,1,0:T(8,128)S(1)}, u32[]{:S(2)}, u32[]{:S(2)}) async-start(f32[16,16,128]{2,1,0:T(8,128)} %broadcast_in_dim.19), calls=%async_computation.6 | async-start | bytes 262144 | tf_op jit(solution)/shard_map/all_to_all | solution.py:959
  158.1 1.2 collective-permute-start.3
  168.4 14.8 %all-to-all-start.7 = ((f32[32,16,128]{2,1,0:T(8,128)}), f32[32,16,128]{2,1,0:T(8,128)S(1)}, u32[]{:S(2)}, u32[]{:S(2)}) async-start(f32[32,16,128]{2,1,0:T(8,128)} %get-tuple-element.177), calls=%async_computation.7 | async-start | bytes 524288 | tf_op jit(solution)/shard_map/all_to_all | solution.py:949
  172.6 205.5 %all-reduce.3.cloned.1.call-start = ((), (), s32[]{:S(2)}) async-start(), calls=%async_computation.11 | async-start | bytes 16777216 | tf_op jit(solution)/shard_map/psum | solution.py:1222
  207.3 14.7 %copy-start.7 = (bf16[896,512]{1,0:T(8,128)(2,1)S(1)}, bf16[896,512]{1,0:T(8,128)(2,1)}, u32[]{:S(2)}) copy-start(bf16[896,512]{1,0:T(8,128)(2,1)} %get-tuple-element.188.refs_1_) | copy-start | bytes 2752516
  207.3 14.7 %copy-start.8 = (bf16[896,512]{1,0:T(8,128)(2,1)S(1)}, bf16[896,512]{1,0:T(8,128)(2,1)}, u32[]{:S(2)}) copy-start(bf16[896,512]{1,0:T(8,128)(2,1)} %get-tuple-element.189.refs_2_) | copy-start | bytes 2752516
  222.0 5.7 %copy-start.10 = (f32[8,512]{1,0:T(8,128)}, f32[8,512]{1,0:T(8,128)S(1)}, u32[]{:S(2)}) copy-start(f32[8,512]{1,0:T(8,128)S(1)} %get-tuple-element.267) | copy-start | bytes 49156
  228.8 20.9 %collective-permute-start.5 = (f32[640,512]{1,0:T(8,128)}, f32[640,512]{1,0:T(8,128)}, u32[]{:S(2)}, u32[]{:S(2)}) collective-permute-start(f32[640,512]{1,0:T(8,128)} %get-tuple-element.192), channel_id=1, source_target_pairs={{0,1},{1,0},{2,3},{3,2},{4,5},{5,4},{6,7},{7,6},{8,9},{9,8},{10,11... | collective-permute-start | bytes 3932168 | tf_op jit(solution)/shard_map/ppermute | solution.py:1042
  230.0 10.8 %all-to-all-start.9 = ((f32[32,8,128]{2,1,0:T(8,128)}), f32[32,8,128]{2,1,0:T(8,128)S(1)}, u32[]{:S(2)}, u32[]{:S(2)}) async-start(f32[32,8,128]{2,1,0:T(8,128)} %get-tuple-element.187), calls=%async_computation.9 | async-start | bytes 262144 | tf_op jit(solution)/shard_map/all_to_all | solution.py:949
  240.8 6.0 %copy-start.2 = (bf16[896,512]{1,0:T(8,128)(2,1)S(1)}, bf16[896,512]{1,0:T(8,128)(2,1)}, u32[]{:S(2)}) copy-start(bf16[896,512]{1,0:T(8,128)(2,1)} %get-tuple-element.169.inputs) | copy-start | bytes 2752516
  248.5 11.9 %collective-permute-start.4 = (f32[256,512]{1,0:T(8,128)S(1)}, f32[256,512]{1,0:T(8,128)S(1)}, u32[]{:S(2)}, u32[]{:S(2)}) collective-permute-start(f32[256,512]{1,0:T(8,128)S(1)} %weight_grad_stage.6), channel_id=1, source_target_pairs={{0,1},{1,0},{2,3},{3,2},{4,5},{5,4},{6,7},{7,6},{8,9},{9,8},{10,11... | collective-permute-start | bytes 1572872 | tf_op jit(solution)/shard_map/ppermute | solution.py:1042
  254.1 21.5 %collective-permute-start.10 = (f32[160,512]{1,0:T(8,128)S(1)}, f32[160,512]{1,0:T(8,128)S(1)}, u32[]{:S(2)}, u32[]{:S(2)}) collective-permute-start(f32[160,512]{1,0:T(8,128)S(1)} %get-tuple-element.212), channel_id=1, source_target_pairs={{0,4},{2,6},{4,0},{6,2},{1,5},{3,7},{5,1},{7,3},{8,12},{10,14},{12... | collective-permute-start | bytes 983048 | tf_op jit(solution)/shard_map/ppermute | solution.py:1027
  254.7 25.2 %collective-permute-start.11 = (f32[160,512]{1,0:T(8,128)}, f32[160,512]{1,0:T(8,128)S(1)}, u32[]{:S(2)}, u32[]{:S(2)}) collective-permute-start(f32[160,512]{1,0:T(8,128)} %get-tuple-element.213), channel_id=1, source_target_pairs={{0,6},{2,4},{4,2},{6,0},{1,7},{3,5},{5,3},{7,1},{8,14},{10,12},{12... | collective-permute-start | bytes 983048 | tf_op jit(solution)/shard_map/ppermute | solution.py:1027
  256.0 23.9 %collective-permute-start.9 = (f32[160,512]{1,0:T(8,128)}, f32[160,512]{1,0:T(8,128)}, u32[]{:S(2)}, u32[]{:S(2)}) collective-permute-start(f32[160,512]{1,0:T(8,128)} %get-tuple-element.211), channel_id=1, source_target_pairs={{0,2},{2,0},{4,6},{6,4},{1,3},{3,1},{5,7},{7,5},{8,10},{10,8},{12,... | collective-permute-start | bytes 983048 | tf_op jit(solution)/shard_map/ppermute | solution.py:1027
  257.6 28.9 %all-to-all-start.10 = ((f32[32,8,128]{2,1,0:T(8,128)}), f32[32,8,128]{2,1,0:T(8,128)S(1)}, u32[]{:S(2)}, u32[]{:S(2)}) async-start(f32[32,8,128]{2,1,0:T(8,128)} %get-tuple-element.207), calls=%async_computation.10 | async-start | bytes 262144 | tf_op jit(solution)/shard_map/all_to_all | solution.py:949
  261.3 22.3 %collective-permute-start.6 = (f32[64,512]{1,0:T(8,128)}, f32[64,512]{1,0:T(8,128)S(1)}, u32[]{:S(2)}, u32[]{:S(2)}) collective-permute-start(f32[64,512]{1,0:T(8,128)} %get-tuple-element.208), channel_id=1, source_target_pairs={{0,2},{2,0},{4,6},{6,4},{1,3},{3,1},{5,7},{7,5},{8,10},{10,8},{12,... | collective-permute-start | bytes 393224 | tf_op jit(solution)/shard_map/ppermute | solution.py:1027
  262.8 23.5 %collective-permute-start.7 = (f32[64,512]{1,0:T(8,128)}, f32[64,512]{1,0:T(8,128)S(1)}, u32[]{:S(2)}, u32[]{:S(2)}) collective-permute-start(f32[64,512]{1,0:T(8,128)} %get-tuple-element.209), channel_id=1, source_target_pairs={{0,4},{2,6},{4,0},{6,2},{1,5},{3,7},{5,1},{7,3},{8,12},{10,14},{12... | collective-permute-start | bytes 393224 | tf_op jit(solution)/shard_map/ppermute | solution.py:1027
  275.6 10.7 %collective-permute-start.8 = (f32[64,512]{1,0:T(8,128)}, f32[64,512]{1,0:T(8,128)S(1)}, u32[]{:S(2)}, u32[]{:S(2)}) collective-permute-start(f32[64,512]{1,0:T(8,128)} %get-tuple-element.210), channel_id=1, source_target_pairs={{0,6},{2,4},{4,2},{6,0},{1,7},{3,5},{5,3},{7,1},{8,14},{10,12},{12... | collective-permute-start | bytes 393224 | tf_op jit(solution)/shard_map/ppermute | solution.py:1027
  281.8 7.9 %collective-permute-start.15 = (f32[40,512]{1,0:T(8,128)S(1)}, f32[40,512]{1,0:T(8,128)S(1)}, u32[]{:S(2)}, u32[]{:S(2)}) collective-permute-start(f32[40,512]{1,0:T(8,128)S(1)} %get-tuple-element.231), channel_id=1, source_target_pairs={{0,8},{8,0},{16,24},{24,16},{1,9},{9,1},{17,25},{25,17},{2,10},{10... | collective-permute-start | bytes 245768 | tf_op jit(solution)/shard_map/ppermute | solution.py:1027
  282.8 8.7 %collective-permute-start.16 = (f32[40,512]{1,0:T(8,128)S(1)}, f32[40,512]{1,0:T(8,128)S(1)}, u32[]{:S(2)}, u32[]{:S(2)}) collective-permute-start(f32[40,512]{1,0:T(8,128)S(1)} %get-tuple-element.232), channel_id=1, source_target_pairs={{0,16},{8,24},{16,0},{24,8},{1,17},{9,25},{17,1},{25,9},{2,18},{10... | collective-permute-start | bytes 245768 | tf_op jit(solution)/shard_map/ppermute | solution.py:1027
  283.6 7.9 %collective-permute-start.17 = (f32[40,512]{1,0:T(8,128)S(1)}, f32[40,512]{1,0:T(8,128)S(1)}, u32[]{:S(2)}, u32[]{:S(2)}) collective-permute-start(f32[40,512]{1,0:T(8,128)S(1)} %get-tuple-element.233), channel_id=1, source_target_pairs={{0,24},{8,16},{16,8},{24,0},{1,25},{9,17},{17,9},{25,1},{2,26},{10... | collective-permute-start | bytes 245768 | tf_op jit(solution)/shard_map/ppermute | solution.py:1027
  291.6 20.3 %collective-permute-start.21 = (f32[40,512]{1,0:T(8,128)S(1)}, f32[40,512]{1,0:T(8,128)S(1)}, u32[]{:S(2)}, u32[]{:S(2)}) collective-permute-start(f32[40,512]{1,0:T(8,128)S(1)} %sum_and_cut.10.refs_0_), channel_id=1, source_target_pairs={{0,8},{8,0},{16,24},{24,16},{1,9},{9,1},{17,25},{25,17},{2,10},{10... | collective-permute-start | bytes 245768 | tf_op jit(solution)/shard_map/ppermute | solution.py:1027
  298.4 13.5 %collective-permute-start.22 = (f32[40,512]{1,0:T(8,128)S(1)}, f32[40,512]{1,0:T(8,128)S(1)}, u32[]{:S(2)}, u32[]{:S(2)}) collective-permute-start(f32[40,512]{1,0:T(8,128)S(1)} %sum_and_cut.10.refs_0_), channel_id=1, source_target_pairs={{0,16},{8,24},{16,0},{24,8},{1,17},{9,25},{17,1},{25,9},{2,18},{10... | collective-permute-start | bytes 245768 | tf_op jit(solution)/shard_map/ppermute | solution.py:1027
  298.4 13.5 %collective-permute-start.23 = (f32[40,512]{1,0:T(8,128)S(1)}, f32[40,512]{1,0:T(8,128)S(1)}, u32[]{:S(2)}, u32[]{:S(2)}) collective-permute-start(f32[40,512]{1,0:T(8,128)S(1)} %sum_and_cut.10.refs_0_), channel_id=1, source_target_pairs={{0,24},{8,16},{16,8},{24,0},{1,25},{9,17},{17,9},{25,1},{2,26},{10... | collective-permute-start | bytes 245768 | tf_op jit(solution)/shard_map/ppermute | solution.py:1027
  300.8 4.5 %collective-permute-start.12 = (f32[16,512]{1,0:T(8,128)S(1)}, f32[16,512]{1,0:T(8,128)S(1)}, u32[]{:S(2)}, u32[]{:S(2)}) collective-permute-start(f32[16,512]{1,0:T(8,128)S(1)} %get-tuple-element.228), channel_id=1, source_target_pairs={{0,8},{8,0},{16,24},{24,16},{1,9},{9,1},{17,25},{25,17},{2,10},{10... | collective-permute-start | bytes 98312 | tf_op jit(solution)/shard_map/ppermute | solution.py:1027
  301.9 4.8 %collective-permute-start.13 = (f32[16,512]{1,0:T(8,128)S(1)}, f32[16,512]{1,0:T(8,128)S(1)}, u32[]{:S(2)}, u32[]{:S(2)}) collective-permute-start(f32[16,512]{1,0:T(8,128)S(1)} %get-tuple-element.229), channel_id=1, source_target_pairs={{0,16},{8,24},{16,0},{24,8},{1,17},{9,25},{17,1},{25,9},{2,18},{10... | collective-permute-start | bytes 98312 | tf_op jit(solution)/shard_map/ppermute | solution.py:1027
  305.4 6.5 %collective-permute-start.14 = (f32[16,512]{1,0:T(8,128)S(1)}, f32[16,512]{1,0:T(8,128)S(1)}, u32[]{:S(2)}, u32[]{:S(2)}) collective-permute-start(f32[16,512]{1,0:T(8,128)S(1)} %get-tuple-element.230), channel_id=1, source_target_pairs={{0,24},{8,16},{16,8},{24,0},{1,25},{9,17},{17,9},{25,1},{2,26},{10... | collective-permute-start | bytes 98312 | tf_op jit(solution)/shard_map/ppermute | solution.py:1027
  312.1 13.2 %collective-permute-start.27 = (f32[160,512]{1,0:T(8,128)S(1)}, f32[160,512]{1,0:T(8,128)S(1)}, u32[]{:S(2)}, u32[]{:S(2)}) collective-permute-start(f32[160,512]{1,0:T(8,128)S(1)} %join.6.refs_0_), channel_id=1, source_target_pairs={{0,2},{2,0},{4,6},{6,4},{1,3},{3,1},{5,7},{7,5},{8,10},{10,8},{12,... | collective-permute-start | bytes 983048 | tf_op jit(solution)/shard_map/ppermute | solution.py:1027
  312.2 13.2 %collective-permute-start.28 = (f32[160,512]{1,0:T(8,128)S(1)}, f32[160,512]{1,0:T(8,128)S(1)}, u32[]{:S(2)}, u32[]{:S(2)}) collective-permute-start(f32[160,512]{1,0:T(8,128)S(1)} %join.6.refs_0_), channel_id=1, source_target_pairs={{0,4},{2,6},{4,0},{6,2},{1,5},{3,7},{5,1},{7,3},{8,12},{10,14},{12... | collective-permute-start | bytes 983048 | tf_op jit(solution)/shard_map/ppermute | solution.py:1027
  314.4 13.4 %collective-permute-start.29 = (f32[160,512]{1,0:T(8,128)S(1)}, f32[160,512]{1,0:T(8,128)S(1)}, u32[]{:S(2)}, u32[]{:S(2)}) collective-permute-start(f32[160,512]{1,0:T(8,128)S(1)} %join.6.refs_0_), channel_id=1, source_target_pairs={{0,6},{2,4},{4,2},{6,0},{1,7},{3,5},{5,3},{7,1},{8,14},{10,12},{12... | collective-permute-start | bytes 983048 | tf_op jit(solution)/shard_map/ppermute | solution.py:1027
  315.6 3.9 collective-permute-start.18
  315.6 5.5 %collective-permute-start.19 = (f32[16,512]{1,0:T(8,128)S(1)}, f32[16,512]{1,0:T(8,128)S(1)}, u32[]{:S(2)}, u32[]{:S(2)}) collective-permute-start(f32[16,512]{1,0:T(8,128)S(1)} %sum_and_cut.11.refs_0_), channel_id=1, source_target_pairs={{0,16},{8,24},{16,0},{24,8},{1,17},{9,25},{17,1},{25,9},{2,18},{10... | collective-permute-start | bytes 98312 | tf_op jit(solution)/shard_map/ppermute | solution.py:1027
  319.6 5.7 %collective-permute-start.20 = (f32[16,512]{1,0:T(8,128)S(1)}, f32[16,512]{1,0:T(8,128)S(1)}, u32[]{:S(2)}, u32[]{:S(2)}) collective-permute-start(f32[16,512]{1,0:T(8,128)S(1)} %sum_and_cut.11.refs_0_), channel_id=1, source_target_pairs={{0,24},{8,16},{16,8},{24,0},{1,25},{9,17},{17,9},{25,1},{2,26},{10... | collective-permute-start | bytes 98312 | tf_op jit(solution)/shard_map/ppermute | solution.py:1027
  328.0 17.2 %collective-permute-start.31 = (f32[640,512]{1,0:T(8,128)S(1)}, f32[640,512]{1,0:T(8,128)}, u32[]{:S(2)}, u32[]{:S(2)}) collective-permute-start(f32[640,512]{1,0:T(8,128)S(1)} %join.8.refs_0_), channel_id=1, source_target_pairs={{0,1},{1,0},{2,3},{3,2},{4,5},{5,4},{6,7},{7,6},{8,9},{9,8},{10,11... | collective-permute-start | bytes 3932168 | tf_op jit(solution)/shard_map/ppermute | solution.py:1027
  328.1 6.4 %collective-permute-start.24 = (f32[64,512]{1,0:T(8,128)S(1)}, f32[64,512]{1,0:T(8,128)S(1)}, u32[]{:S(2)}, u32[]{:S(2)}) collective-permute-start(f32[64,512]{1,0:T(8,128)S(1)} %join.7.refs_0_), channel_id=1, source_target_pairs={{0,2},{2,0},{4,6},{6,4},{1,3},{3,1},{5,7},{7,5},{8,10},{10,8},{12,... | collective-permute-start | bytes 393224 | tf_op jit(solution)/shard_map/ppermute | solution.py:1027
  328.7 8.4 %collective-permute-start.25 = (f32[64,512]{1,0:T(8,128)S(1)}, f32[64,512]{1,0:T(8,128)S(1)}, u32[]{:S(2)}, u32[]{:S(2)}) collective-permute-start(f32[64,512]{1,0:T(8,128)S(1)} %join.7.refs_0_), channel_id=1, source_target_pairs={{0,4},{2,6},{4,0},{6,2},{1,5},{3,7},{5,1},{7,3},{8,12},{10,14},{12... | collective-permute-start | bytes 393224 | tf_op jit(solution)/shard_map/ppermute | solution.py:1027
  329.8 7.4 %collective-permute-start.26 = (f32[64,512]{1,0:T(8,128)S(1)}, f32[64,512]{1,0:T(8,128)S(1)}, u32[]{:S(2)}, u32[]{:S(2)}) collective-permute-start(f32[64,512]{1,0:T(8,128)S(1)} %join.7.refs_0_), channel_id=1, source_target_pairs={{0,6},{2,4},{4,2},{6,0},{1,7},{3,5},{5,3},{7,1},{8,14},{10,12},{12... | collective-permute-start | bytes 393224 | tf_op jit(solution)/shard_map/ppermute | solution.py:1027
  337.3 11.5 %collective-permute-start.30 = (f32[256,512]{1,0:T(8,128)S(1)}, f32[256,512]{1,0:T(8,128)S(1)}, u32[]{:S(2)}, u32[]{:S(2)}) collective-permute-start(f32[256,512]{1,0:T(8,128)S(1)} %join.9.refs_0_), channel_id=1, source_target_pairs={{0,1},{1,0},{2,3},{3,2},{4,5},{5,4},{6,7},{7,6},{8,9},{9,8},{10,11... | collective-permute-start | bytes 1572872 | tf_op jit(solution)/shard_map/ppermute | solution.py:1027
  378.1 4.9 %copy-start.14 = (f32[2048,512]{1,0:T(8,128)S(1)}, f32[2048,512]{1,0:T(8,128)}, u32[]{:S(2)}) copy-start(f32[2048,512]{1,0:T(8,128)} %get-tuple-element.305) | copy-start | bytes 12582916
  (11 other events, 15.9 us)
Sparse Core Ops, SparseCore 0:
  183.3 194.7 all-reduce.2

commit v5 on v4

--- a/solution.py
+++ b/solution.py
@@ -335,7 +335,7 @@
             high[imag, :] = new_imag.astype(BF16)
             return carry
 
-        lax.fori_loop(0, half // 16, product, 0, unroll=4)
+        lax.fori_loop(0, half // 16, product, 0, unroll=23)
         out[...] = ahead(back_t, high[...])
 
         def measure(at, carry):
@@ -382,7 +382,7 @@
         parts = (proj, proj * proj, proj * x, proj * u)
         return tuple(old + fold(part) for old, part in zip(carry, parts))
 
-    add_sums(sums, lax.fori_loop(0, canvas, measure, zeros(4, channels), unroll=7))
+    add_sums(sums, lax.fori_loop(0, canvas, measure, zeros(4, channels), unroll=14))
     publish(sums, sent)
 
 
@@ -494,7 +494,7 @@
         parts = (proj, proj * proj, proj * u, u)
         return tuple(old + fold(part) for old, part in zip(carry, parts))
 
-    add_sums(sums, lax.fori_loop(0, canvas, measure, zeros(4, channels), unroll=7))
+    add_sums(sums, lax.fori_loop(0, canvas, measure, zeros(4, channels), unroll=14))
     publish(sums, sent)
 
 
@@ -539,7 +539,7 @@
             grad_out[rows(at), block] = grad.astype(BF16)
             return carry[0] + fold(grad), carry[1] + fold(grad * hidden)
 
-        pair = lax.fori_loop(0, canvas, measure, zeros(2, channels), unroll=7)
+        pair = lax.fori_loop(0, canvas, measure, zeros(2, channels), unroll=14)
         parts[0].append(pair[0])
         parts[1].append(pair[1])
     add_sums(sums, [jnp.concatenate(part, axis=1) for part in parts])
@@ -583,7 +583,7 @@
         parts = (grad, grad * x_in[rows(at), :].astype(F32), grad * proj_in[rows(at), :])
         return tuple(old + fold(part) for old, part in zip(carry, parts))
 
-    add_sums(sums, lax.fori_loop(0, canvas, measure, zeros(3, channels), unroll=7))
+    add_sums(sums, lax.fori_loop(0, canvas, measure, zeros(3, channels), unroll=14))
     publish(sums, sent)
 
 
@@ -641,7 +641,7 @@
         parts = (grad, grad * large_conv, grad * small_conv)
         return tuple(old + fold(part) for old, part in zip(carry, parts))
 
-    add_sums(sums, lax.fori_loop(0, canvas, measure, zeros(3, channels), unroll=7))
+    add_sums(sums, lax.fori_loop(0, canvas, measure, zeros(3, channels), unroll=14))
     publish(sums, sent)
 
 
@@ -703,7 +703,7 @@
         large_sum[...] = jnp.zeros_like(large_sum)
         small_sum[...] = jnp.zeros_like(small_sum)
 
-    lax.fori_loop(0, half // 16, product, 0, unroll=4)
+    lax.fori_loop(0, half // 16, product, 0, unroll=23)
     grad_out[...] = back_once(back_t, summed[...])
     reciprocal = first_seen[1:2]
     factor = scale[1:2] * reciprocal
@@ -717,7 +717,7 @@
         grad_out[rows(at), :] = grad
         return carry[0] + fold(grad), carry[1] + fold(grad * pre)
 
-    add_sums(sums, lax.fori_loop(0, canvas, measure, zeros(2, channels), unroll=7))
+    add_sums(sums, lax.fori_loop(0, canvas, measure, zeros(2, channels), unroll=14))
     publish(sums, sent)
 
 

time: 394 us -> 390 us (0.990)
  Pallas kernels: 134 us -> 128 us
    pallas_call x16, Pallas kernels: 111 us -> 105 us  [call(): pl.pallas_call(body, grid=(crops,), in_specs=specs, out_specs=[spec(shape...]
  transfers between devices with their start and end apart: 41 -> 41, of which waited for: 23 -> 24; matrix products, arithmetic and copies ran while one was open for 4% -> 4% of each run, Pallas kernels for 18% -> 18%
where the time goes in v5:
time: 390 us; the launch traced here: 388 us
  Pallas kernels  128 us (33%)
  waiting for transfers between devices  112 us (29%)
  starting transfers between devices  63.4 us (16%)
  blocking collectives  39.2 us (10%)
  local copies, waits for them, and re-layouts  31.1 us (8%)
  between operations  14.6 us (4%)
    pallas_call x16, Pallas kernels, call(): pl.pallas_call(body, grid=(crops,), in_specs=specs, out_specs=[spec(shape...  105 us
    all_to_all x7, waiting for transfers between devices, exchange(): return lax.all_to_all(sent, AXES, 0, 0, tiled=True)  38.6 us
    ppermute x26, waiting for transfers between devices, across(): lax.ppermute(part, axis, [(at, at ^ k) for at in range(size)])  36.3 us
    ppermute x26, starting transfers between devices, across(): lax.ppermute(part, axis, [(at, at ^ k) for at in range(size)])  33.3 us
    psum x1, waiting for transfers between devices, local(): grad_down, grad_up = lax.psum((grad_down, grad_up), AXES)  31.4 us
    all_to_all x2, blocking collectives, exchange(): return lax.all_to_all(sent, AXES, 0, 0, tiled=True)  28.3 us
    all_to_all x7, starting transfers between devices, exchange(): return lax.all_to_all(sent, AXES, 0, 0, tiled=True)  24.6 us
    unnamed x42, local copies, waits for them, and re-layouts  19.1 us
  transfers between devices with their start and end apart: 41, of which 24 were waited for; matrix products, arithmetic and copies ran while one was open for 4% of the time, Pallas kernels for 18%

profile of v5, /device:TPU:0, one launch (start us, length us, event | category | flops | bytes accessed | tf_op | source)
XLA Modules:
  0.0 388.2 jit_solution(8641204861620526208)
XLA Ops:
  8.8 2.8 enter_stage.1
  11.6 7.3 %all-to-all-start = ((f32[32,16,128]{2,1,0:T(8,128)}), f32[32,16,128]{2,1,0:T(8,128)S(1)}, u32[]{:S(2)}, u32[]{:S(2)}) async-start(f32[32,16,128]{2,1,0:T(8,128)} %get-tuple-element.141), calls=%async_computation | async-start | bytes 524288 | tf_op jit(solution)/shard_map/all_to_all | solution.py:949
  19.0 4.5 %kernel_waves_stage.1 = (f32[736,512]{1,0:T(8,128)S(1)}, f32[736,512]{1,0:T(8,128)S(1)}) custom-call(bf16[31,31,512]{2,1,0:T(8,128)(2,1)} %refs_0_.15, bf16[5,5,512]{2,1,0:T(8,128)(2,1)} %refs_1_.2, bf16[736,992]{1,0:T(8,128)(2,1)} %constant.45.clone.refs_2_, bf16[736,992]{1,0:T(8,128)(2,1)} %constant.46.clone.refs_3_, ...), custom_call_target="tpu_custom_call" | custom-call | bytes 7180288 | tf_op jit(solution)/shard_map/kernel_waves_stage/pallas_call | solution.py:891
  25.7 3.8 all-to-all-done.refs_1_
  29.6 4.6 %first_stage.1 = (bf16[896,512]{1,0:T(8,128)(2,1)}, f32[896,512]{1,0:T(8,128)}, f32[32,8,128]{2,1,0:T(8,128)}, f32[8,512]{1,0:T(8,128)S(1)}) custom-call(s32[4]{0:T(128)S(1)} %copy-done.9, f32[32,16,128]{2,1,0:T(8,128)S(1)} %all-to-all-done.refs_1_, f32[7,512]{1,0:T(8,128)} %refs_3_.10, f32[7,512]{1,0:T(8,128)} %refs_4_.12, ...), custom_call_target="tpu_custom_call" | custom-call | bytes 4632592 | tf_op jit(solution)/shard_map/first_stage/pallas_call | solution.py:891
  34.2 2.6 all-to-all-start.1
  40.3 4.7 %all-to-all-done.1.refs_1_ = f32[32,8,128]{2,1,0:T(8,128)S(1)} async-done(((f32[32,8,128]{2,1,0:T(8,128)}), f32[32,8,128]{2,1,0:T(8,128)S(1)}, u32[]{:S(2)}, u32[]{:S(2)}) %all-to-all-start.1) | async-done | bytes 131104 | tf_op jit(solution)/shard_map/all_to_all | solution.py:949
  45.0 11.8 %mixer_stage.1 = (bf16[896,512]{1,0:T(8,128)(2,1)}, f32[896,512]{1,0:T(8,128)}, f32[896,512]{1,0:T(8,128)}, bf16[2944,512]{1,0:T(8,128)(2,1)}, f32[32,16,128]{2,1,0:T(8,128)}, /*index=5*/f32[8,512]{1,0:T(8,128)S(1)}) custom-call(s32[4]{0:T(128)S(1)} %copy-done.9, f32[32,8,128]{2,1,0:T(8,128)S(1)} %all-to-all-done.1.refs_1_, ...), custom_call_target="tpu_custom_call" | custom-call | bytes 14225424 | tf_op jit(solution)/shard_map/mixer_stage/pallas_call | solution.py:891
  56.8 2.6 all-to-all-start.2
  59.5 2.6 copy.41
  63.1 6.9 %all-to-all-done.2.refs_1_ = f32[32,16,128]{2,1,0:T(8,128)S(1)} async-done(((f32[32,16,128]{2,1,0:T(8,128)}), f32[32,16,128]{2,1,0:T(8,128)S(1)}, u32[]{:S(2)}, u32[]{:S(2)}) %all-to-all-start.2) | async-done | bytes 262176 | tf_op jit(solution)/shard_map/all_to_all | solution.py:949
  70.0 5.8 %merge_stage.1 = (bf16[896,512]{1,0:T(8,128)(2,1)}, f32[896,512]{1,0:T(8,128)}, f32[32,16,128]{2,1,0:T(8,128)}, f32[8,512]{1,0:T(8,128)S(1)}) custom-call(s32[4]{0:T(128)S(1)} %copy-done.9, f32[32,16,128]{2,1,0:T(8,128)S(1)} %all-to-all-done.2.refs_1_, f32[8,512]{1,0:T(8,128)S(1)} %get-tuple-element.150.refs_2_.refs_3_.refs_4_, f32[7,512]{1,0:T(8,128)} %refs_3_.10, ...), custom_call_target="tpu_custom_call" | custom-call | bytes 9367568 | tf_op jit(solution)/shard_map/merge_stage/pallas_call | solution.py:891
  75.9 2.6 all-to-all-start.3
  78.5 10.6 %all-to-all-done.3.refs_2_ = f32[32,16,128]{2,1,0:T(8,128)S(1)} async-done(((f32[32,16,128]{2,1,0:T(8,128)}), f32[32,16,128]{2,1,0:T(8,128)S(1)}, u32[]{:S(2)}, u32[]{:S(2)}) %all-to-all-start.3) | async-done | bytes 262176 | tf_op jit(solution)/shard_map/all_to_all | solution.py:949
  89.1 6.8 %widen_stage.1 = (bf16[896,512]{1,0:T(8,128)(2,1)}, bf16[896,2048]{1,0:T(8,128)(2,1)}, f32[16,128]{1,0:T(8,128)S(1)}, f32[16,128]{1,0:T(8,128)S(1)}, f32[8,512]{1,0:T(8,128)S(1)}) custom-call(s32[4]{0:T(128)S(1)} %copy-done.9, s32[1]{0:T(128)} %bitcast.refs_1_.refs_0_.place, f32[32,16,128]{2,1,0:T(8,128)S(1)} %all-to-all-done.3.refs_2_, ...), custom_call_target="tpu_custom_call" | custom-call | bytes 9777172 | tf_op jit(solution)/shard_map/widen_stage/pallas_call | solution.py:891
  97.0 10.9 %all_to_all.55 = f32[16,16,128]{2,1,0:T(8,128)S(1)} all-to-all(f32[16,16,128]{2,1,0:T(8,128)S(1)} %broadcast_in_dim.15), channel_id=1, replica_groups=mesh['node'=4,'chip'=4,'core'=2] {'node','chip'}, dimensions={0} | all-to-all | bytes 262144 | tf_op jit(solution)/shard_map/all_to_all | solution.py:959
  109.2 9.8 %narrow_stage.1 = (bf16[896,2048]{1,0:T(8,128)(2,1)}, bf16[896,2048]{1,0:T(8,128)(2,1)}, f32[896,512]{1,0:T(8,128)}, f32[32,16,128]{2,1,0:T(8,128)S(1)}, f32[8,2048]{1,0:T(8,128)S(1)}) custom-call(s32[4]{0:T(128)S(1)} %copy-done.9, s32[1]{0:T(128)} %bitcast.refs_1_.refs_0_.place, f32[16,128]{1,0:T(8,128)S(1)} %reduce_sum.18.refs_2_, ...), custom_call_target="tpu_custom_call" | custom-call | bytes 16236564 | tf_op jit(solution)/shard_map/narrow_stage/pallas_call | solution.py:891
  118.9 12.5 %all_to_all.56.refs_2_ = f32[32,16,128]{2,1,0:T(8,128)S(1)} all-to-all(f32[32,16,128]{2,1,0:T(8,128)S(1)} %get-tuple-element.165), channel_id=1, replica_groups=mesh['node'=4,'chip'=4,'core'=2] {'node','chip','core'}, dimensions={0} | all-to-all | bytes 524288 | tf_op jit(solution)/shard_map/all_to_all | solution.py:949
  131.5 8.7 %wide_back_stage.1 = (bf16[896,512]{1,0:T(8,128)(2,1)}, bf16[896,2048]{1,0:T(8,128)(2,1)}, f32[16,128]{1,0:T(8,128)S(1)}, f32[16,128]{1,0:T(8,128)S(1)}, f32[8,512]{1,0:T(8,128)S(1)}) custom-call(s32[4]{0:T(128)S(1)} %copy-done.9, s32[1]{0:T(128)} %bitcast.refs_1_.refs_0_.place, f32[32,16,128]{2,1,0:T(8,128)S(1)} %all_to_all.56.refs_2_, ...), custom_call_target="tpu_custom_call" | custom-call | bytes 17117204 | tf_op jit(solution)/shard_map/wide_back_stage/pallas_call | solution.py:891
  142.0 3.7 all-to-all-start.6
  145.7 6.3 %weight_grad_stage.4 = f32[2048,512]{1,0:T(8,128)} custom-call(s32[1]{0:T(128)} %constant.39.clone.1.place, bf16[896,2048]{1,0:T(8,128)(2,1)} %get-tuple-element.172.inputs, bf16[896,512]{1,0:T(8,128)(2,1)} %get-tuple-element.173.gradient), custom_call_target="tpu_custom_call" | custom-call | flops 1879048192 | bytes 8781824 | tf_op jit(solution)/shard_map/weight_grad_stage/pallas_call | solution.py:924
  154.8 8.9 %narrow_back_stage.1 = (bf16[896,2048]{1,0:T(8,128)(2,1)}, f32[896,512]{1,0:T(8,128)}, f32[32,16,128]{2,1,0:T(8,128)}, f32[8,2048]{1,0:T(8,128)S(1)}) custom-call(s32[4]{0:T(128)S(1)} %copy-done.9, s32[1]{0:T(128)} %bitcast.refs_1_.refs_0_.place, f32[16,128]{1,0:T(8,128)S(1)} %reduce_sum.19.refs_2_, f32[16,128]{1,0:T(8,128)S(1)} %collective-permute-done.3.refs_3_, ...), custom_call_target="tpu_custom_call" | custom-call | bytes 18112532 | tf_op jit(solution)/shard_map/narrow_back_stage/pallas_call | solution.py:891
  163.6 4.2 %all-to-all-start.7 = ((f32[32,16,128]{2,1,0:T(8,128)}), f32[32,16,128]{2,1,0:T(8,128)S(1)}, u32[]{:S(2)}, u32[]{:S(2)}) async-start(f32[32,16,128]{2,1,0:T(8,128)} %get-tuple-element.177), calls=%async_computation.7 | async-start | bytes 524288 | tf_op jit(solution)/shard_map/all_to_all | solution.py:949
  167.8 6.3 %weight_grad_stage.5 = f32[512,2048]{1,0:T(8,128)} custom-call(s32[1]{0:T(128)} %constant.39.clone.1.place, bf16[896,512]{1,0:T(8,128)(2,1)} %get-tuple-element.178.inputs, bf16[896,2048]{1,0:T(8,128)(2,1)} %get-tuple-element.179.gradient), custom_call_target="tpu_custom_call" | custom-call | flops 1879048192 | bytes 8781824 | tf_op jit(solution)/shard_map/weight_grad_stage/pallas_call | solution.py:924
  174.1 4.3 %all-to-all-done.7.refs_1_ = f32[32,16,128]{2,1,0:T(8,128)S(1)} async-done(((f32[32,16,128]{2,1,0:T(8,128)}), f32[32,16,128]{2,1,0:T(8,128)S(1)}, u32[]{:S(2)}, u32[]{:S(2)}) %all-to-all-start.7) | async-done | bytes 262176 | tf_op jit(solution)/shard_map/all_to_all | solution.py:949
  178.4 8.1 %mid_back_stage.1 = (f32[896,512]{1,0:T(8,128)}, bf16[896,512]{1,0:T(8,128)(2,1)}, f32[896,512]{1,0:T(8,128)}, f32[32,16,128]{2,1,0:T(8,128)S(1)}, f32[8,512]{1,0:T(8,128)S(1)}) custom-call(s32[4]{0:T(128)S(1)} %copy-done.9, f32[32,16,128]{2,1,0:T(8,128)S(1)} %all-to-all-done.7.refs_1_, f32[8,512]{1,0:T(8,128)S(1)} %get-tuple-element.150.refs_2_.refs_3_.refs_4_, ...), custom_call_target="tpu_custom_call" | custom-call | bytes 14921744 | tf_op jit(solution)/shard_map/mid_back_stage/pallas_call | solution.py:891
  186.5 15.7 %all_to_all.57.refs_1_ = f32[32,16,128]{2,1,0:T(8,128)S(1)} all-to-all(f32[32,16,128]{2,1,0:T(8,128)S(1)} %get-tuple-element.183), channel_id=1, replica_groups=mesh['node'=4,'chip'=4,'core'=2] {'node','chip','core'}, dimensions={0} | all-to-all | bytes 524288 | tf_op jit(solution)/shard_map/all_to_all | solution.py:949
  202.2 13.5 %mixer_back_stage.1 = (f32[896,512]{1,0:T(8,128)}, f32[736,512]{1,0:T(8,128)S(1)}, f32[736,512]{1,0:T(8,128)S(1)}, f32[32,8,128]{2,1,0:T(8,128)}, f32[8,512]{1,0:T(8,128)S(1)}) custom-call(s32[4]{0:T(128)S(1)} %copy-done.9, f32[32,16,128]{2,1,0:T(8,128)S(1)} %all_to_all.57.refs_1_, f32[8,512]{1,0:T(8,128)S(1)} %get-tuple-element.150.refs_2_.refs_3_.refs_4_, ...), custom_call_target="tpu_custom_call" | custom-call | bytes 20025360 | tf_op jit(solution)/shard_map/mixer_back_stage/pallas_call | solution.py:891
  215.8 5.7 %kernel_grad_stage.1 = (f32[640,512]{1,0:T(8,128)}, f32[640,512]{1,0:T(8,128)S(1)}) custom-call(s32[1]{0:T(128)} %bitcast.refs_1_.refs_0_.place, bf16[896,512]{1,0:T(8,128)(2,1)S(1)} %copy-done.7, bf16[896,512]{1,0:T(8,128)(2,1)S(1)} %copy-done.8, f32[736,512]{1,0:T(8,128)S(1)} %get-tuple-element.190.refs_3_, f32[736,512]{1,0:T(8,128)S(1)} %get-tuple-element.191.refs_4_, ...), custom_call_target="tpu_custom_call" | custom-call | bytes 9732100 | tf_op jit(solution)/shard_map/kernel_grad_stage/pallas_call | solution.py:891
  223.8 2.6 all-to-all-start.9
  226.4 8.2 %all-to-all-done.9.refs_1_ = f32[32,8,128]{2,1,0:T(8,128)S(1)} async-done(((f32[32,8,128]{2,1,0:T(8,128)}), f32[32,8,128]{2,1,0:T(8,128)S(1)}, u32[]{:S(2)}, u32[]{:S(2)}) %all-to-all-start.9) | async-done | bytes 131104 | tf_op jit(solution)/shard_map/all_to_all | solution.py:949
  234.6 5.4 %first_back_stage.1 = (bf16[896,512]{1,0:T(8,128)(2,1)}, f32[896,512]{1,0:T(8,128)}, f32[32,8,128]{2,1,0:T(8,128)}, f32[8,512]{1,0:T(8,128)S(1)}) custom-call(s32[4]{0:T(128)S(1)} %copy-done.9, f32[32,8,128]{2,1,0:T(8,128)S(1)} %all-to-all-done.9.refs_1_, f32[8,512]{1,0:T(8,128)S(1)} %get-tuple-element.150.refs_2_.refs_3_.refs_4_, ...), custom_call_target="tpu_custom_call" | custom-call | bytes 8189968 | tf_op jit(solution)/shard_map/first_back_stage/pallas_call | solution.py:891
  244.8 3.1 sum_and_cut.6
  251.4 2.8 all-to-all-start.10
  258.1 11.3 %collective-permute-done.10.refs_2_ = f32[160,512]{1,0:T(8,128)S(1)} collective-permute-done((f32[160,512]{1,0:T(8,128)S(1)}, f32[160,512]{1,0:T(8,128)S(1)}, u32[]{:S(2)}, u32[]{:S(2)}) %collective-permute-start.10) | collective-permute-done | bytes 327712 | tf_op jit(solution)/shard_map/ppermute | solution.py:1027
  270.2 3.3 block_out_stage.1
  277.3 2.6 collective-permute-start.17
  280.1 3.2 leave_stage.1
  284.6 7.0 %collective-permute-start.21 = (f32[40,512]{1,0:T(8,128)S(1)}, f32[40,512]{1,0:T(8,128)S(1)}, u32[]{:S(2)}, u32[]{:S(2)}) collective-permute-start(f32[40,512]{1,0:T(8,128)S(1)} %sum_and_cut.10.refs_0_), channel_id=1, source_target_pairs={{0,8},{8,0},{16,24},{24,16},{1,9},{9,1},{17,25},{25,17},{2,10},{10... | collective-permute-start | bytes 245768 | tf_op jit(solution)/shard_map/ppermute | solution.py:1027
  296.0 2.6 collective-permute-done.12.refs_1_
  299.9 5.0 %collective-permute-done.14.refs_3_ = f32[16,512]{1,0:T(8,128)S(1)} collective-permute-done((f32[16,512]{1,0:T(8,128)S(1)}, f32[16,512]{1,0:T(8,128)S(1)}, u32[]{:S(2)}, u32[]{:S(2)}) %collective-permute-start.14) | collective-permute-done | bytes 32800 | tf_op jit(solution)/shard_map/ppermute | solution.py:1027
  305.2 3.6 collective-permute-start.28
  310.1 2.7 collective-permute-done.18.refs_1_
  313.8 4.7 %collective-permute-done.20.refs_3_ = f32[16,512]{1,0:T(8,128)S(1)} collective-permute-done((f32[16,512]{1,0:T(8,128)S(1)}, f32[16,512]{1,0:T(8,128)S(1)}, u32[]{:S(2)}, u32[]{:S(2)}) %collective-permute-start.20) | collective-permute-done | bytes 32800 | tf_op jit(solution)/shard_map/ppermute | solution.py:1027
  325.0 2.8 collective-permute-done.24.refs_1_
  327.8 2.6 collective-permute-done.25.refs_2_
  343.2 31.4 %all-reduce.3.cloned.1.call-done = (f32[512,2048]{1,0:T(8,128)}, f32[2048,512]{1,0:T(8,128)}) async-done(((f32[512,2048]{1,0:T(8,128)}, f32[2048,512]{1,0:T(8,128)}), (f32[512,2048]{1,0:T(8,128)}, f32[2048,512]{1,0:T(8,128)})) %all-reduce.3.cloned.1.call-update) | async-done | bytes 8388624 | tf_op jit(solution)/shard_map/psum | solution.py:1222
  374.5 4.8 %copy.47 = f32[512,2048]{1,0:T(8,128)} copy(f32[512,2048]{1,0:T(8,128)} %get-tuple-element.304) | data formatting | bytes 8388608
  (130 shorter events, 65.4 us)
Async XLA Ops:
  11.6 17.9 %all-to-all-start = ((f32[32,16,128]{2,1,0:T(8,128)}), f32[32,16,128]{2,1,0:T(8,128)S(1)}, u32[]{:S(2)}, u32[]{:S(2)}) async-start(f32[32,16,128]{2,1,0:T(8,128)} %get-tuple-element.141), calls=%async_computation | async-start | bytes 524288 | tf_op jit(solution)/shard_map/all_to_all | solution.py:949
  19.0 17.8 %copy-start.13 = (bf16[2048,512]{1,0:T(8,128)(2,1)S(1)}, bf16[2048,512]{1,0:T(8,128)(2,1)}, u32[]{:S(2)}) copy-start(bf16[2048,512]{1,0:T(8,128)(2,1)} %refs_9_.4) | copy-start | bytes 6291460
  34.2 10.8 %all-to-all-start.1 = ((f32[32,8,128]{2,1,0:T(8,128)}), f32[32,8,128]{2,1,0:T(8,128)S(1)}, u32[]{:S(2)}, u32[]{:S(2)}) async-start(f32[32,8,128]{2,1,0:T(8,128)} %get-tuple-element.146), calls=%async_computation.1 | async-start | bytes 262144 | tf_op jit(solution)/shard_map/all_to_all | solution.py:949
  45.0 14.4 %copy-start.12 = (bf16[512,2048]{1,0:T(8,128)(2,1)S(1)}, bf16[512,2048]{1,0:T(8,128)(2,1)}, u32[]{:S(2)}) copy-start(bf16[512,2048]{1,0:T(8,128)(2,1)} %refs_8_.3) | copy-start | bytes 6291460
  56.8 13.2 %all-to-all-start.2 = ((f32[32,16,128]{2,1,0:T(8,128)}), f32[32,16,128]{2,1,0:T(8,128)S(1)}, u32[]{:S(2)}, u32[]{:S(2)}) async-start(f32[32,16,128]{2,1,0:T(8,128)} %get-tuple-element.152), calls=%async_computation.2 | async-start | bytes 524288 | tf_op jit(solution)/shard_map/all_to_all | solution.py:949
  75.9 13.2 %all-to-all-start.3 = ((f32[32,16,128]{2,1,0:T(8,128)}), f32[32,16,128]{2,1,0:T(8,128)S(1)}, u32[]{:S(2)}, u32[]{:S(2)}) async-start(f32[32,16,128]{2,1,0:T(8,128)} %get-tuple-element.159), calls=%async_computation.3 | async-start | bytes 524288 | tf_op jit(solution)/shard_map/all_to_all | solution.py:949
  95.8 1.2 collective-permute-start
  108.0 1.2 collective-permute-start.1
  140.1 1.2 collective-permute-start.2
  142.0 11.5 %all-to-all-start.6 = ((f32[16,16,128]{2,1,0:T(8,128)}), f32[16,16,128]{2,1,0:T(8,128)S(1)}, u32[]{:S(2)}, u32[]{:S(2)}) async-start(f32[16,16,128]{2,1,0:T(8,128)} %broadcast_in_dim.19), calls=%async_computation.6 | async-start | bytes 262144 | tf_op jit(solution)/shard_map/all_to_all | solution.py:959
  153.5 1.2 collective-permute-start.3
  163.6 14.8 %all-to-all-start.7 = ((f32[32,16,128]{2,1,0:T(8,128)}), f32[32,16,128]{2,1,0:T(8,128)S(1)}, u32[]{:S(2)}, u32[]{:S(2)}) async-start(f32[32,16,128]{2,1,0:T(8,128)} %get-tuple-element.177), calls=%async_computation.7 | async-start | bytes 524288 | tf_op jit(solution)/shard_map/all_to_all | solution.py:949
  167.8 206.7 %all-reduce.3.cloned.1.call-start = ((), (), s32[]{:S(2)}) async-start(), calls=%async_computation.11 | async-start | bytes 16777216 | tf_op jit(solution)/shard_map/psum | solution.py:1222
  202.2 13.6 %copy-start.7 = (bf16[896,512]{1,0:T(8,128)(2,1)S(1)}, bf16[896,512]{1,0:T(8,128)(2,1)}, u32[]{:S(2)}) copy-start(bf16[896,512]{1,0:T(8,128)(2,1)} %get-tuple-element.188.refs_1_) | copy-start | bytes 2752516
  202.2 13.6 %copy-start.8 = (bf16[896,512]{1,0:T(8,128)(2,1)S(1)}, bf16[896,512]{1,0:T(8,128)(2,1)}, u32[]{:S(2)}) copy-start(bf16[896,512]{1,0:T(8,128)(2,1)} %get-tuple-element.189.refs_2_) | copy-start | bytes 2752516
  215.8 5.7 %copy-start.10 = (f32[8,512]{1,0:T(8,128)}, f32[8,512]{1,0:T(8,128)S(1)}, u32[]{:S(2)}) copy-start(f32[8,512]{1,0:T(8,128)S(1)} %get-tuple-element.267) | copy-start | bytes 49156
  222.5 20.9 %collective-permute-start.5 = (f32[640,512]{1,0:T(8,128)}, f32[640,512]{1,0:T(8,128)}, u32[]{:S(2)}, u32[]{:S(2)}) collective-permute-start(f32[640,512]{1,0:T(8,128)} %get-tuple-element.192), channel_id=1, source_target_pairs={{0,1},{1,0},{2,3},{3,2},{4,5},{5,4},{6,7},{7,6},{8,9},{9,8},{10,11... | collective-permute-start | bytes 3932168 | tf_op jit(solution)/shard_map/ppermute | solution.py:1042
  223.8 10.8 %all-to-all-start.9 = ((f32[32,8,128]{2,1,0:T(8,128)}), f32[32,8,128]{2,1,0:T(8,128)S(1)}, u32[]{:S(2)}, u32[]{:S(2)}) async-start(f32[32,8,128]{2,1,0:T(8,128)} %get-tuple-element.187), calls=%async_computation.9 | async-start | bytes 262144 | tf_op jit(solution)/shard_map/all_to_all | solution.py:949
  234.6 6.0 %copy-start.2 = (bf16[896,512]{1,0:T(8,128)(2,1)S(1)}, bf16[896,512]{1,0:T(8,128)(2,1)}, u32[]{:S(2)}) copy-start(bf16[896,512]{1,0:T(8,128)(2,1)} %get-tuple-element.169.inputs) | copy-start | bytes 2752516
  242.3 11.9 %collective-permute-start.4 = (f32[256,512]{1,0:T(8,128)S(1)}, f32[256,512]{1,0:T(8,128)S(1)}, u32[]{:S(2)}, u32[]{:S(2)}) collective-permute-start(f32[256,512]{1,0:T(8,128)S(1)} %weight_grad_stage.6), channel_id=1, source_target_pairs={{0,1},{1,0},{2,3},{3,2},{4,5},{5,4},{6,7},{7,6},{8,9},{9,8},{10,11... | collective-permute-start | bytes 1572872 | tf_op jit(solution)/shard_map/ppermute | solution.py:1042
  247.9 21.5 %collective-permute-start.10 = (f32[160,512]{1,0:T(8,128)S(1)}, f32[160,512]{1,0:T(8,128)S(1)}, u32[]{:S(2)}, u32[]{:S(2)}) collective-permute-start(f32[160,512]{1,0:T(8,128)S(1)} %get-tuple-element.212), channel_id=1, source_target_pairs={{0,4},{2,6},{4,0},{6,2},{1,5},{3,7},{5,1},{7,3},{8,12},{10,14},{12... | collective-permute-start | bytes 983048 | tf_op jit(solution)/shard_map/ppermute | solution.py:1027
  248.8 24.7 %collective-permute-start.11 = (f32[160,512]{1,0:T(8,128)}, f32[160,512]{1,0:T(8,128)S(1)}, u32[]{:S(2)}, u32[]{:S(2)}) collective-permute-start(f32[160,512]{1,0:T(8,128)} %get-tuple-element.213), channel_id=1, source_target_pairs={{0,6},{2,4},{4,2},{6,0},{1,7},{3,5},{5,3},{7,1},{8,14},{10,12},{12... | collective-permute-start | bytes 983048 | tf_op jit(solution)/shard_map/ppermute | solution.py:1027
  249.9 23.7 %collective-permute-start.9 = (f32[160,512]{1,0:T(8,128)}, f32[160,512]{1,0:T(8,128)}, u32[]{:S(2)}, u32[]{:S(2)}) collective-permute-start(f32[160,512]{1,0:T(8,128)} %get-tuple-element.211), channel_id=1, source_target_pairs={{0,2},{2,0},{4,6},{6,4},{1,3},{3,1},{5,7},{7,5},{8,10},{10,8},{12,... | collective-permute-start | bytes 983048 | tf_op jit(solution)/shard_map/ppermute | solution.py:1027
  251.4 28.7 %all-to-all-start.10 = ((f32[32,8,128]{2,1,0:T(8,128)}), f32[32,8,128]{2,1,0:T(8,128)S(1)}, u32[]{:S(2)}, u32[]{:S(2)}) async-start(f32[32,8,128]{2,1,0:T(8,128)} %get-tuple-element.207), calls=%async_computation.10 | async-start | bytes 262144 | tf_op jit(solution)/shard_map/all_to_all | solution.py:949
  255.1 22.2 %collective-permute-start.6 = (f32[64,512]{1,0:T(8,128)}, f32[64,512]{1,0:T(8,128)S(1)}, u32[]{:S(2)}, u32[]{:S(2)}) collective-permute-start(f32[64,512]{1,0:T(8,128)} %get-tuple-element.208), channel_id=1, source_target_pairs={{0,2},{2,0},{4,6},{6,4},{1,3},{3,1},{5,7},{7,5},{8,10},{10,8},{12,... | collective-permute-start | bytes 393224 | tf_op jit(solution)/shard_map/ppermute | solution.py:1027
  256.6 23.4 %collective-permute-start.7 = (f32[64,512]{1,0:T(8,128)}, f32[64,512]{1,0:T(8,128)S(1)}, u32[]{:S(2)}, u32[]{:S(2)}) collective-permute-start(f32[64,512]{1,0:T(8,128)} %get-tuple-element.209), channel_id=1, source_target_pairs={{0,4},{2,6},{4,0},{6,2},{1,5},{3,7},{5,1},{7,3},{8,12},{10,14},{12... | collective-permute-start | bytes 393224 | tf_op jit(solution)/shard_map/ppermute | solution.py:1027
  269.4 10.6 %collective-permute-start.8 = (f32[64,512]{1,0:T(8,128)}, f32[64,512]{1,0:T(8,128)S(1)}, u32[]{:S(2)}, u32[]{:S(2)}) collective-permute-start(f32[64,512]{1,0:T(8,128)} %get-tuple-element.210), channel_id=1, source_target_pairs={{0,6},{2,4},{4,2},{6,0},{1,7},{3,5},{5,3},{7,1},{8,14},{10,12},{12... | collective-permute-start | bytes 393224 | tf_op jit(solution)/shard_map/ppermute | solution.py:1027
  275.5 7.9 %collective-permute-start.15 = (f32[40,512]{1,0:T(8,128)S(1)}, f32[40,512]{1,0:T(8,128)S(1)}, u32[]{:S(2)}, u32[]{:S(2)}) collective-permute-start(f32[40,512]{1,0:T(8,128)S(1)} %get-tuple-element.231), channel_id=1, source_target_pairs={{0,8},{8,0},{16,24},{24,16},{1,9},{9,1},{17,25},{25,17},{2,10},{10... | collective-permute-start | bytes 245768 | tf_op jit(solution)/shard_map/ppermute | solution.py:1027
  276.3 8.3 %collective-permute-start.16 = (f32[40,512]{1,0:T(8,128)S(1)}, f32[40,512]{1,0:T(8,128)S(1)}, u32[]{:S(2)}, u32[]{:S(2)}) collective-permute-start(f32[40,512]{1,0:T(8,128)S(1)} %get-tuple-element.232), channel_id=1, source_target_pairs={{0,16},{8,24},{16,0},{24,8},{1,17},{9,25},{17,1},{25,9},{2,18},{10... | collective-permute-start | bytes 245768 | tf_op jit(solution)/shard_map/ppermute | solution.py:1027
  277.3 7.3 %collective-permute-start.17 = (f32[40,512]{1,0:T(8,128)S(1)}, f32[40,512]{1,0:T(8,128)S(1)}, u32[]{:S(2)}, u32[]{:S(2)}) collective-permute-start(f32[40,512]{1,0:T(8,128)S(1)} %get-tuple-element.233), channel_id=1, source_target_pairs={{0,24},{8,16},{16,8},{24,0},{1,25},{9,17},{17,9},{25,1},{2,26},{10... | collective-permute-start | bytes 245768 | tf_op jit(solution)/shard_map/ppermute | solution.py:1027
  284.6 20.3 %collective-permute-start.21 = (f32[40,512]{1,0:T(8,128)S(1)}, f32[40,512]{1,0:T(8,128)S(1)}, u32[]{:S(2)}, u32[]{:S(2)}) collective-permute-start(f32[40,512]{1,0:T(8,128)S(1)} %sum_and_cut.10.refs_0_), channel_id=1, source_target_pairs={{0,8},{8,0},{16,24},{24,16},{1,9},{9,1},{17,25},{25,17},{2,10},{10... | collective-permute-start | bytes 245768 | tf_op jit(solution)/shard_map/ppermute | solution.py:1027
  291.6 13.3 %collective-permute-start.22 = (f32[40,512]{1,0:T(8,128)S(1)}, f32[40,512]{1,0:T(8,128)S(1)}, u32[]{:S(2)}, u32[]{:S(2)}) collective-permute-start(f32[40,512]{1,0:T(8,128)S(1)} %sum_and_cut.10.refs_0_), channel_id=1, source_target_pairs={{0,16},{8,24},{16,0},{24,8},{1,17},{9,25},{17,1},{25,9},{2,18},{10... | collective-permute-start | bytes 245768 | tf_op jit(solution)/shard_map/ppermute | solution.py:1027
  291.6 13.3 %collective-permute-start.23 = (f32[40,512]{1,0:T(8,128)S(1)}, f32[40,512]{1,0:T(8,128)S(1)}, u32[]{:S(2)}, u32[]{:S(2)}) collective-permute-start(f32[40,512]{1,0:T(8,128)S(1)} %sum_and_cut.10.refs_0_), channel_id=1, source_target_pairs={{0,24},{8,16},{16,8},{24,0},{1,25},{9,17},{17,9},{25,1},{2,26},{10... | collective-permute-start | bytes 245768 | tf_op jit(solution)/shard_map/ppermute | solution.py:1027
  294.1 4.5 %collective-permute-start.12 = (f32[16,512]{1,0:T(8,128)S(1)}, f32[16,512]{1,0:T(8,128)S(1)}, u32[]{:S(2)}, u32[]{:S(2)}) collective-permute-start(f32[16,512]{1,0:T(8,128)S(1)} %get-tuple-element.228), channel_id=1, source_target_pairs={{0,8},{8,0},{16,24},{24,16},{1,9},{9,1},{17,25},{25,17},{2,10},{10... | collective-permute-start | bytes 98312 | tf_op jit(solution)/shard_map/ppermute | solution.py:1027
  295.1 4.8 %collective-permute-start.13 = (f32[16,512]{1,0:T(8,128)S(1)}, f32[16,512]{1,0:T(8,128)S(1)}, u32[]{:S(2)}, u32[]{:S(2)}) collective-permute-start(f32[16,512]{1,0:T(8,128)S(1)} %get-tuple-element.229), channel_id=1, source_target_pairs={{0,16},{8,24},{16,0},{24,8},{1,17},{9,25},{17,1},{25,9},{2,18},{10... | collective-permute-start | bytes 98312 | tf_op jit(solution)/shard_map/ppermute | solution.py:1027
  298.6 6.3 %collective-permute-start.14 = (f32[16,512]{1,0:T(8,128)S(1)}, f32[16,512]{1,0:T(8,128)S(1)}, u32[]{:S(2)}, u32[]{:S(2)}) collective-permute-start(f32[16,512]{1,0:T(8,128)S(1)} %get-tuple-element.230), channel_id=1, source_target_pairs={{0,24},{8,16},{16,8},{24,0},{1,25},{9,17},{17,9},{25,1},{2,26},{10... | collective-permute-start | bytes 98312 | tf_op jit(solution)/shard_map/ppermute | solution.py:1027
  305.1 13.5 %collective-permute-start.27 = (f32[160,512]{1,0:T(8,128)S(1)}, f32[160,512]{1,0:T(8,128)S(1)}, u32[]{:S(2)}, u32[]{:S(2)}) collective-permute-start(f32[160,512]{1,0:T(8,128)S(1)} %join.6.refs_0_), channel_id=1, source_target_pairs={{0,2},{2,0},{4,6},{6,4},{1,3},{3,1},{5,7},{7,5},{8,10},{10,8},{12,... | collective-permute-start | bytes 983048 | tf_op jit(solution)/shard_map/ppermute | solution.py:1027
  305.2 13.8 %collective-permute-start.28 = (f32[160,512]{1,0:T(8,128)S(1)}, f32[160,512]{1,0:T(8,128)S(1)}, u32[]{:S(2)}, u32[]{:S(2)}) collective-permute-start(f32[160,512]{1,0:T(8,128)S(1)} %join.6.refs_0_), channel_id=1, source_target_pairs={{0,4},{2,6},{4,0},{6,2},{1,5},{3,7},{5,1},{7,3},{8,12},{10,14},{12... | collective-permute-start | bytes 983048 | tf_op jit(solution)/shard_map/ppermute | solution.py:1027
  308.8 12.3 %collective-permute-start.29 = (f32[160,512]{1,0:T(8,128)S(1)}, f32[160,512]{1,0:T(8,128)S(1)}, u32[]{:S(2)}, u32[]{:S(2)}) collective-permute-start(f32[160,512]{1,0:T(8,128)S(1)} %join.6.refs_0_), channel_id=1, source_target_pairs={{0,6},{2,4},{4,2},{6,0},{1,7},{3,5},{5,3},{7,1},{8,14},{10,12},{12... | collective-permute-start | bytes 983048 | tf_op jit(solution)/shard_map/ppermute | solution.py:1027
  308.8 3.9 %collective-permute-start.18 = (f32[16,512]{1,0:T(8,128)S(1)}, f32[16,512]{1,0:T(8,128)S(1)}, u32[]{:S(2)}, u32[]{:S(2)}) collective-permute-start(f32[16,512]{1,0:T(8,128)S(1)} %sum_and_cut.11.refs_0_), channel_id=1, source_target_pairs={{0,8},{8,0},{16,24},{24,16},{1,9},{9,1},{17,25},{25,17},{2,10},{10... | collective-permute-start | bytes 98312 | tf_op jit(solution)/shard_map/ppermute | solution.py:1027
  308.8 5.0 %collective-permute-start.19 = (f32[16,512]{1,0:T(8,128)S(1)}, f32[16,512]{1,0:T(8,128)S(1)}, u32[]{:S(2)}, u32[]{:S(2)}) collective-permute-start(f32[16,512]{1,0:T(8,128)S(1)} %sum_and_cut.11.refs_0_), channel_id=1, source_target_pairs={{0,16},{8,24},{16,0},{24,8},{1,17},{9,25},{17,1},{25,9},{2,18},{10... | collective-permute-start | bytes 98312 | tf_op jit(solution)/shard_map/ppermute | solution.py:1027
  312.8 5.7 %collective-permute-start.20 = (f32[16,512]{1,0:T(8,128)S(1)}, f32[16,512]{1,0:T(8,128)S(1)}, u32[]{:S(2)}, u32[]{:S(2)}) collective-permute-start(f32[16,512]{1,0:T(8,128)S(1)} %sum_and_cut.11.refs_0_), channel_id=1, source_target_pairs={{0,24},{8,16},{16,8},{24,0},{1,25},{9,17},{17,9},{25,1},{2,26},{10... | collective-permute-start | bytes 98312 | tf_op jit(solution)/shard_map/ppermute | solution.py:1027
  321.4 17.2 %collective-permute-start.31 = (f32[640,512]{1,0:T(8,128)S(1)}, f32[640,512]{1,0:T(8,128)}, u32[]{:S(2)}, u32[]{:S(2)}) collective-permute-start(f32[640,512]{1,0:T(8,128)S(1)} %join.8.refs_0_), channel_id=1, source_target_pairs={{0,1},{1,0},{2,3},{3,2},{4,5},{5,4},{6,7},{7,6},{8,9},{9,8},{10,11... | collective-permute-start | bytes 3932168 | tf_op jit(solution)/shard_map/ppermute | solution.py:1027
  321.4 6.4 %collective-permute-start.24 = (f32[64,512]{1,0:T(8,128)S(1)}, f32[64,512]{1,0:T(8,128)S(1)}, u32[]{:S(2)}, u32[]{:S(2)}) collective-permute-start(f32[64,512]{1,0:T(8,128)S(1)} %join.7.refs_0_), channel_id=1, source_target_pairs={{0,2},{2,0},{4,6},{6,4},{1,3},{3,1},{5,7},{7,5},{8,10},{10,8},{12,... | collective-permute-start | bytes 393224 | tf_op jit(solution)/shard_map/ppermute | solution.py:1027
  322.1 8.4 %collective-permute-start.25 = (f32[64,512]{1,0:T(8,128)S(1)}, f32[64,512]{1,0:T(8,128)S(1)}, u32[]{:S(2)}, u32[]{:S(2)}) collective-permute-start(f32[64,512]{1,0:T(8,128)S(1)} %join.7.refs_0_), channel_id=1, source_target_pairs={{0,4},{2,6},{4,0},{6,2},{1,5},{3,7},{5,1},{7,3},{8,12},{10,14},{12... | collective-permute-start | bytes 393224 | tf_op jit(solution)/shard_map/ppermute | solution.py:1027
  323.6 6.9 %collective-permute-start.26 = (f32[64,512]{1,0:T(8,128)S(1)}, f32[64,512]{1,0:T(8,128)S(1)}, u32[]{:S(2)}, u32[]{:S(2)}) collective-permute-start(f32[64,512]{1,0:T(8,128)S(1)} %join.7.refs_0_), channel_id=1, source_target_pairs={{0,6},{2,4},{4,2},{6,0},{1,7},{3,5},{5,3},{7,1},{8,14},{10,12},{12... | collective-permute-start | bytes 393224 | tf_op jit(solution)/shard_map/ppermute | solution.py:1027
  330.6 11.6 %collective-permute-start.30 = (f32[256,512]{1,0:T(8,128)S(1)}, f32[256,512]{1,0:T(8,128)S(1)}, u32[]{:S(2)}, u32[]{:S(2)}) collective-permute-start(f32[256,512]{1,0:T(8,128)S(1)} %join.9.refs_0_), channel_id=1, source_target_pairs={{0,1},{1,0},{2,3},{3,2},{4,5},{5,4},{6,7},{7,6},{8,9},{9,8},{10,11... | collective-permute-start | bytes 1572872 | tf_op jit(solution)/shard_map/ppermute | solution.py:1027
  374.5 4.9 %copy-start.14 = (f32[2048,512]{1,0:T(8,128)S(1)}, f32[2048,512]{1,0:T(8,128)}, u32[]{:S(2)}) copy-start(f32[2048,512]{1,0:T(8,128)} %get-tuple-element.305) | copy-start | bytes 12582916
  (11 other events, 15.8 us)
Sparse Core Ops, SparseCore 0:
  178.5 195.9 all-reduce.2
